TPU v7x, 32 devices: a whole 2x2x4 slice. The times are simulated.
32 devices in a mesh: dp: 4 (over y, core), mp: 8 (over z, x).
Axes of the slice: x: 2, y: 2, z: 4, core: 2. Of those that a mesh axis runs over, the one named last changes fastest.
Arguments:
- tokens: int32 [4, 8, 256], P('dp'), may hold values from 0 to 3839
- lengths: int32 [4, 8], P('dp'), may hold values from 1 to 256, as said below
- places: int32 [4, 8, 25], P('dp', 'mp'), may hold values from 0 to 255, as said below
- targets: int32 [4, 8, 25], P('dp'), may hold values from 0 to 3839
- ramp: int32 [2, 3072], replicated, may hold values from 0 to 8
- attn: float32 [2, 4, 768, 768], P(None, None, 'mp'), may hold values from -0.21875 to 0.21875
- attn_m: float32 [2, 4, 768, 768], P(None, None, 'mp'), may hold values from -0.00036621094 to 0.00036621094
- attn_v: float32 [2, 4, 768, 768], P(None, None, 'mp'), may hold values from 4.9846235e-11 to 1.9938494e-10
- ffn: float32 [2, 2, 3072, 768], P(None, None, 'mp'), may hold values from -0.21875 to 0.21875
- ffn_m: float32 [2, 2, 3072, 768], P(None, None, 'mp'), may hold values from -0.00036621094 to 0.00036621094
- ffn_v: float32 [2, 2, 3072, 768], P(None, None, 'mp'), may hold values from 4.9846235e-11 to 1.9938494e-10
- table: float32 [3840, 768], P(None, 'mp'), may hold values from -0.625 to 0.625
- table_m: float32 [3840, 768], P(None, 'mp'), may hold values from -2.2888184e-05 to 2.2888184e-05
- table_v: float32 [3840, 768], P(None, 'mp'), may hold values from 2.0769264e-13 to 8.3077057e-13
- out_table: float32 [3840, 768], P('mp'), may hold values from -0.5412659 to 0.5412659
- out_m: float32 [3840, 768], P('mp'), may hold values from -0.00036621094 to 0.00036621094
- out_v: float32 [3840, 768], P('mp'), may hold values from 4.9846235e-11 to 1.9938494e-10
- gains: float32 [5, 2, 768], replicated, may hold values from -1 to 2
- gains_m: float32 [5, 2, 768], replicated, may hold values from -0.0012207031 to 0.0012207031
- gains_v: float32 [5, 2, 768], replicated, may hold values from 4.984623e-10 to 1.9938493e-09
Outputs:
- loss: float32 [2], replicated
- grad_norm: float32 [1], replicated
- attn_m_new: float32 [2, 4, 768, 768], P(None, None, 'mp')
- attn_v_new: float32 [2, 4, 768, 768], P(None, None, 'mp')
- attn_new: float32 [2, 4, 768, 768], P(None, None, 'mp')
- ffn_m_new: float32 [2, 2, 3072, 768], P(None, None, 'mp')
- ffn_v_new: float32 [2, 2, 3072, 768], P(None, None, 'mp')
- ffn_new: float32 [2, 2, 3072, 768], P(None, None, 'mp')
- table_m_new: float32 [3840, 768], P(None, 'mp')
- table_v_new: float32 [3840, 768], P(None, 'mp')
- table_new: float32 [3840, 768], P(None, 'mp')
- out_m_new: float32 [3840, 768], P('mp')
- out_v_new: float32 [3840, 768], P('mp')
- out_new: float32 [3840, 768], P('mp')
- gains_m_new: float32 [5, 2, 768], replicated
- gains_v_new: float32 [5, 2, 768], replicated
- gains_new: float32 [5, 2, 768], replicated
Inputs may be any that keep to these rules, and one draw needn't show every extreme that they name: `lengths`: each group of 8 sequences along dp holds one sequence of exactly 256 tokens. `places`: each slot lies below its sequence's length.
All inputs are finite; a program needn't handle non-finite values.
Results may differ from a plain program's by a relative error of at most 0.0075.
The roundings to bfloat16 on the way count: a program that leaves them out, or rounds other values in their place, can miss the bound.
Values may be sent and summed in bfloat16 or wider, within the bound.
A program may use at most 320 MiB of HBM per device.

v0:
```python
import math

import jax
import jax.numpy as jnp
from jax import lax
from jax.sharding import PartitionSpec as P

HEADS = 12
LAYERS = 2
STEP = 10
RAMP = 4


norm_eps = 1e-05
beta_one = 0.9
beta_two = 0.999
learn_rate = 0.02
gain_rate = 0.3
weight_decay = 0.01
adam_eps = 1e-08
clip_limit = 1.0
masked_score = -1000000000.0


def merged(value, axis, join):
    pieces = jax.tree.map(lambda part: lax.all_gather(part, axis), value)
    head = jax.tree.map(lambda part: part[0], pieces)
    tail = jax.tree.map(lambda part: part[1:], pieces)
    total, _ = lax.scan(lambda total, section: (join(total, section), None), head, tail)
    return total


def sinusoid(count, width):
    places = jnp.arange(count, dtype=jnp.float32)[:, None]
    freqs = jnp.exp(jnp.arange(width // 2, dtype=jnp.float32) * (-2.0 * math.log(10000.0) / width))
    angles = places * freqs[None, :]
    return jnp.concatenate([jnp.sin(angles), jnp.cos(angles)], axis=1)


def layer_norm(values, gain, shift):
    centre = jnp.mean(values, axis=-1, keepdims=True)
    offset = values - centre
    spread = jnp.mean(offset * offset, axis=-1, keepdims=True)
    inverse = lax.rsqrt(spread + norm_eps)
    normed = offset * inverse
    return (normed * gain + shift, (normed, inverse))


def norm_backward(grad, saved, gain):
    normed, inverse = saved
    scaled = grad * gain
    centred = scaled - jnp.mean(scaled, axis=-1, keepdims=True)
    result = inverse * (centred - normed * jnp.mean(scaled * normed, axis=-1, keepdims=True))
    return (result, jnp.stack([jnp.sum(grad * normed, axis=0), jnp.sum(grad, axis=0)]))


def gelu_exact(values):
    return jax.nn.gelu(values, approximate=False)


def gelu_back(hidden, grad):
    unused, pullback = jax.vjp(gelu_exact, hidden)
    return pullback(grad)[0]


def masked_scores(query, keyed, length):
    scale = query.shape[-1] ** (-0.5)
    scores = jnp.einsum("hqe,hke->hqk", query, keyed, preferred_element_type=jnp.float32) * scale
    visible = jnp.arange(keyed.shape[1]) < length
    return jnp.where(visible[None, None, :], scores, masked_score)


def fetch_forward(attn_part, ffn_part):
    return (
        lax.all_gather(attn_part, "mp", axis=1, tiled=True),
        lax.all_gather(ffn_part, "mp", axis=1, tiled=True),
    )


def fetch_backward(attn_part, ffn_part):
    return (
        lax.all_gather(attn_part, "mp", axis=1, tiled=True),
        lax.all_gather(ffn_part, "mp", axis=1, tiled=True),
    )


def reduce_layer(attn_grad, ffn_grad):
    return (
        lax.psum_scatter(attn_grad, "mp", scatter_dimension=1, tiled=True),
        lax.psum_scatter(ffn_grad, "mp", scatter_dimension=1, tiled=True),
    )


def ffn_forward(middle_b, ffn_w, unit_mask):
    hidden = jnp.einsum("td,fd->tf", middle_b, ffn_w[0], preferred_element_type=jnp.float32)
    active = (gelu_exact(hidden) * unit_mask[None, :]).astype(jnp.bfloat16)
    output = jnp.einsum("tf,fd->td", active, ffn_w[1], preferred_element_type=jnp.float32)
    return (hidden, active, output)


def ffn_backward(grad_out, middle_b, hidden, active, ffn_w, unit_mask):
    grad_active = jnp.einsum("td,fd->tf", grad_out, ffn_w[1], preferred_element_type=jnp.float32)
    grad_hidden = gelu_back(hidden, grad_active * unit_mask[None, :]).astype(jnp.bfloat16)
    up_grad = jnp.einsum("tf,td->fd", grad_hidden, middle_b, preferred_element_type=jnp.float32)
    down_grad = jnp.einsum("tf,td->fd", active, grad_out, preferred_element_type=jnp.float32)
    from_ffn = jnp.einsum("tf,fd->td", grad_hidden, ffn_w[0], preferred_element_type=jnp.float32)
    return (jnp.stack([up_grad, down_grad]), from_ffn)


def layer_forward(states, attn_w, ffn_w, pair, length, unit_mask):
    count = states.shape[0]
    inputs = states.astype(jnp.bfloat16)
    projected = jnp.einsum(
        "td,kde->kte", inputs, attn_w[:3], preferred_element_type=jnp.float32
    ).astype(jnp.bfloat16)
    heads = projected.reshape(3, count, HEADS, -1).transpose(0, 2, 1, 3)
    scores = masked_scores(heads[0], heads[1], length)
    peak = jnp.max(scores, axis=-1, keepdims=True)
    expo = jnp.exp(scores - peak)
    total = jnp.sum(expo, axis=-1, keepdims=True)
    log_total = peak + jnp.log(total)
    probs = (expo / total).astype(jnp.bfloat16)
    mixed = jnp.einsum("hqk,hke->hqe", probs, heads[2], preferred_element_type=jnp.float32)
    mixed = mixed.transpose(1, 0, 2).reshape(count, -1).astype(jnp.bfloat16)
    branch = jnp.dot(mixed, attn_w[3], preferred_element_type=jnp.float32)
    middle, norm_one = layer_norm(states + branch, pair[0, 0], pair[0, 1])
    middle_b = middle.astype(jnp.bfloat16)
    hidden, active, output = ffn_forward(middle_b, ffn_w, unit_mask)
    result, norm_two = layer_norm(middle + output, pair[1, 0], pair[1, 1])
    return (result, (inputs, heads, log_total, mixed, norm_one, middle_b, hidden, active, norm_two))


def layer_backward(grad, attn_w, ffn_w, pair, length, unit_mask, kept):
    inputs, heads, log_total, mixed, norm_one, middle_b, hidden, active, norm_two = kept
    count = inputs.shape[0]
    grad_two, pair_two = norm_backward(grad, norm_two, pair[1, 0])
    ffn_grad, from_ffn = ffn_backward(
        grad_two.astype(jnp.bfloat16), middle_b, hidden, active, ffn_w, unit_mask
    )
    grad_one, pair_one = norm_backward(grad_two + from_ffn, norm_one, pair[0, 0])
    grad_branch = grad_one.astype(jnp.bfloat16)
    output_grad = jnp.einsum("td,te->de", mixed, grad_branch, preferred_element_type=jnp.float32)
    grad_mixed = jnp.einsum("te,de->td", grad_branch, attn_w[3], preferred_element_type=jnp.float32)
    grad_mixed = grad_mixed.astype(jnp.bfloat16).reshape(count, HEADS, -1).transpose(1, 0, 2)
    scale = heads.shape[-1] ** (-0.5)
    probs = jnp.exp(masked_scores(heads[0], heads[1], length) - log_total)
    grad_values = jnp.einsum(
        "hqk,hqe->hke", probs.astype(jnp.bfloat16), grad_mixed, preferred_element_type=jnp.float32
    )
    grad_probs = jnp.einsum(
        "hqe,hke->hqk", grad_mixed, heads[2], preferred_element_type=jnp.float32
    )
    grad_scores = probs * (grad_probs - jnp.sum(grad_probs * probs, axis=-1, keepdims=True))
    grad_scores = grad_scores.astype(jnp.bfloat16)
    grad_query = (
        jnp.einsum("hqk,hke->hqe", grad_scores, heads[1], preferred_element_type=jnp.float32)
        * scale
    )
    grad_key = (
        jnp.einsum("hqk,hqe->hke", grad_scores, heads[0], preferred_element_type=jnp.float32)
        * scale
    )
    stacked = (
        jnp.stack([grad_query, grad_key, grad_values]).transpose(0, 2, 1, 3).reshape(3, count, -1)
    )
    stacked = stacked.astype(jnp.bfloat16)
    input_grad = jnp.einsum("td,kte->kde", inputs, stacked, preferred_element_type=jnp.float32)
    from_attn = jnp.einsum("kte,kde->td", stacked, attn_w[:3], preferred_element_type=jnp.float32)
    attn_grad = jnp.concatenate([input_grad, output_grad[None]], axis=0)
    return (grad_one + from_attn, attn_grad, ffn_grad, jnp.stack([pair_one, pair_two]))


def adamw(weight, moment_one, moment_two, grad, decay, rate):
    moment_one = beta_one * moment_one + (1.0 - beta_one) * grad
    moment_two = beta_two * moment_two + (1.0 - beta_two) * grad * grad
    fixed_one = moment_one / (1.0 - beta_one**STEP)
    fixed_two = moment_two / (1.0 - beta_two**STEP)
    weight = weight - rate * (fixed_one / (jnp.sqrt(fixed_two) + adam_eps) + decay * weight)
    return (moment_one, moment_two, weight)


def combine_vocab(first, second):
    peak = jnp.maximum(first[0], second[0])
    total = first[1] * jnp.exp(first[0] - peak) + second[1] * jnp.exp(second[0] - peak)
    return (peak, total, first[2] + second[2])


def local(
    tokens,
    lengths,
    places,
    targets,
    ramp,
    attn,
    attn_m,
    attn_v,
    ffn,
    ffn_m,
    ffn_v,
    table,
    table_m,
    table_v,
    out_table,
    out_m,
    out_v,
    gains,
    gains_m,
    gains_v,
):
    rank = lax.axis_index("mp")
    count = tokens.shape[2]
    flat_ids = tokens.reshape(-1)
    all_lengths = lengths.reshape(-1)
    length = lax.dynamic_index_in_dim(all_lengths, rank, keepdims=False)
    masks = jnp.minimum(ramp, RAMP).astype(jnp.float32) / RAMP
    unit_masks = [masks[depth] for depth in range(LAYERS)]
    looked = jnp.take(table, flat_ids, axis=0)
    embedded = lax.all_to_all(looked, "mp", split_axis=0, concat_axis=1, tiled=True)
    states, norm_zero = layer_norm(
        embedded + sinusoid(count, embedded.shape[1]), gains[0, 0], gains[0, 1]
    )
    kept_all = []
    weights_all = []
    for depth in range(LAYERS):
        attn_w, ffn_w = fetch_forward(
            attn[depth].astype(jnp.bfloat16), ffn[depth].astype(jnp.bfloat16)
        )
        states, kept = layer_forward(
            states, attn_w, ffn_w, gains[1 + 2 * depth : 3 + 2 * depth], length, unit_masks[depth]
        )
        kept_all.append(kept)
        weights_all.append(None)
    spots = places.reshape(-1)
    picked = jnp.take(states, spots, axis=0).astype(jnp.bfloat16)
    picked_all = lax.all_gather(picked, "mp", axis=0, tiled=True)
    out_b = out_table.astype(jnp.bfloat16)
    logits = jnp.einsum("rd,vd->rv", picked_all, out_b, preferred_element_type=jnp.float32)
    labels = targets.reshape(-1)
    columns = rank * out_table.shape[0] + jnp.arange(out_table.shape[0])
    hits = (labels[:, None] == columns[None, :]).astype(jnp.float32)
    peak = jnp.max(logits, axis=1)
    expsum = jnp.sum(jnp.exp(logits - peak[:, None]), axis=1)
    target_part = jnp.sum(hits * logits, axis=1)
    peak_all, expsum_all, target_all = merged((peak, expsum, target_part), "mp", combine_vocab)
    log_total = peak_all + jnp.log(expsum_all)
    slot_count = targets.shape[2]
    counted = jnp.maximum(1, all_lengths * slot_count // count)
    valid = (jnp.arange(slot_count)[None, :] < counted[:, None]).reshape(-1)
    loss_pair = jnp.stack(
        [
            jnp.sum(jnp.where(valid, log_total - target_all, 0.0)),
            jnp.sum(counted).astype(jnp.float32),
        ]
    )
    grad_logits = jnp.where(
        valid[:, None], jnp.exp(logits - log_total[:, None]) - hits, 0.0
    ).astype(jnp.bfloat16)
    out_grad = jnp.einsum("rv,rd->vd", grad_logits, picked_all, preferred_element_type=jnp.float32)
    picked_grad = lax.psum_scatter(
        jnp.dot(grad_logits, out_b, preferred_element_type=jnp.float32),
        "mp",
        scatter_dimension=0,
        tiled=True,
    )
    grad = jnp.zeros_like(states).at[spots].add(picked_grad)
    attn_parts = [None] * LAYERS
    ffn_parts = [None] * LAYERS
    pair_grads = [None] * LAYERS
    for depth in reversed(range(LAYERS)):
        attn_w, ffn_w = fetch_backward(
            attn[depth].astype(jnp.bfloat16), ffn[depth].astype(jnp.bfloat16)
        )
        grad, attn_grad, ffn_grad, pair_grad = layer_backward(
            grad,
            attn_w,
            ffn_w,
            gains[1 + 2 * depth : 3 + 2 * depth],
            length,
            unit_masks[depth],
            kept_all[depth],
        )
        attn_parts[depth], ffn_parts[depth] = reduce_layer(attn_grad, ffn_grad)
        pair_grads[depth] = pair_grad
    grad_sum, zero_grad = norm_backward(grad, norm_zero, gains[0, 0])
    returned = lax.all_to_all(grad_sum, "mp", split_axis=1, concat_axis=0, tiled=True)
    table_grad = jnp.zeros_like(table).at[flat_ids].add(returned)
    gains_grad = jnp.concatenate([zero_grad[None]] + pair_grads, axis=0)
    attn_sum, ffn_sum, table_sum, out_sum, gains_part, loss = lax.psum(
        (jnp.stack(attn_parts), jnp.stack(ffn_parts), table_grad, out_grad, gains_grad, loss_pair),
        "dp",
    )
    shard_squares = (
        jnp.sum(attn_sum * attn_sum)
        + jnp.sum(ffn_sum * ffn_sum)
        + jnp.sum(table_sum * table_sum)
        + jnp.sum(out_sum * out_sum)
    )
    square_total, gains_sum = lax.psum((shard_squares, gains_part), "mp")
    grad_norm = jnp.sqrt(square_total + jnp.sum(gains_sum * gains_sum))
    factor = clip_limit / jnp.maximum(grad_norm, clip_limit)
    attn_m_new, attn_v_new, attn_new = adamw(
        attn, attn_m, attn_v, attn_sum * factor, weight_decay, learn_rate
    )
    ffn_m_new, ffn_v_new, ffn_new = adamw(
        ffn, ffn_m, ffn_v, ffn_sum * factor, weight_decay, learn_rate
    )
    table_m_new, table_v_new, table_new = adamw(
        table, table_m, table_v, table_sum * factor, weight_decay, learn_rate
    )
    out_m_new, out_v_new, out_new = adamw(
        out_table, out_m, out_v, out_sum * factor, weight_decay, learn_rate
    )
    gains_m_new, gains_v_new, gains_new = adamw(
        gains, gains_m, gains_v, gains_sum * factor, 0.0, gain_rate
    )
    return (
        loss,
        grad_norm.reshape(1),
        attn_m_new,
        attn_v_new,
        attn_new,
        ffn_m_new,
        ffn_v_new,
        ffn_new,
        table_m_new,
        table_v_new,
        table_new,
        out_m_new,
        out_v_new,
        out_new,
        gains_m_new,
        gains_v_new,
        gains_new,
    )


def solution(mesh):
    in_specs = (
        P("dp", None, None),
        P("dp", None),
        P("dp", "mp", None),
        P("dp", None, None),
        P(),
        P(None, None, "mp", None),
        P(None, None, "mp", None),
        P(None, None, "mp", None),
        P(None, None, "mp", None),
        P(None, None, "mp", None),
        P(None, None, "mp", None),
        P(None, "mp"),
        P(None, "mp"),
        P(None, "mp"),
        P("mp", None),
        P("mp", None),
        P("mp", None),
        P(),
        P(),
        P(),
    )
    out_specs = (
        P(),
        P(),
        P(None, None, "mp", None),
        P(None, None, "mp", None),
        P(None, None, "mp", None),
        P(None, None, "mp", None),
        P(None, None, "mp", None),
        P(None, None, "mp", None),
        P(None, "mp"),
        P(None, "mp"),
        P(None, "mp"),
        P("mp", None),
        P("mp", None),
        P("mp", None),
        P(),
        P(),
        P(),
    )
    return jax.shard_map(local, mesh=mesh, in_specs=in_specs, out_specs=out_specs, check_vma=False)
```

profile of v0, /device:TPU:0, one launch (start us, length us, event | category | flops | bytes accessed | tf_op | source)
XLA Modules:
  0.0 2214.4 jit_solution(4200881986127916065)
XLA Ops:
  10.2 2.6 convert.21
  17.2 5.5 gather_fusion
  24.0 7.3 all-to-all-start
  41.0 20.5 all-to-all-done
  63.5 43.4 %all-gather.13.cloned.1.call-done = bf16[1,4,768,768]{3,2,1,0:T(8,128)(2,1)} async-done(((bf16[1,4,96,768]{3,2,1,0:T(8,128)(2,1)}), bf16[1,4,768,768]{3,2,1,0:T(8,128)(2,1)}) %all-gather.13.cloned.1.call-update) | async-done | bytes 4718608 | tf_op jit(solution)/shard_map/all_gather | solution.py:75
  106.8 3.1 fusion.45
  115.7 2.1 fusion.138
  119.6 126.2 %all-gather.15.cloned.1.call-done = bf16[1,2,3072,768]{3,2,1,0:T(8,128)(2,1)} async-done(((bf16[1,2,384,768]{3,2,1,0:T(8,128)(2,1)}), bf16[1,2,3072,768]{3,2,1,0:T(8,128)(2,1)}) %all-gather.15.cloned.1.call-update) | async-done | bytes 9437200 | tf_op jit(solution)/shard_map/all_gather | solution.py:76
  245.8 11.6 multiply_convert_fusion.3
  260.1 66.6 %all-gather.17.cloned.1.call-done = bf16[1,4,768,768]{3,2,1,0:T(8,128)(2,1)} async-done(((bf16[1,4,96,768]{3,2,1,0:T(8,128)(2,1)}), bf16[1,4,768,768]{3,2,1,0:T(8,128)(2,1)}) %all-gather.17.cloned.1.call-update) | async-done | bytes 4718608 | tf_op jit(solution)/shard_map/all_gather | solution.py:75
  326.7 4.4 fusion.46
  331.1 2.6 copy.180
  333.7 2.0 fusion.140
  336.2 2.1 fusion.60
  338.3 2.0 fusion.141
  341.5 124.1 %all-gather.19.cloned.1.call-done = bf16[1,2,3072,768]{3,2,1,0:T(8,128)(2,1)} async-done(((bf16[1,2,384,768]{3,2,1,0:T(8,128)(2,1)}), bf16[1,2,3072,768]{3,2,1,0:T(8,128)(2,1)}) %all-gather.19.cloned.1.call-update) | async-done | bytes 9437200 | tf_op jit(solution)/shard_map/all_gather | solution.py:76
  465.6 11.6 multiply_convert_fusion.2
  481.9 31.0 %all-gather.7 = bf16[8,25,768]{2,1,0:T(8,128)(2,1)S(1)} all-gather(bf16[1,25,768]{2,1,0:T(8,128)(2,1)S(1)} %fusion.110), channel_id=1, replica_groups=mesh['dp'=4,'mp'=8] {'mp'}, dimensions={0}, use_global_device_ids=true | all-gather | bytes 345600 | tf_op jit(solution)/shard_map/all_gather | solution.py:235
  513.7 2.5 fusion.143
  523.8 35.4 %all-reduce.8 = (f32[1600]{0:T(1024)}, f32[1600]{0:T(1024)}, f32[1600]{0:T(1024)}) all-reduce(f32[1600]{0:T(1024)} %dynamic-update-slice, f32[1600]{0:T(1024)} %dynamic-update-slice.1, f32[1600]{0:T(1024)} %dynamic-update-slice.2), channel_id=6, replica_groups=mesh['dp'=4,'mp'=8] {'mp'}, use_global_device_ids=true, to_apply=%add | all-reduce | flops 4800 | bytes 38400
  571.2 27.5 %while.14 = (s32[]{:T(128)}, f32[200]{0:T(256)}, f32[200]{0:T(256)}, f32[200]{0:T(256)}, f32[7,200]{1,0:T(8,128)}, /*index=5*/f32[7,200]{1,0:T(8,128)}, f32[7,200]{1,0:T(8,128)}, s32[]{:T(128)}) while((s32[]{:T(128)}, f32[200]{0:T(256)}, f32[200]{0:T(256)}, f32[200]{0:T(256)}, f32[7,200]{1,0:T(8,128)}, /*index=5*/f32[7,200]{1,0:T(8,128)}, ...), condition=%wide.region_18.19_spmd, body=%wide.region_17.18_spmd.sunk | while | flops 1402 | bytes 12101 | solution.py:29
  600.6 2.6 fusion.95
  603.2 23.5 %fusion = f32[32,768]{1,0:T(8,128)} fusion(f32[200,768]{1,0:T(8,128)} %fusion.95), kind=kCustom, calls=%all-reduce-scatter | all-reduce-scatter fusion | flops 196609 | bytes 713216
  627.6 2.9 collective-permute-start
  634.4 4.7 concatenate.22
  639.1 2.4 scatter_custom_fusion
  641.5 2.5 multiply_reduce_fusion.6
  645.9 5.8 add_convert_fusion.1
  651.8 2.3 multiply_reduce_fusion.7
  656.3 2.5 convolution_convert_fusion.1
  660.7 2.7 fusion.69
  663.8 1.9 multiply_reduce_fusion.2
  668.4 2.0 multiply_reduce_fusion.8
  673.5 2.6 add_convert_fusion
  676.2 2.3 multiply_reduce_fusion.9
  678.8 1.9 convolution_bitcast_fusion.7
  680.7 2.5 convolution_convert_fusion
  685.2 2.5 fusion.47
  692.4 4.3 pad_maximum_fusion.3
  696.7 12.1 copy.196
  710.6 4.3 pad_maximum_fusion.2
  714.9 12.0 copy.193
  728.1 3.0 convolution_bitcast_fusion.2
  732.7 6.7 pad_maximum_fusion
  740.5 3.0 convolution_bitcast_fusion
  745.2 6.9 pad_maximum_fusion.1
  753.4 3.3 multiply_reduce_fusion.10
  758.2 4.2 all-to-all-start.1
  764.8 33.8 %all-to-all-done.1 = f32[256,8,96]{0,2,1:T(8,128)S(1)} async-done(((f32[256,8,96]{0,2,1:T(8,128)}), f32[256,8,96]{0,2,1:T(8,128)S(1)}, u32[]{:S(2)}, u32[]{:S(2)}) %all-to-all-start.1) | async-done | bytes 786464 | tf_op jit(solution)/shard_map/all_to_all | solution.py:285
  798.9 12.3 scatter_custom_fusion.1
  813.0 498.1 %all-reduce.15.cloned.1.call-done = (f32[4,768,768]{2,0,1:T(4,128)}, f32[4,768,768]{2,0,1:T(4,128)}) async-done(((f32[4,768,768]{2,0,1:T(4,128)}, f32[4,768,768]{2,0,1:T(4,128)}), (f32[4,768,768]{2,0,1:T(4,128)}, f32[4,768,768]{2,0,1:T(4,128)})) %all-reduce.15.cloned.1.call-update) | async-done | bytes 18874384
  1315.8 311.3 %reduce-scatter.5.cloned.1.call-done = f32[2,384,768]{2,1,0:T(8,128)} async-done(((f32[2,3072,768]{2,1,0:T(8,128)}), f32[2,384,768]{2,1,0:T(8,128)}) %reduce-scatter.5.cloned.1.call-update) | async-done | bytes 2359312 | tf_op jit(solution)/shard_map/reduce_scatter | solution.py:90
  1627.0 316.5 %reduce-scatter.7.cloned.1.call-done = f32[2,384,768]{2,1,0:T(8,128)} async-done(((f32[2,3072,768]{2,1,0:T(8,128)}), f32[2,384,768]{2,1,0:T(8,128)}) %reduce-scatter.7.cloned.1.call-update) | async-done | bytes 2359312 | tf_op jit(solution)/shard_map/reduce_scatter | solution.py:90
  1943.5 4.9 pad_maximum_fusion.4
  1950.1 12.8 all-reduce.10
  1962.9 165.6 %all-reduce.17.cloned.1.call-done = (f32[2,4,96,768]{3,2,1,0:T(8,128)}, f32[2,2,384,768]{3,2,1,0:T(8,128)}, f32[3840,96]{0,1:T(8,128)}, f32[480,768]{1,0:T(8,128)}) async-done(((f32[2,4,96,768]{3,2,1,0:T(8,128)}, f32[2,2,384,768]{3,2,1,0:T(8,128)}, f32[3840,96]{0,1:T(8,128)}, f32[480,768]{1,0:T(8,128)}), (f32[2,4,96,768]{3,2,1,0:T(8,128)}, f32[2,2,384,768]{3,2,1,0:T(8,128)}, f32[3840,96]{0,1:T(8,128)}, ...) | async-done | bytes 10027024 | tf_op jit(solution)/shard_map/psum | solution.py:288
  2128.5 2.4 multiply_reduce_fusion.4
  2130.9 2.5 multiply_reduce_fusion.5
  2133.4 4.2 multiply_reduce_fusion
  2141.4 37.2 %all-reduce.7 = (f32[]{:T(128)}, f32[5,2,768]{2,1,0:T(2,128)S(1)}) all-reduce(f32[]{:T(128)S(6)} %add.381, f32[5,2,768]{2,1,0:T(2,128)S(1)} %get-tuple-element.181), channel_id=1, replica_groups=mesh['dp'=4,'mp'=8] {'mp'}, use_global_device_ids=true, to_apply=%region_49.50 | all-reduce | flops 7681 | bytes 61448 | tf_op jit(solution)/shard_map/psum | solution.py:298
  2181.3 5.7 multiply_subtract_fusion.3
  2187.0 4.6 multiply_subtract_fusion.2
  2191.6 6.2 multiply_subtract_fusion.1
  2197.9 8.1 multiply_subtract_fusion
  (485 shorter events, 130.3 us)
Async XLA Ops:
  7.2 99.6 %all-gather.13.cloned.1.call-start = ((), (), s32[]{:S(2)}) async-start(), calls=%async_computation.6 | async-start | bytes 5308416 | tf_op jit(solution)/shard_map/all_gather | solution.py:75
  10.1 235.7 %all-gather.15.cloned.1.call-start = ((), (), s32[]{:S(2)}) async-start(), calls=%async_computation.7 | async-start | bytes 10616832 | tf_op jit(solution)/shard_map/all_gather | solution.py:76
  14.4 312.3 %all-gather.17.cloned.1.call-start = ((), (), s32[]{:S(2)}) async-start(), calls=%async_computation.8 | async-start | bytes 5308416 | tf_op jit(solution)/shard_map/all_gather | solution.py:75
  15.1 450.4 %all-gather.19.cloned.1.call-start = ((), (), s32[]{:S(2)}) async-start(), calls=%async_computation.9 | async-start | bytes 10616832 | tf_op jit(solution)/shard_map/all_gather | solution.py:76
  22.6 8.7 copy-start.129
  22.6 9.9 copy-start.128
  22.7 10.5 copy-start.57
  22.7 14.9 copy-start.118
  22.7 16.3 copy-start.116
  22.7 18.2 copy-start.79
  24.0 37.5 %all-to-all-start = ((f32[8,256,96]{1,2,0:T(8,128)}), f32[8,256,96]{1,2,0:T(8,128)S(1)}, u32[]{:S(2)}, u32[]{:S(2)}) async-start(f32[8,256,96]{1,2,0:T(8,128)} %broadcast_select_fusion), calls=%async_computation | async-start | bytes 1572864 | tf_op jit(solution)/shard_map/all_to_all | solution.py:218
  31.3 1279.7 %all-reduce.15.cloned.1.call-start = ((), (), s32[]{:S(2)}) async-start(), calls=%async_computation.10 | async-start | bytes 37748736
  33.2 82.5 %copy-start.71 = (f32[768]{0:T(1024)}, f32[768]{0:T(1024)S(1)}, u32[]{:S(2)}) copy-start(f32[768]{0:T(1024)S(1)} %get-tuple-element.157) | copy-start | bytes 9220
  33.2 224.2 %copy-start.65 = (f32[768]{0:T(1024)}, f32[768]{0:T(1024)S(1)}, u32[]{:S(2)}) copy-start(f32[768]{0:T(1024)S(1)} %get-tuple-element.155) | copy-start | bytes 9220
  33.2 224.2 %copy-start.95 = (f32[768]{0:T(1024)}, f32[768]{0:T(1024)S(1)}, u32[]{:S(2)}) copy-start(f32[768]{0:T(1024)S(1)} %get-tuple-element.154) | copy-start | bytes 9220
  33.2 305.0 %copy-start.68 = (f32[768]{0:T(1024)}, f32[768]{0:T(1024)S(1)}, u32[]{:S(2)}) copy-start(f32[768]{0:T(1024)S(1)} %get-tuple-element.153) | copy-start | bytes 9220
  33.3 305.0 %copy-start.97 = (f32[768]{0:T(1024)}, f32[768]{0:T(1024)S(1)}, u32[]{:S(2)}) copy-start(f32[768]{0:T(1024)S(1)} %get-tuple-element.152) | copy-start | bytes 9220
  33.3 443.9 %copy-start.62 = (f32[768]{0:T(1024)}, f32[768]{0:T(1024)S(1)}, u32[]{:S(2)}) copy-start(f32[768]{0:T(1024)S(1)} %get-tuple-element.151) | copy-start | bytes 9220
  33.3 443.9 %copy-start.93 = (f32[768]{0:T(1024)}, f32[768]{0:T(1024)S(1)}, u32[]{:S(2)}) copy-start(f32[768]{0:T(1024)S(1)} %get-tuple-element.150) | copy-start | bytes 9220
  33.3 445.7 %copy-start.60 = (f32[768]{0:T(1024)}, f32[768]{0:T(1024)S(1)}, u32[]{:S(2)}) copy-start(f32[768]{0:T(1024)S(1)} %get-tuple-element.149) | copy-start | bytes 9220
  41.0 204.9 %copy-start.101 = (f32[1,3072]{1,0:T(1,128)}, f32[1,3072]{1,0:T(1,128)S(1)}, u32[]{:S(2)}) copy-start(f32[1,3072]{1,0:T(1,128)S(1)} %get-tuple-element.218) | copy-start | bytes 36868
  41.0 424.6 %copy-start.103 = (f32[1,3072]{1,0:T(1,128)}, f32[1,3072]{1,0:T(1,128)S(1)}, u32[]{:S(2)}) copy-start(f32[1,3072]{1,0:T(1,128)S(1)} %get-tuple-element.217) | copy-start | bytes 36868
  62.2 47.7 %copy-start.81 = (f32[256]{0:T(256)}, f32[256]{0:T(256)S(1)}, u32[]{:S(2)}) copy-start(f32[256]{0:T(256)S(1)} %add_rsqrt_fusion.4) | copy-start | bytes 3076
  63.5 46.5 %copy-start.32 = (f32[256,768]{1,0:T(8,128)}, f32[256,768]{1,0:T(8,128)S(1)}, u32[]{:S(2)}) copy-start(f32[256,768]{1,0:T(8,128)S(1)} %fusion.75) | copy-start | bytes 2359300
  117.9 139.6 %copy-start.83 = (f32[256]{0:T(256)}, f32[256]{0:T(256)S(1)}, u32[]{:S(2)}) copy-start(f32[256]{0:T(256)S(1)} %broadcast_multiply_fusion.13) | copy-start | bytes 3076
  119.0 138.5 %copy-start.107 = (f32[256]{0:T(256)}, f32[256]{0:T(256)S(1)}, u32[]{:S(2)}) copy-start(f32[256]{0:T(256)S(1)} %add_rsqrt_fusion.3) | copy-start | bytes 3076
  245.8 11.6 copy-start.13
  245.8 11.6 copy-start.126
  259.0 79.3 %copy-start.89 = (f32[256]{0:T(256)}, f32[256]{0:T(256)S(1)}, u32[]{:S(2)}) copy-start(f32[256]{0:T(256)S(1)} %broadcast_multiply_fusion.12) | copy-start | bytes 3076
  260.1 78.2 %copy-start.113 = (f32[256]{0:T(256)}, f32[256]{0:T(256)S(1)}, u32[]{:S(2)}) copy-start(f32[256]{0:T(256)S(1)} %add_rsqrt_fusion.2) | copy-start | bytes 3076
  340.3 136.8 %copy-start.86 = (f32[256]{0:T(256)}, f32[256]{0:T(256)S(1)}, u32[]{:S(2)}) copy-start(f32[256]{0:T(256)S(1)} %broadcast_multiply_fusion.11) | copy-start | bytes 3076
  341.5 135.7 %copy-start.110 = (f32[256]{0:T(256)}, f32[256]{0:T(256)S(1)}, u32[]{:S(2)}) copy-start(f32[256]{0:T(256)S(1)} %add_rsqrt_fusion.1) | copy-start | bytes 3076
  465.6 11.6 copy-start.17
  465.6 11.6 copy-start.127
  627.6 6.8 collective-permute-start
  630.5 3.3 collective-permute-start.1
  644.0 7.7 slice-start.11
  645.8 5.9 copy-start.35
  645.8 5.8 copy-start.18
  645.9 5.8 copy-start.63
  645.9 5.8 copy-start.87
  696.7 12.1 copy-start.48
  696.7 12.2 copy-start.47
  727.0 900.0 %reduce-scatter.5.cloned.1.call-start = ((), (), s32[]{:S(2)}) async-start(), calls=%async_computation.4 | async-start | bytes 21233664 | tf_op jit(solution)/shard_map/reduce_scatter | solution.py:90
  739.4 1204.0 %reduce-scatter.7.cloned.1.call-start = ((), (), s32[]{:S(2)}) async-start(), calls=%async_computation.5 | async-start | bytes 21233664 | tf_op jit(solution)/shard_map/reduce_scatter | solution.py:90
  756.7 6.4 copy-start.43
  756.7 6.4 copy-start.75
  756.7 6.4 copy-start.80
  756.7 6.4 copy-start.106
  756.8 6.4 copy-start.117
  758.2 40.5 %all-to-all-start.1 = ((f32[256,8,96]{0,2,1:T(8,128)}), f32[256,8,96]{0,2,1:T(8,128)S(1)}, u32[]{:S(2)}, u32[]{:S(2)}) async-start(f32[256,8,96]{0,2,1:T(8,128)} %bitcast.83), calls=%async_computation.3 | async-start | bytes 1572864 | tf_op jit(solution)/shard_map/all_to_all | solution.py:285
  762.3 1366.2 %all-reduce.17.cloned.1.call-start = ((), (), s32[]{:S(2)}) async-start(), calls=%async_computation.11 | async-start | bytes 20054016 | tf_op jit(solution)/shard_map/psum | solution.py:288
  2130.9 6.7 copy-start.7
  2133.4 47.2 %copy-start.58 = (f32[5,2,768]{2,1,0:T(2,128)S(1)}, f32[5,2,768]{2,1,0:T(2,128)}, u32[]{:S(2)}) copy-start(f32[5,2,768]{2,1,0:T(2,128)} %param.39) | copy-start | bytes 92164
  2133.4 47.2 %copy-start.76 = (f32[5,2,768]{2,1,0:T(2,128)S(1)}, f32[5,2,768]{2,1,0:T(2,128)}, u32[]{:S(2)}) copy-start(f32[5,2,768]{2,1,0:T(2,128)} %param.41) | copy-start | bytes 92164
  2133.4 47.2 %copy-start.77 = (f32[5,2,768]{2,1,0:T(2,128)S(1)}, f32[5,2,768]{2,1,0:T(2,128)}, u32[]{:S(2)}) copy-start(f32[5,2,768]{2,1,0:T(2,128)} %param.40) | copy-start | bytes 92164
  2181.3 10.3 copy-start.6
  2181.3 10.3 copy-start.46
  2187.0 10.8 slice-start
  2187.0 10.8 slice-start.2
  2187.0 10.8 slice-start.4
  2191.6 6.2 slice-start.1
  2191.6 6.3 slice-start.3
  2191.6 6.3 slice-start.5
  (95 other events, 244.8 us)
Sparse Core Ops, SparseCore 0:
  10.8 95.9 all-gather.12
  109.6 136.1 all-gather.14
  248.6 78.0 all-gather.16
  329.3 136.1 all-gather.18
  727.1 583.8 all-reduce.14
  1314.7 312.2 reduce-scatter.4
  1630.9 312.5 reduce-scatter.6
  1948.5 179.9 all-reduce.16
where the time goes:
time: 2220 us; the launch traced here: 2210 us
  waiting for transfers between devices  1710 us (77%)
  blocking collectives  140 us (6%)
  other arithmetic  124 us (6%)
  local copies, waits for them, and re-layouts  101 us (5%)
  matrix products  101 us (5%)
  between operations  24.5 us (1%)
    reduce_scatter x2, waiting for transfers between devices, reduce_layer(): lax.psum_scatter(ffn_grad, 'mp', scatter_dimension=1, tiled=True)  628 us
    unnamed x11, waiting for transfers between devices  500 us
    all_gather x2, waiting for transfers between devices, fetch_forward(): lax.all_gather(ffn_part, 'mp', axis=1, tiled=True)  250 us
    psum x1, waiting for transfers between devices, local(): lax.psum((jnp.stack(attn_parts), jnp.stack(ffn_parts), table_grad, out_gr...  166 us
    all_gather x2, waiting for transfers between devices, fetch_forward(): lax.all_gather(attn_part, 'mp', axis=1, tiled=True)  110 us
    unnamed x2, blocking collectives  58.9 us
  transfers between devices with their start and end apart: 12, of which 11 were waited for; matrix products, arithmetic and copies ran while one was open for 5% of the time, Pallas kernels for 0%

commit v1 on v0

--- a/solution.py
+++ b/solution.py
@@ -1,8 +1,11 @@
+import functools
 import math
 
 import jax
 import jax.numpy as jnp
 from jax import lax
+from jax.experimental import pallas as pl
+from jax.experimental.pallas import tpu as pltpu
 from jax.sharding import PartitionSpec as P
 
 HEADS = 12
@@ -20,6 +23,361 @@
 adam_eps = 1e-08
 clip_limit = 1.0
 masked_score = -1000000000.0
+
+
+MESH = pl.DeviceIdType.MESH
+VMEM_LIMIT = 60 * 1024 * 1024
+
+
+def dot_nn(left, right):
+    return lax.dot_general(
+        left, right, (((1,), (0,)), ((), ())), preferred_element_type=jnp.float32
+    )
+
+
+def dot_nt(left, right):
+    return lax.dot_general(
+        left, right, (((1,), (1,)), ((), ())), preferred_element_type=jnp.float32
+    )
+
+
+def dot_tn(left, right):
+    return lax.dot_general(
+        left, right, (((0,), (0,)), ((), ())), preferred_element_type=jnp.float32
+    )
+
+
+def ring_index(place, n):
+    late = place // (n // 2)
+    return (1 - late) * 2 * place + late * (2 * (n - 1 - place) + 1)
+
+
+def ring_place(index, n):
+    odd = index % 2
+    return (1 - odd) * (index // 2) + odd * (n - 1 - index // 2)
+
+
+class Spot:
+    def __init__(self, n):
+        self.n = n
+        self.dp = lax.axis_index("dp")
+        self.mp = lax.axis_index("mp")
+        self.core = self.dp % 2
+        self.place = ring_place(self.mp, n)
+        self.partner = (self.dp + 1 - 2 * self.core, self.mp)
+        self.across = ((self.dp + 2) % 4, self.mp)
+        self.ring = (
+            (self.dp, ring_index((self.place + 1) % n, n)),
+            (self.dp, ring_index((self.place + n - 1) % n, n)),
+        )
+
+    def shard(self, offset):
+        return ring_index((self.place + offset + self.n) % self.n, self.n)
+
+
+def greet(devices):
+    barrier = pltpu.get_barrier_semaphore()
+    for device in devices:
+        pl.semaphore_signal(barrier, inc=1, device_id=device, device_id_type=MESH)
+    pl.semaphore_wait(barrier, len(devices))
+
+
+def last_step(n, way, part):
+    return n // 2 if way == part else n // 2 - 1
+
+
+WAYS = ((0, 0), (1, 1), (0, 1), (1, 0))
+
+
+def normed_of(values):
+    centre = jnp.mean(values, axis=-1, keepdims=True)
+    offset = values - centre
+    spread = jnp.mean(offset * offset, axis=-1, keepdims=True)
+    inverse = lax.rsqrt(spread + norm_eps)
+    return offset * inverse, inverse
+
+
+def forward_kernel(
+    n,
+    visible_ref,
+    states_ref,
+    gains_ref,
+    mask_ref,
+    attn_sh,
+    ffn_sh,
+    attn_full,
+    ffn_full,
+    final_ref,
+    inputs_ref,
+    proj_ref,
+    mixed_ref,
+    pre_ref,
+    mid_ref,
+    slope_ref,
+    act_ref,
+    wa,
+    wf,
+    state,
+    own_sem,
+    out_sem,
+    ring_send,
+    ring_recv,
+    core_send,
+    core_recv,
+):
+    spot = Spot(n)
+    core = spot.core
+    rows_a = attn_sh.shape[2]
+    rows_f = ffn_sh.shape[2]
+    part_f = rows_f // 2
+    width = attn_sh.shape[3]
+    steps = n // 2
+
+    def rows_at(shard, rows):
+        return pl.ds(pl.multiple_of(shard * rows, 16), rows)
+
+    def chunk(piece, shard, part):
+        kind, depth = piece % 2, piece // 2
+        if kind == 0:
+            return wa.at[depth, 2 * core + part, rows_at(shard, rows_a), :]
+        start = pl.multiple_of(shard * rows_f + part * part_f, 16)
+        return wf.at[depth, core, pl.ds(start, part_f), :]
+
+    def chunk_other(piece, shard, part):
+        kind, depth = piece % 2, piece // 2
+        if kind == 0:
+            return wa.at[depth, 2 * (1 - core) + part, rows_at(shard, rows_a), :]
+        start = pl.multiple_of(shard * rows_f + part * part_f, 16)
+        return wf.at[depth, 1 - core, pl.ds(start, part_f), :]
+
+    def chunk_own(piece, part):
+        kind, depth = piece % 2, piece // 2
+        if kind == 0:
+            return attn_sh.at[depth, 2 * core + part]
+        return ffn_sh.at[depth, core, pl.ds(part * part_f, part_f), :]
+
+    def sign(way):
+        return -1 if way == 0 else 1
+
+    def ring_out(piece, way, part, step):
+        target = chunk(piece, spot.shard(sign(way) * (step - 1)), part)
+        return pltpu.make_async_remote_copy(
+            src_ref=chunk_own(piece, part) if step == 1 else target,
+            dst_ref=target,
+            send_sem=ring_send.at[piece, way, part, step - 1],
+            recv_sem=ring_recv.at[piece, way, part, step - 1],
+            device_id=spot.ring[way],
+            device_id_type=MESH,
+        )
+
+    def ring_in(piece, way, part, step):
+        target = chunk(piece, spot.shard(sign(way) * step), part)
+        return pltpu.make_async_remote_copy(
+            src_ref=target,
+            dst_ref=target,
+            send_sem=ring_send.at[piece, way, part, step - 1],
+            recv_sem=ring_recv.at[piece, way, part, step - 1],
+            device_id=spot.ring[way],
+            device_id_type=MESH,
+        )
+
+    def core_out(piece, way, part, step):
+        target = chunk(piece, spot.shard(sign(way) * step), part)
+        return pltpu.make_async_remote_copy(
+            src_ref=target,
+            dst_ref=target,
+            send_sem=core_send.at[piece, way, part, step - 1],
+            recv_sem=core_recv.at[piece, way, part, step - 1],
+            device_id=spot.partner,
+            device_id_type=MESH,
+        )
+
+    def core_in(piece, way, part, step):
+        target = chunk_other(piece, spot.shard(sign(way) * step), part)
+        return pltpu.make_async_remote_copy(
+            src_ref=target,
+            dst_ref=target,
+            send_sem=core_send.at[piece, way, part, step - 1],
+            recv_sem=core_recv.at[piece, way, part, step - 1],
+            device_id=spot.partner,
+            device_id_type=MESH,
+        )
+
+    own_copies = []
+    for depth in range(LAYERS):
+        for which in range(4):
+            own_copies.append(
+                pltpu.make_async_copy(
+                    attn_sh.at[depth, which],
+                    wa.at[depth, which, rows_at(spot.mp, rows_a), :],
+                    own_sem.at[2 * depth, which],
+                )
+            )
+        for which in range(2):
+            own_copies.append(
+                pltpu.make_async_copy(
+                    ffn_sh.at[depth, which],
+                    wf.at[depth, which, rows_at(spot.mp, rows_f), :],
+                    own_sem.at[2 * depth + 1, which],
+                )
+            )
+    greet((spot.ring[0], spot.ring[1], spot.partner))
+
+    def launch(piece):
+        for way, part in WAYS:
+            ring_out(piece, way, part, 1).start()
+
+    def pass_on(piece, step):
+        for way, part in WAYS:
+            if step <= last_step(n, way, part):
+                ring_in(piece, way, part, step).wait_recv()
+                if step < last_step(n, way, part):
+                    ring_out(piece, way, part, step + 1).start()
+                core_out(piece, way, part, step).start()
+
+    def settle(piece, step):
+        for way, part in WAYS:
+            if step <= last_step(n, way, part):
+                core_in(piece, way, part, step).wait_recv()
+
+    launch(0)
+    for copy in own_copies:
+        copy.start()
+    state[...] = states_ref[...]
+    for copy in own_copies:
+        copy.wait()
+
+    lanes = lax.broadcasted_iota(jnp.int32, (1, 128), 1) < 64
+    visible = visible_ref[...] > 0.0
+
+    def head_pair(depth, pair):
+        columns = pl.ds(pl.multiple_of(pair * 128, 128), 128)
+        query = proj_ref[depth, 0, :, columns]
+        keyed = proj_ref[depth, 1, :, columns]
+        valued = proj_ref[depth, 2, :, columns]
+        outs = []
+        for side in range(2):
+            mine = lanes if side == 0 else jnp.logical_not(lanes)
+            scores = dot_nt(jnp.where(mine, query, jnp.zeros_like(query)), keyed) * 0.125
+            scores = jnp.where(visible, scores, masked_score)
+            expo = jnp.exp(scores - jnp.max(scores, axis=-1, keepdims=True))
+            total = jnp.sum(expo, axis=-1, keepdims=True)
+            outs.append(dot_nn((expo / total).astype(jnp.bfloat16), valued))
+        mixed_ref[depth, :, columns] = jnp.where(lanes, outs[0], outs[1]).astype(jnp.bfloat16)
+
+    def ffn_shard(depth, offset):
+        shard = spot.shard(offset)
+        rows = rows_at(shard, rows_f)
+        hidden = dot_nt(mid_ref[depth], wf[depth, 0, rows, :])
+        spread = 0.5 * (1.0 + lax.erf(hidden * (0.5**0.5)))
+        mask = mask_ref[depth : depth + 1, pl.ds(pl.multiple_of(shard * rows_f, 128), rows_f)]
+        bell = jnp.exp(hidden * hidden * -0.5) * (1.0 / math.sqrt(2.0 * math.pi))
+        slope_ref[depth, shard] = (spread + hidden * bell) * mask
+        active = (hidden * spread * mask).astype(jnp.bfloat16)
+        act_ref[depth, shard] = active
+        pre_ref[depth, 1] += dot_nn(active, wf[depth, 1, rows, :])
+
+    out_copies = []
+    for depth in range(LAYERS):
+        piece_a, piece_f = 2 * depth, 2 * depth + 1
+        for step in range(1, steps + 1):
+            pass_on(piece_a, step)
+            if step == steps - 1:
+                launch(piece_f)
+        for step in range(1, steps + 1):
+            settle(piece_a, step)
+        copy = pltpu.make_async_copy(wa.at[depth], attn_full.at[depth], out_sem.at[piece_a])
+        copy.start()
+        out_copies.append(copy)
+        inputs = state[...].astype(jnp.bfloat16)
+        inputs_ref[depth] = inputs
+        for which in range(3):
+            proj_ref[depth, which] = dot_nn(inputs, wa[depth, which]).astype(jnp.bfloat16)
+        pass_on(piece_f, 1)
+
+        @pl.loop(0, HEADS // 2)
+        def _(pair):
+            head_pair(depth, pair)
+
+        pre_ref[depth, 0] = state[...] + dot_nn(mixed_ref[depth], wa[depth, 3])
+        normed, _ = normed_of(pre_ref[depth, 0])
+        middle = (
+            normed * gains_ref[1 + 2 * depth, 0:1, :] + gains_ref[1 + 2 * depth, 1:2, :]
+        )
+        mid_ref[depth] = middle.astype(jnp.bfloat16)
+        pre_ref[depth, 1] = middle
+        ffn_shard(depth, 0)
+        pass_on(piece_f, 2)
+        settle(piece_f, 1)
+        ffn_shard(depth, -1)
+        ffn_shard(depth, 1)
+        pass_on(piece_f, 3)
+        if depth + 1 < LAYERS:
+            launch(piece_a + 2)
+        settle(piece_f, 2)
+        ffn_shard(depth, -2)
+        ffn_shard(depth, 2)
+        settle(piece_f, 3)
+        ffn_shard(depth, -3)
+        ffn_shard(depth, 3)
+        pass_on(piece_f, 4)
+        settle(piece_f, 4)
+        ffn_shard(depth, 4)
+        copy = pltpu.make_async_copy(wf.at[depth], ffn_full.at[depth], out_sem.at[piece_f])
+        copy.start()
+        out_copies.append(copy)
+        normed, _ = normed_of(pre_ref[depth, 1])
+        state[...] = normed * gains_ref[2 + 2 * depth, 0:1, :] + gains_ref[2 + 2 * depth, 1:2, :]
+    final_ref[...] = state[...]
+    for piece in range(2 * LAYERS):
+        for way, part in WAYS:
+            for step in range(1, last_step(n, way, part) + 1):
+                ring_out(piece, way, part, step).wait_send()
+                core_out(piece, way, part, step).wait_send()
+    for copy in out_copies:
+        copy.wait()
+
+
+def forward_call(n, visible, states, gains, masks, attn_b, ffn_b):
+    count, width = states.shape
+    rows_f = ffn_b.shape[2]
+    f32, bf16 = jnp.float32, jnp.bfloat16
+    vmem = pl.BlockSpec(memory_space=pltpu.VMEM)
+    anywhere = pl.BlockSpec(memory_space=pl.ANY)
+    shape = jax.ShapeDtypeStruct
+    sems = pltpu.SemaphoreType.DMA((2 * LAYERS, 2, 2, n // 2))
+    return pl.pallas_call(
+        functools.partial(forward_kernel, n),
+        out_shape=(
+            shape((LAYERS, 4, width, width), bf16),
+            shape((LAYERS, 2, rows_f * n, width), bf16),
+            shape((count, width), f32),
+            shape((LAYERS, count, width), bf16),
+            shape((LAYERS, 3, count, width), bf16),
+            shape((LAYERS, count, width), bf16),
+            shape((LAYERS, 2, count, width), f32),
+            shape((LAYERS, count, width), bf16),
+            shape((LAYERS, n, count, rows_f), f32),
+            shape((LAYERS, n, count, rows_f), bf16),
+        ),
+        in_specs=[vmem, vmem, vmem, vmem, anywhere, anywhere],
+        out_specs=(anywhere, anywhere) + (vmem,) * 8,
+        scratch_shapes=[
+            pltpu.VMEM((LAYERS, 4, width, width), bf16),
+            pltpu.VMEM((LAYERS, 2, rows_f * n, width), bf16),
+            pltpu.VMEM((count, width), f32),
+            pltpu.SemaphoreType.DMA((2 * LAYERS, 4)),
+            pltpu.SemaphoreType.DMA((2 * LAYERS,)),
+            sems,
+            sems,
+            sems,
+            sems,
+        ],
+        compiler_params=pltpu.CompilerParams(
+            collective_id=1, has_side_effects=True, vmem_limit_bytes=VMEM_LIMIT
+        ),
+        name="forward_layers",
+    )(visible, states, gains, masks, attn_b, ffn_b)
 
 
 def merged(value, axis, join):
@@ -183,6 +541,204 @@
     peak = jnp.maximum(first[0], second[0])
     total = first[1] * jnp.exp(first[0] - peak) + second[1] * jnp.exp(second[0] - peak)
     return (peak, total, first[2] + second[2])
+
+
+def ffn_backward_kept(grad_out, middle_b, hidden, active, ffn_w, unit_mask):
+    grad_active = jnp.einsum("td,fd->tf", grad_out, ffn_w[1], preferred_element_type=jnp.float32)
+    grad_hidden = (hidden * grad_active).astype(jnp.bfloat16)
+    up_grad = jnp.einsum("tf,td->fd", grad_hidden, middle_b, preferred_element_type=jnp.float32)
+    down_grad = jnp.einsum("tf,td->fd", active, grad_out, preferred_element_type=jnp.float32)
+    from_ffn = jnp.einsum("tf,fd->td", grad_hidden, ffn_w[0], preferred_element_type=jnp.float32)
+    return (jnp.stack([up_grad, down_grad]), from_ffn)
+
+
+def layer_backward_kept(grad, attn_w, ffn_w, pair, length, unit_mask, kept):
+    inputs, heads, log_total, mixed, norm_one, middle_b, hidden, active, norm_two = kept
+    count = inputs.shape[0]
+    grad_two, pair_two = norm_backward(grad, norm_two, pair[1, 0])
+    ffn_grad, from_ffn = ffn_backward_kept(
+        grad_two.astype(jnp.bfloat16), middle_b, hidden, active, ffn_w, unit_mask
+    )
+    grad_one, pair_one = norm_backward(grad_two + from_ffn, norm_one, pair[0, 0])
+    grad_branch = grad_one.astype(jnp.bfloat16)
+    output_grad = jnp.einsum("td,te->de", mixed, grad_branch, preferred_element_type=jnp.float32)
+    grad_mixed = jnp.einsum("te,de->td", grad_branch, attn_w[3], preferred_element_type=jnp.float32)
+    grad_mixed = grad_mixed.astype(jnp.bfloat16).reshape(count, HEADS, -1).transpose(1, 0, 2)
+    scale = heads.shape[-1] ** (-0.5)
+    probs = jnp.exp(masked_scores(heads[0], heads[1], length) - log_total)
+    grad_values = jnp.einsum(
+        "hqk,hqe->hke", probs.astype(jnp.bfloat16), grad_mixed, preferred_element_type=jnp.float32
+    )
+    grad_probs = jnp.einsum(
+        "hqe,hke->hqk", grad_mixed, heads[2], preferred_element_type=jnp.float32
+    )
+    grad_scores = probs * (grad_probs - jnp.sum(grad_probs * probs, axis=-1, keepdims=True))
+    grad_scores = grad_scores.astype(jnp.bfloat16)
+    grad_query = (
+        jnp.einsum("hqk,hke->hqe", grad_scores, heads[1], preferred_element_type=jnp.float32)
+        * scale
+    )
+    grad_key = (
+        jnp.einsum("hqk,hqe->hke", grad_scores, heads[0], preferred_element_type=jnp.float32)
+        * scale
+    )
+    stacked = (
+        jnp.stack([grad_query, grad_key, grad_values]).transpose(0, 2, 1, 3).reshape(3, count, -1)
+    )
+    stacked = stacked.astype(jnp.bfloat16)
+    input_grad = jnp.einsum("td,kte->kde", inputs, stacked, preferred_element_type=jnp.float32)
+    from_attn = jnp.einsum("kte,kde->td", stacked, attn_w[:3], preferred_element_type=jnp.float32)
+    attn_grad = jnp.concatenate([input_grad, output_grad[None]], axis=0)
+    return (grad_one + from_attn, attn_grad, ffn_grad, jnp.stack([pair_one, pair_two]))
+
+
+def local_general(
+    tokens,
+    lengths,
+    places,
+    targets,
+    ramp,
+    attn,
+    attn_m,
+    attn_v,
+    ffn,
+    ffn_m,
+    ffn_v,
+    table,
+    table_m,
+    table_v,
+    out_table,
+    out_m,
+    out_v,
+    gains,
+    gains_m,
+    gains_v,
+):
+    rank = lax.axis_index("mp")
+    count = tokens.shape[2]
+    flat_ids = tokens.reshape(-1)
+    all_lengths = lengths.reshape(-1)
+    length = lax.dynamic_index_in_dim(all_lengths, rank, keepdims=False)
+    masks = jnp.minimum(ramp, RAMP).astype(jnp.float32) / RAMP
+    unit_masks = [masks[depth] for depth in range(LAYERS)]
+    looked = jnp.take(table, flat_ids, axis=0)
+    embedded = lax.all_to_all(looked, "mp", split_axis=0, concat_axis=1, tiled=True)
+    states, norm_zero = layer_norm(
+        embedded + sinusoid(count, embedded.shape[1]), gains[0, 0], gains[0, 1]
+    )
+    kept_all = []
+    weights_all = []
+    for depth in range(LAYERS):
+        attn_w, ffn_w = fetch_forward(
+            attn[depth].astype(jnp.bfloat16), ffn[depth].astype(jnp.bfloat16)
+        )
+        states, kept = layer_forward(
+            states, attn_w, ffn_w, gains[1 + 2 * depth : 3 + 2 * depth], length, unit_masks[depth]
+        )
+        kept_all.append(kept)
+        weights_all.append(None)
+    spots = places.reshape(-1)
+    picked = jnp.take(states, spots, axis=0).astype(jnp.bfloat16)
+    picked_all = lax.all_gather(picked, "mp", axis=0, tiled=True)
+    out_b = out_table.astype(jnp.bfloat16)
+    logits = jnp.einsum("rd,vd->rv", picked_all, out_b, preferred_element_type=jnp.float32)
+    labels = targets.reshape(-1)
+    columns = rank * out_table.shape[0] + jnp.arange(out_table.shape[0])
+    hits = (labels[:, None] == columns[None, :]).astype(jnp.float32)
+    peak = jnp.max(logits, axis=1)
+    expsum = jnp.sum(jnp.exp(logits - peak[:, None]), axis=1)
+    target_part = jnp.sum(hits * logits, axis=1)
+    peak_all, expsum_all, target_all = merged((peak, expsum, target_part), "mp", combine_vocab)
+    log_total = peak_all + jnp.log(expsum_all)
+    slot_count = targets.shape[2]
+    counted = jnp.maximum(1, all_lengths * slot_count // count)
+    valid = (jnp.arange(slot_count)[None, :] < counted[:, None]).reshape(-1)
+    loss_pair = jnp.stack(
+        [
+            jnp.sum(jnp.where(valid, log_total - target_all, 0.0)),
+            jnp.sum(counted).astype(jnp.float32),
+        ]
+    )
+    grad_logits = jnp.where(
+        valid[:, None], jnp.exp(logits - log_total[:, None]) - hits, 0.0
+    ).astype(jnp.bfloat16)
+    out_grad = jnp.einsum("rv,rd->vd", grad_logits, picked_all, preferred_element_type=jnp.float32)
+    picked_grad = lax.psum_scatter(
+        jnp.dot(grad_logits, out_b, preferred_element_type=jnp.float32),
+        "mp",
+        scatter_dimension=0,
+        tiled=True,
+    )
+    grad = jnp.zeros_like(states).at[spots].add(picked_grad)
+    attn_parts = [None] * LAYERS
+    ffn_parts = [None] * LAYERS
+    pair_grads = [None] * LAYERS
+    for depth in reversed(range(LAYERS)):
+        attn_w, ffn_w = fetch_backward(
+            attn[depth].astype(jnp.bfloat16), ffn[depth].astype(jnp.bfloat16)
+        )
+        grad, attn_grad, ffn_grad, pair_grad = layer_backward(
+            grad,
+            attn_w,
+            ffn_w,
+            gains[1 + 2 * depth : 3 + 2 * depth],
+            length,
+            unit_masks[depth],
+            kept_all[depth],
+        )
+        attn_parts[depth], ffn_parts[depth] = reduce_layer(attn_grad, ffn_grad)
+        pair_grads[depth] = pair_grad
+    grad_sum, zero_grad = norm_backward(grad, norm_zero, gains[0, 0])
+    returned = lax.all_to_all(grad_sum, "mp", split_axis=1, concat_axis=0, tiled=True)
+    table_grad = jnp.zeros_like(table).at[flat_ids].add(returned)
+    gains_grad = jnp.concatenate([zero_grad[None]] + pair_grads, axis=0)
+    attn_sum, ffn_sum, table_sum, out_sum, gains_part, loss = lax.psum(
+        (jnp.stack(attn_parts), jnp.stack(ffn_parts), table_grad, out_grad, gains_grad, loss_pair),
+        "dp",
+    )
+    shard_squares = (
+        jnp.sum(attn_sum * attn_sum)
+        + jnp.sum(ffn_sum * ffn_sum)
+        + jnp.sum(table_sum * table_sum)
+        + jnp.sum(out_sum * out_sum)
+    )
+    square_total, gains_sum = lax.psum((shard_squares, gains_part), "mp")
+    grad_norm = jnp.sqrt(square_total + jnp.sum(gains_sum * gains_sum))
+    factor = clip_limit / jnp.maximum(grad_norm, clip_limit)
+    attn_m_new, attn_v_new, attn_new = adamw(
+        attn, attn_m, attn_v, attn_sum * factor, weight_decay, learn_rate
+    )
+    ffn_m_new, ffn_v_new, ffn_new = adamw(
+        ffn, ffn_m, ffn_v, ffn_sum * factor, weight_decay, learn_rate
+    )
+    table_m_new, table_v_new, table_new = adamw(
+        table, table_m, table_v, table_sum * factor, weight_decay, learn_rate
+    )
+    out_m_new, out_v_new, out_new = adamw(
+        out_table, out_m, out_v, out_sum * factor, weight_decay, learn_rate
+    )
+    gains_m_new, gains_v_new, gains_new = adamw(
+        gains, gains_m, gains_v, gains_sum * factor, 0.0, gain_rate
+    )
+    return (
+        loss,
+        grad_norm.reshape(1),
+        attn_m_new,
+        attn_v_new,
+        attn_new,
+        ffn_m_new,
+        ffn_v_new,
+        ffn_new,
+        table_m_new,
+        table_v_new,
+        table_new,
+        out_m_new,
+        out_v_new,
+        out_new,
+        gains_m_new,
+        gains_v_new,
+        gains_new,
+    )
 
 
 def local(
@@ -219,17 +775,22 @@
     states, norm_zero = layer_norm(
         embedded + sinusoid(count, embedded.shape[1]), gains[0, 0], gains[0, 1]
     )
+    n = attn.shape[3] // attn.shape[2]
+    visible = (jnp.arange(count) < length).astype(jnp.float32)[None, :]
+    (
+        attn_full, ffn_full, states, inputs_all, proj_all, mixed_all, pre_all, mid_all, slope_all, act_all,
+    ) = forward_call(
+        n, visible, states, gains, masks, attn.astype(jnp.bfloat16), ffn.astype(jnp.bfloat16)
+    )
     kept_all = []
-    weights_all = []
     for depth in range(LAYERS):
-        attn_w, ffn_w = fetch_forward(
-            attn[depth].astype(jnp.bfloat16), ffn[depth].astype(jnp.bfloat16)
-        )
-        states, kept = layer_forward(
-            states, attn_w, ffn_w, gains[1 + 2 * depth : 3 + 2 * depth], length, unit_masks[depth]
-        )
-        kept_all.append(kept)
-        weights_all.append(None)
+        heads = proj_all[depth].reshape(3, count, HEADS, -1).transpose(0, 2, 1, 3)
+        scores = masked_scores(heads[0], heads[1], length)
+        log_total = jax.nn.logsumexp(scores, axis=-1, keepdims=True)
+        slope = slope_all[depth].transpose(1, 0, 2).reshape(count, -1)
+        act = act_all[depth].transpose(1, 0, 2).reshape(count, -1)
+        kept_all.append((inputs_all[depth], heads, log_total, mixed_all[depth], normed_of(pre_all[depth, 0]),
+           mid_all[depth], slope, act, normed_of(pre_all[depth, 1])))
     spots = places.reshape(-1)
     picked = jnp.take(states, spots, axis=0).astype(jnp.bfloat16)
     picked_all = lax.all_gather(picked, "mp", axis=0, tiled=True)
@@ -267,10 +828,8 @@
     ffn_parts = [None] * LAYERS
     pair_grads = [None] * LAYERS
     for depth in reversed(range(LAYERS)):
-        attn_w, ffn_w = fetch_backward(
-            attn[depth].astype(jnp.bfloat16), ffn[depth].astype(jnp.bfloat16)
-        )
-        grad, attn_grad, ffn_grad, pair_grad = layer_backward(
+        attn_w, ffn_w = attn_full[depth], ffn_full[depth]
+        grad, attn_grad, ffn_grad, pair_grad = layer_backward_kept(
             grad,
             attn_w,
             ffn_w,
@@ -376,4 +935,7 @@
         P(),
         P(),
     )
-    return jax.shard_map(local, mesh=mesh, in_specs=in_specs, out_specs=out_specs, check_vma=False)
+    rows_attn, rows_ffn = 768 // mesh.shape['mp'], 3072 // mesh.shape['mp']
+    fits = mesh.shape['mp'] == 8
+    chosen = local if fits else local_general
+    return jax.shard_map(chosen, mesh=mesh, in_specs=in_specs, out_specs=out_specs, check_vma=False)

time: 2220 us -> 1980 us (0.89)
  waiting for transfers between devices: 1710 us -> 1320 us
  Pallas kernels: 0 us -> 150 us
  matrix products: 101 us -> 62.5 us
  local copies, waits for them, and re-layouts: 101 us -> 132 us
    all_gather x4 -> x0, waiting for transfers between devices: 360 us -> none  [the longest x2 250 us: fetch_forward(): lax.all_gather(ffn_part, 'mp', axis=1, tiled=True)]
    pallas_call x0 -> x1, Pallas kernels: none -> 150 us  [forward_call(): pl.pallas_call(functools.partial(forward_kernel, n), out_shape=(shape((LA...]
    dot_general x34 -> x24, matrix products: 90.2 us -> 49.8 us  [the longest x2 10.5 us: ffn_backward_kept(): jnp.einsum('tf,fd->td', grad_hidden, ffn_w[0], preferred_element_type=jnp...]
    unnamed x11 -> x7, waiting for transfers between devices: 500 us -> 490 us
  transfers between devices with their start and end apart: 12 -> 8, of which waited for: 11 -> 6; matrix products, arithmetic and copies ran while one was open for 5% -> 6% of each run, Pallas kernels for 0% -> 0%
where the time goes in v1:
time: 1980 us; the launch traced here: 1970 us
  waiting for transfers between devices  1320 us (67%)
  Pallas kernels  150 us (8%)
  blocking collectives  141 us (7%)
  local copies, waits for them, and re-layouts  132 us (7%)
  other arithmetic  127 us (6%)
  matrix products  62.5 us (3%)
  between operations  23.4 us (1%)
    reduce_scatter x2, waiting for transfers between devices, reduce_layer(): lax.psum_scatter(ffn_grad, 'mp', scatter_dimension=1, tiled=True)  628 us
    unnamed x7, waiting for transfers between devices  490 us
    psum x1, waiting for transfers between devices, local(): lax.psum((jnp.stack(attn_parts), jnp.stack(ffn_parts), table_grad, out_gr...  166 us
    pallas_call x1, Pallas kernels, forward_call(): pl.pallas_call(functools.partial(forward_kernel, n), out_shape=(shape((LA...  150 us
    unnamed x2, blocking collectives  59.6 us
  transfers between devices with their start and end apart: 8, of which 6 were waited for; matrix products, arithmetic and copies ran while one was open for 6% of the time, Pallas kernels for 0%

profile of v1, /device:TPU:0, one launch (start us, length us, event | category | flops | bytes accessed | tf_op | source)
XLA Modules:
  0.0 1973.8 jit_solution(8476435551156402715)
XLA Ops:
  7.2 1.8 copy.182
  9.7 7.6 gather_fusion
  20.0 7.3 all-to-all-start
  33.4 4.0 convert_element_type.95.ffn_sh
  44.2 3.2 all-to-all-done
  49.5 150.2 %forward_layers.1 = (bf16[2,4,768,768]{3,2,1,0:T(8,128)(2,1)}, bf16[2,2,3072,768]{3,2,1,0:T(8,128)(2,1)}, f32[256,768]{1,0:T(8,128)}, bf16[2,256,768]{2,1,0:T(8,...) custom-call(f32[1,256]{1,0:T(1,128)} %compare_convert_fusion.1.visib, ...), custom_call_target="tpu_custom_call" | custom-call | tf_op jit(solution)/shard_map/forward_layers/pallas_call | solution.py:349
  201.5 31.2 %all-gather.3 = bf16[8,25,768]{2,1,0:T(8,128)(2,1)S(1)} all-gather(bf16[1,25,768]{2,1,0:T(8,128)(2,1)S(1)} %fusion.131), channel_id=1, replica_groups=mesh['dp'=4,'mp'=8] {'mp'}, dimensions={0}, use_global_device_ids=true | all-gather | bytes 345600 | tf_op jit(solution)/shard_map/all_gather | solution.py:796
  242.6 36.1 %all-reduce.8 = (f32[1600]{0:T(1024)}, f32[1600]{0:T(1024)}, f32[1600]{0:T(1024)}) all-reduce(f32[1600]{0:T(1024)} %dynamic-update-slice, f32[1600]{0:T(1024)} %dynamic-update-slice.1, f32[1600]{0:T(1024)} %dynamic-update-slice.2), channel_id=2, replica_groups=mesh['dp'=4,'mp'=8] {'mp'}, use_global_device_ids=true, to_apply=%add | all-reduce | flops 4800 | bytes 38400
  290.6 27.5 %while.14 = (s32[]{:T(128)}, f32[200]{0:T(256)}, f32[200]{0:T(256)}, f32[200]{0:T(256)}, f32[7,200]{1,0:T(8,128)}, /*index=5*/f32[7,200]{1,0:T(8,128)}, f32[7,200]{1,0:T(8,128)}, s32[]{:T(128)}) while((s32[]{:T(128)}, f32[200]{0:T(256)}, f32[200]{0:T(256)}, f32[200]{0:T(256)}, f32[7,200]{1,0:T(8,128)}, /*index=5*/f32[7,200]{1,0:T(8,128)}, ...), condition=%wide.region_6.7_spmd, body=%wide.region_5.6_spmd.sunk | while | flops 1402 | bytes 12101 | solution.py:387
  320.2 2.6 fusion.115
  322.8 23.5 %fusion = f32[32,768]{1,0:T(8,128)} fusion(f32[200,768]{1,0:T(8,128)} %fusion.115), kind=kCustom, calls=%all-reduce-scatter | all-reduce-scatter fusion | flops 196609 | bytes 713216
  347.8 2.9 collective-permute-start
  350.7 1.9 collective-permute-start.1
  354.7 6.3 slice_bitcast_fusion
  362.6 2.6 copy.185
  365.2 3.5 fusion.32
  370.0 2.4 copy.188
  372.3 3.8 exponential_reduce_fusion.1
  380.3 3.5 copy.186
  383.9 3.5 copy.187
  387.4 3.5 copy.194
  390.9 3.5 copy.195
  394.5 4.7 concatenate.21
  399.2 2.5 scatter_custom_fusion
  401.7 2.6 multiply_reduce_fusion.6
  404.6 4.1 fusion.23
  408.8 5.2 multiply_reduce_fusion.7
  415.1 2.5 convolution_convert_fusion.1
  417.6 1.9 copy.189
  419.6 2.9 fusion.58
  422.9 2.2 multiply_reduce_fusion.2
  427.9 2.0 multiply_reduce_fusion.8
  430.2 4.1 fusion.20
  434.4 5.3 multiply_reduce_fusion.9
  442.1 1.9 copy.196
  444.1 2.7 fusion.55
  453.8 4.2 pad_maximum_fusion.3
  458.0 12.0 copy.204
  472.4 4.4 pad_maximum_fusion.2
  476.8 12.1 copy.201
  490.8 2.3 slice_bitcast_fusion.3
  493.0 1.8 copy.207
  494.9 2.5 convolution_bitcast_fusion.1
  498.9 6.7 pad_maximum_fusion.1
  505.6 1.8 copy.206
  507.5 2.5 convolution_bitcast_fusion.3
  511.4 6.9 pad_maximum_fusion
  520.1 3.3 multiply_reduce_fusion.10
  524.9 3.5 all-to-all-start.1
  530.9 35.5 %all-to-all-done.1 = f32[256,8,96]{0,2,1:T(8,128)S(1)} async-done(((f32[256,8,96]{0,2,1:T(8,128)}), f32[256,8,96]{0,2,1:T(8,128)S(1)}, u32[]{:S(2)}, u32[]{:S(2)}) %all-to-all-start.1) | async-done | bytes 786464 | tf_op jit(solution)/shard_map/all_to_all | solution.py:844
  566.7 12.3 scatter_custom_fusion.1
  580.7 490.0 %all-reduce.15.cloned.1.call-done = (f32[4,768,768]{2,0,1:T(4,128)}, f32[4,768,768]{2,0,1:T(4,128)}) async-done(((f32[4,768,768]{2,0,1:T(4,128)}, f32[4,768,768]{2,0,1:T(4,128)}), (f32[4,768,768]{2,0,1:T(4,128)}, f32[4,768,768]{2,0,1:T(4,128)})) %all-reduce.15.cloned.1.call-update) | async-done | bytes 18874384
  1075.5 311.5 %reduce-scatter.7.cloned.1.call-done = f32[2,384,768]{2,1,0:T(8,128)} async-done(((f32[2,3072,768]{2,1,0:T(8,128)}), f32[2,384,768]{2,1,0:T(8,128)}) %reduce-scatter.7.cloned.1.call-update) | async-done | bytes 2359312 | tf_op jit(solution)/shard_map/reduce_scatter | solution.py:448
  1387.0 316.3 %reduce-scatter.5.cloned.1.call-done = f32[2,384,768]{2,1,0:T(8,128)} async-done(((f32[2,3072,768]{2,1,0:T(8,128)}), f32[2,384,768]{2,1,0:T(8,128)}) %reduce-scatter.5.cloned.1.call-update) | async-done | bytes 2359312 | tf_op jit(solution)/shard_map/reduce_scatter | solution.py:448
  1703.3 4.9 pad_maximum_fusion.4
  1709.9 12.8 all-reduce.10
  1722.7 165.6 %all-reduce.17.cloned.1.call-done = (f32[2,4,96,768]{3,2,1,0:T(8,128)}, f32[2,2,384,768]{3,2,1,0:T(8,128)}, f32[3840,96]{0,1:T(8,128)}, f32[480,768]{1,0:T(8,128)}) async-done(((f32[2,4,96,768]{3,2,1,0:T(8,128)}, f32[2,2,384,768]{3,2,1,0:T(8,128)}, f32[3840,96]{0,1:T(8,128)}, f32[480,768]{1,0:T(8,128)}), (f32[2,4,96,768]{3,2,1,0:T(8,128)}, f32[2,2,384,768]{3,2,1,0:T(8,128)}, f32[3840,96]{0,1:T(8,128)}, ...) | async-done | bytes 10027024 | tf_op jit(solution)/shard_map/psum | solution.py:847
  1888.3 2.9 multiply_reduce_fusion.3
  1891.2 4.3 multiply_reduce_fusion
  1900.0 37.2 %all-reduce.7 = (f32[]{:T(128)}, f32[5,2,768]{2,1,0:T(2,128)S(1)}) all-reduce(f32[]{:T(128)S(6)} %add.302, f32[5,2,768]{2,1,0:T(2,128)S(1)} %get-tuple-element.206), channel_id=1, replica_groups=mesh['dp'=4,'mp'=8] {'mp'}, use_global_device_ids=true, to_apply=%region_49.50 | all-reduce | flops 7681 | bytes 61448 | tf_op jit(solution)/shard_map/psum | solution.py:857
  1939.2 7.4 multiply_subtract_fusion.1
  1946.7 10.7 multiply_subtract_fusion
  1957.8 2.8 multiply_subtract_fusion.3
  1962.1 2.9 multiply_subtract_fusion.2
  (378 shorter events, 119.6 us)
Async XLA Ops:
  17.3 10.0 copy-start.99
  17.3 14.4 copy-start.50
  17.3 15.0 copy-start.8
  20.0 27.4 %all-to-all-start = ((f32[8,256,96]{1,2,0:T(8,128)}), f32[8,256,96]{1,2,0:T(8,128)S(1)}, u32[]{:S(2)}, u32[]{:S(2)}) async-start(f32[8,256,96]{1,2,0:T(8,128)} %broadcast_select_fusion), calls=%async_computation | async-start | bytes 1572864 | tf_op jit(solution)/shard_map/all_to_all | solution.py:774
  27.2 1043.5 %all-reduce.15.cloned.1.call-start = ((), (), s32[]{:S(2)}) async-start(), calls=%async_computation.6 | async-start | bytes 37748736
  32.3 15.8 copy-start.56
  33.4 4.0 copy-start.100
  33.4 4.7 copy-start.89
  33.4 5.3 copy-start.84
  33.4 10.2 copy-start.64
  37.5 10.3 copy-start.98
  49.5 184.1 %copy-start.4 = (f32[480,768]{1,0:T(8,128)S(1)}, f32[480,768]{1,0:T(8,128)}, u32[]{:S(2)}) copy-start(f32[480,768]{1,0:T(8,128)} %param.36) | copy-start | bytes 4423684
  234.6 118.1 %copy-start = (f32[2,2,256,768]{3,2,1,0:T(8,128)S(1)}, f32[2,2,256,768]{3,2,1,0:T(8,128)}, u32[]{:S(2)}) copy-start(f32[2,2,256,768]{3,2,1,0:T(8,128)} %get-tuple-element.71) | copy-start | bytes 9437188
  347.8 46.7 %collective-permute-start = (f32[32,768]{1,0:T(8,128)}, f32[32,768]{1,0:T(8,128)}, u32[]{:S(2)}, u32[]{:S(2)}) collective-permute-start(f32[32,768]{1,0:T(8,128)} %fusion), channel_id=1, source_target_pairs={{0,1},{1,2},{2,3},{3,4},{4,5},{5,6},{6,7},{8,9},{9,10},{10,11},{11... | collective-permute-start | bytes 294920
  350.7 43.8 %collective-permute-start.1 = (f32[17,768]{1,0:T(8,128)}, f32[17,768]{1,0:T(8,128)}, u32[]{:S(2)}, u32[]{:S(2)}) collective-permute-start(f32[17,768]{1,0:T(8,128)} %slice.231), channel_id=1, source_target_pairs={{0,2},{1,3},{2,4},{3,5},{4,6},{5,7},{8,10},{9,11},{10,12},{11,13},... | collective-permute-start | bytes 156680
  354.7 6.3 copy-start.40
  372.3 3.9 copy-start.55
  372.3 5.5 copy-start.65
  376.1 3.0 copy-start.87
  376.2 3.0 copy-start.88
  376.2 3.6 copy-start.86
  401.7 2.9 copy-start.7
  404.6 4.2 copy-start.15
  404.6 4.2 copy-start.71
  404.6 4.2 copy-start.83
  408.7 5.2 copy-start.11
  419.6 3.0 copy-start.3
  419.6 3.3 copy-start.35
  419.6 3.4 copy-start.42
  419.6 5.6 copy-start.53
  419.6 5.6 copy-start.66
  419.6 7.8 slice-start.2
  422.9 4.5 slice-start.3
  430.2 4.2 copy-start.17
  430.2 4.2 copy-start.69
  430.2 4.2 copy-start.81
  434.4 5.4 copy-start.13
  440.9 3.2 copy-start.1
  488.9 898.1 %reduce-scatter.7.cloned.1.call-start = ((), (), s32[]{:S(2)}) async-start(), calls=%async_computation.5 | async-start | bytes 21233664 | tf_op jit(solution)/shard_map/reduce_scatter | solution.py:448
  505.6 1197.7 %reduce-scatter.5.cloned.1.call-start = ((), (), s32[]{:S(2)}) async-start(), calls=%async_computation.4 | async-start | bytes 21233664 | tf_op jit(solution)/shard_map/reduce_scatter | solution.py:448
  520.1 3.3 copy-start.79
  523.5 5.7 copy-start.39
  523.5 5.7 copy-start.61
  523.5 5.7 copy-start.68
  523.5 5.7 copy-start.77
  523.5 5.7 copy-start.85
  524.9 41.5 %all-to-all-start.1 = ((f32[256,8,96]{0,2,1:T(8,128)}), f32[256,8,96]{0,2,1:T(8,128)S(1)}, u32[]{:S(2)}, u32[]{:S(2)}) async-start(f32[256,8,96]{0,2,1:T(8,128)} %bitcast.93), calls=%async_computation.3 | async-start | bytes 1572864 | tf_op jit(solution)/shard_map/all_to_all | solution.py:844
  528.4 1359.9 %all-reduce.17.cloned.1.call-start = ((), (), s32[]{:S(2)}) async-start(), calls=%async_computation.7 | async-start | bytes 20054016 | tf_op jit(solution)/shard_map/psum | solution.py:847
  1891.2 4.3 copy-start.33
  1891.2 5.3 copy-start.31
  1891.2 55.5 %slice-start = ((s8[4718592]{0:T(1024)(128)(4,1)}), s8[524288]{0:T(1024)(128)(4,1)S(1)}, s32[]{:S(2)}) async-start(s8[4718592]{0:T(1024)(128)(4,1)} %bitcast.332), calls=%async_computation.8 | async-start | bytes 1048576
  1895.5 43.7 %copy-start.9 = (f32[2,4,96,768]{3,2,1,0:T(8,128)S(1)}, f32[2,4,96,768]{3,2,1,0:T(8,128)}, u32[]{:S(2)}) copy-start(f32[2,4,96,768]{3,2,1,0:T(8,128)} %param.27) | copy-start | bytes 7077892
  1939.2 7.4 slice-start.1
  1946.7 10.7 copy-start.30
  1946.7 10.7 copy-start.34
  1946.7 10.7 copy-start.43
  1946.7 11.1 copy-start.44
  1957.8 2.9 copy-start.5
  1957.8 2.9 copy-start.32
  1957.8 3.9 copy-start.45
  1957.8 4.3 copy-start.46
  1962.1 2.9 copy-start.51
  1962.1 2.9 copy-start.62
  1962.1 2.9 copy-start.63
  (50 other events, 82.2 us)
Sparse Core Ops, SparseCore 0:
  489.0 581.6 all-reduce.14
  1074.6 312.2 reduce-scatter.6
  1390.8 312.4 reduce-scatter.4
  1708.4 179.8 all-reduce.16

commit v2 on v1

--- a/solution.py
+++ b/solution.py
@@ -380,6 +380,495 @@
     )(visible, states, gains, masks, attn_b, ffn_b)
 
 
+def norm_back(grad, values, gain):
+    normed, inverse = normed_of(values)
+    scaled = grad * gain
+    centred = scaled - jnp.mean(scaled, axis=-1, keepdims=True)
+    result = inverse * (centred - normed * jnp.mean(scaled * normed, axis=-1, keepdims=True))
+    return (
+        result,
+        jnp.sum(grad * normed, axis=0, keepdims=True),
+        jnp.sum(grad, axis=0, keepdims=True),
+    )
+
+
+SLOTS = 3
+
+
+def backward_kernel(
+    n,
+    visible_ref,
+    grad_ref,
+    first_ref,
+    gains_ref,
+    inputs_ref,
+    proj_ref,
+    mixed_ref,
+    pre_ref,
+    mid_ref,
+    attn_full,
+    ffn_full,
+    slope_all,
+    act_all,
+    attn_sum,
+    ffn_sum,
+    grad_out,
+    pair_out,
+    wa,
+    wf,
+    slope,
+    act,
+    sum_a,
+    sum_f,
+    theirs_f,
+    land_f,
+    theirs_a,
+    land_a,
+    ring_a,
+    ring_f,
+    state,
+    grad_rows,
+    left_a,
+    left_f,
+    right_f,
+    spread_a,
+    spread_f,
+    done_a,
+    done_f,
+    wa_sem,
+    load_sem,
+    core_send,
+    core_recv,
+    core_free,
+    swap_send,
+    swap_recv,
+    swap_free,
+    ring_send,
+    ring_recv,
+    ring_free,
+    across_send,
+    across_recv,
+    out_sem,
+    last_send,
+    last_recv,
+):
+    spot = Spot(n)
+    core = spot.core
+    other = 1 - core
+    rows_a = attn_sum.shape[2]
+    rows_f = ffn_sum.shape[2]
+    part_f = rows_f // 2
+    order = (4, 3, -3, 2, -2, 1, -1, 0)
+    total = LAYERS * n
+
+    def rows_at(shard, rows):
+        return pl.ds(pl.multiple_of(shard * rows, 16), rows)
+
+    def remote(source, target, send, recv, device):
+        return pltpu.make_async_remote_copy(
+            src_ref=source,
+            dst_ref=target,
+            send_sem=send,
+            recv_sem=recv,
+            device_id=device,
+            device_id_type=MESH,
+        )
+
+    def turn_of(turn):
+        return LAYERS - 1 - turn // n, spot.shard(order[turn % n])
+
+    def loads(turn):
+        depth, shard = turn_of(turn)
+        slot = turn % SLOTS
+        return (
+            pltpu.make_async_copy(
+                ffn_full.at[depth, :, rows_at(shard, rows_f), :], wf.at[slot], load_sem.at[0, slot]
+            ),
+            pltpu.make_async_copy(slope_all.at[depth, shard], slope.at[slot], load_sem.at[1, slot]),
+            pltpu.make_async_copy(act_all.at[depth, shard], act.at[slot], load_sem.at[2, slot]),
+        )
+
+    def load_attn(depth):
+        return pltpu.make_async_copy(attn_full.at[depth], wa, wa_sem.at[0])
+
+    def core_copy(turn):
+        slot = turn % SLOTS
+        return remote(
+            theirs_f.at[slot],
+            land_f.at[slot],
+            core_send.at[turn],
+            core_recv.at[turn],
+            spot.partner,
+        )
+
+    def fold(turn):
+        depth, shard = turn_of(turn)
+        core_copy(turn).wait_recv()
+        sum_f[depth, shard] = (
+            sum_f[depth, shard].astype(jnp.float32)
+            + land_f[turn % SLOTS].astype(jnp.float32)
+        ).astype(jnp.bfloat16)
+        if turn + SLOTS < total:
+            pl.semaphore_signal(
+                core_free.at[0], inc=1, device_id=spot.partner, device_id_type=MESH
+            )
+
+    def swap_copy(depth, part):
+        return remote(
+            theirs_a.at[part],
+            land_a.at[part],
+            swap_send.at[depth, part],
+            swap_recv.at[depth, part],
+            spot.partner,
+        )
+
+    def summed(piece, shard, part):
+        kind, depth = piece % 2, piece // 2
+        if kind == 0:
+            return sum_a.at[depth, part, rows_at(shard, rows_a), :]
+        return sum_f.at[depth, shard, pl.ds(part * part_f, part_f), :]
+
+    def landed(piece, way, part, step):
+        return (ring_a if piece % 2 == 0 else ring_f).at[way, part, step - 1]
+
+    def ring_copy(piece, way, part, step):
+        offset = last_step(n, way, part) - step + 1
+        shard = spot.shard(offset if way == 0 else -offset)
+        return remote(
+            summed(piece, shard, part),
+            landed(piece, way, part, step),
+            ring_send.at[piece, way, part, step - 1],
+            ring_recv.at[piece, way, part, step - 1],
+            spot.ring[way],
+        )
+
+    def launch(piece, long):
+        for way, part in WAYS:
+            if (way == part) == long:
+                if piece // 2 < LAYERS - 1:
+                    pl.semaphore_wait(ring_free.at[piece % 2, way, part], 1)
+                ring_copy(piece, way, part, 1).start()
+
+    def relay(piece, step):
+        for way, part in WAYS:
+            last = last_step(n, way, part)
+            if step < last:
+                ring_copy(piece, way, part, step).wait_recv()
+                shard = spot.shard(last - step if way == 0 else step - last)
+                into = summed(piece, shard, part)
+                into[...] = (
+                    into[...].astype(jnp.float32)
+                    + landed(piece, way, part, step)[...].astype(jnp.float32)
+                ).astype(jnp.bfloat16)
+                ring_copy(piece, way, part, step + 1).start()
+
+    def across_copy(piece):
+        kind, depth = piece % 2, piece // 2
+        buffer = spread_a if kind == 0 else spread_f
+        return remote(
+            buffer.at[depth, 0],
+            buffer.at[depth, 1],
+            across_send.at[piece],
+            across_recv.at[piece],
+            spot.across,
+        )
+
+    def finish(piece):
+        kind, depth = piece % 2, piece // 2
+        for part in range(2):
+            value = summed(piece, spot.mp, part)[...].astype(jnp.float32)
+            for way in range(2):
+                step = last_step(n, way, part)
+                ring_copy(piece, way, part, step).wait_recv()
+                value = value + landed(piece, way, part, step)[...].astype(jnp.float32)
+            value = value.astype(jnp.bfloat16)
+            if kind == 0:
+                spread_a[depth, 0, part] = value
+            else:
+                spread_f[depth, 0, pl.ds(part * part_f, part_f), :] = value
+            if depth > 0:
+                for way in range(2):
+                    pl.semaphore_signal(
+                        ring_free.at[kind, way, part],
+                        inc=1,
+                        device_id=spot.ring[1 - way],
+                        device_id_type=MESH,
+                    )
+        across_copy(piece).start()
+
+    def out_copies(piece):
+        kind, depth = piece % 2, piece // 2
+        if kind == 0:
+            source, target = done_a, attn_sum.at[depth, pl.ds(2 * core, 2)]
+        else:
+            source, target = done_f, ffn_sum.at[depth, core]
+        return (
+            pltpu.make_async_copy(source, target, out_sem.at[piece]),
+            remote(source, target, last_send.at[piece], last_recv.at[piece], spot.partner),
+        )
+
+    def conclude(piece):
+        kind, depth = piece % 2, piece // 2
+        across_copy(piece).wait_recv()
+        if depth < LAYERS - 1:
+            local, away = out_copies(piece + 2)
+            local.wait()
+            away.wait_send()
+        if kind == 0:
+            done_a[...] = spread_a[depth, 0].astype(jnp.float32) + spread_a[depth, 1].astype(
+                jnp.float32
+            )
+        else:
+            done_f[...] = spread_f[depth, 0].astype(jnp.float32) + spread_f[depth, 1].astype(
+                jnp.float32
+            )
+        for copy in out_copies(piece):
+            copy.start()
+
+    load_attn(LAYERS - 1).start()
+    for turn in range(SLOTS):
+        for copy in loads(turn):
+            copy.start()
+    greet((spot.ring[0], spot.ring[1], spot.partner, spot.across))
+    state[...] = grad_ref[...]
+    lanes = lax.broadcasted_iota(jnp.int32, (1, 128), 1) < 64
+    visible = visible_ref[...] > 0.0
+
+    def ffn_turn(turn):
+        depth, shard = turn_of(turn)
+        slot = turn % SLOTS
+        for copy in loads(turn):
+            copy.wait()
+        grad_active = dot_nt(right_f[1], wf[slot, 1])
+        left_f[0] = (grad_active * slope[slot]).astype(jnp.bfloat16)
+        left_f[1] = act[slot]
+        sum_f[depth, shard] = dot_tn(left_f[core], right_f[core]).astype(jnp.bfloat16)
+        if turn >= SLOTS:
+            core_copy(turn - SLOTS).wait_send()
+        theirs_f[slot] = dot_tn(left_f[other], right_f[other]).astype(jnp.bfloat16)
+        if turn >= SLOTS:
+            pl.semaphore_wait(core_free.at[0], 1)
+        core_copy(turn).start()
+        state[...] += dot_nn(left_f[0], wf[slot, 0])
+        if turn + SLOTS < total:
+            for copy in loads(turn + SLOTS):
+                copy.start()
+
+    def head_pair(depth, pair):
+        columns = pl.ds(pl.multiple_of(pair * 128, 128), 128)
+        query = proj_ref[depth, 0, :, columns]
+        keyed = proj_ref[depth, 1, :, columns]
+        valued = proj_ref[depth, 2, :, columns]
+        grad_mixed = grad_rows[4, :, columns]
+        outs = []
+        for side in range(2):
+            mine = lanes if side == 0 else jnp.logical_not(lanes)
+            scores = dot_nt(jnp.where(mine, query, jnp.zeros_like(query)), keyed) * 0.125
+            scores = jnp.where(visible, scores, masked_score)
+            expo = jnp.exp(scores - jnp.max(scores, axis=-1, keepdims=True))
+            probs = expo / jnp.sum(expo, axis=-1, keepdims=True)
+            grad_probs = dot_nt(jnp.where(mine, grad_mixed, jnp.zeros_like(query)), valued)
+            inner = jnp.sum(grad_probs * probs, axis=-1, keepdims=True)
+            grad_scores = (probs * (grad_probs - inner)).astype(jnp.bfloat16)
+            outs.append(
+                (
+                    dot_nn(grad_scores, keyed) * 0.125,
+                    dot_tn(grad_scores, query) * 0.125,
+                    dot_tn(probs.astype(jnp.bfloat16), grad_mixed),
+                )
+            )
+        for which in range(3):
+            grad_rows[which, :, columns] = jnp.where(
+                lanes, outs[0][which], outs[1][which]
+            ).astype(jnp.bfloat16)
+
+    def layer(depth, hooks):
+        base = (LAYERS - 1 - depth) * n
+        piece_a, piece_f = 2 * depth, 2 * depth + 1
+        grad_two, pair_out[2 + 2 * depth, 0:1, :], pair_out[2 + 2 * depth, 1:2, :] = norm_back(
+            state[...], pre_ref[depth, 1], gains_ref[2 + 2 * depth, 0:1, :]
+        )
+        state[...] = grad_two
+        right_f[0] = mid_ref[depth]
+        right_f[1] = grad_two.astype(jnp.bfloat16)
+        for step in range(n):
+            ffn_turn(base + step)
+            if step >= 1:
+                fold(base + step - 1)
+            if step == 1:
+                launch(piece_f, True)
+            if step == 3:
+                launch(piece_f, False)
+            hooks.get(("ffn", step), lambda: None)()
+        fold(base + n - 1)
+        hooks.get("middle", lambda: None)()
+        grad_one, pair_out[1 + 2 * depth, 0:1, :], pair_out[1 + 2 * depth, 1:2, :] = norm_back(
+            state[...], pre_ref[depth, 0], gains_ref[1 + 2 * depth, 0:1, :]
+        )
+        state[...] = grad_one
+        grad_rows[3] = grad_one.astype(jnp.bfloat16)
+        load_attn(depth).wait()
+        grad_rows[4] = dot_nt(grad_rows[3], wa[3]).astype(jnp.bfloat16)
+
+        @pl.loop(0, HEADS // 2)
+        def _(pair):
+            head_pair(depth, pair)
+
+        hooks.get("heads", lambda: None)()
+        left_a[0] = inputs_ref[depth]
+        left_a[1] = mixed_ref[depth]
+        for part in range(2):
+            if depth < LAYERS - 1:
+                swap_copy(depth + 1, part).wait_send()
+            left = 0 if part == 0 else other
+            theirs_a[part] = dot_tn(left_a[left], grad_rows[2 * other + part]).astype(jnp.bfloat16)
+            if depth < LAYERS - 1:
+                pl.semaphore_wait(swap_free.at[part], 1)
+            swap_copy(depth, part).start()
+        for part in range(2):
+            left = 0 if part == 0 else core
+            sum_a[depth, part] = dot_tn(left_a[left], grad_rows[2 * core + part]).astype(
+                jnp.bfloat16
+            )
+        hooks.get("mats", lambda: None)()
+        for part in range(2):
+            swap_copy(depth, part).wait_recv()
+
+            @pl.loop(0, n)
+            def _(block):
+                rows = rows_at(block, rows_a)
+                sum_a[depth, part, rows, :] = (
+                    sum_a[depth, part, rows, :].astype(jnp.float32)
+                    + land_a[part, rows, :].astype(jnp.float32)
+                ).astype(jnp.bfloat16)
+
+            if depth > 0:
+                pl.semaphore_signal(
+                    swap_free.at[part], inc=1, device_id=spot.partner, device_id_type=MESH
+                )
+        launch(piece_a, True)
+        launch(piece_a, False)
+        for which in range(3):
+            state[...] += dot_nt(grad_rows[which], wa[which])
+        if depth > 0:
+            load_attn(depth - 1).start()
+
+    layer(
+        1,
+        {
+            "middle": lambda: relay(3, 1),
+            "heads": lambda: relay(3, 2),
+        },
+    )
+    relay(3, 3)
+    finish(3)
+    layer(
+        0,
+        {
+            ("ffn", 3): lambda: relay(2, 1),
+            ("ffn", 5): lambda: conclude(3),
+            "middle": lambda: relay(2, 2),
+            "heads": lambda: relay(1, 1),
+            "mats": lambda: (relay(2, 3), finish(2)),
+        },
+    )
+    grad_sum, pair_out[0, 0:1, :], pair_out[0, 1:2, :] = norm_back(
+        state[...], first_ref[...], gains_ref[0, 0:1, :]
+    )
+    grad_out[...] = grad_sum
+    relay(1, 2)
+    conclude(2)
+    relay(0, 1)
+    relay(1, 3)
+    relay(0, 2)
+    finish(1)
+    relay(0, 3)
+    conclude(1)
+    finish(0)
+    conclude(0)
+    for turn in range(total - SLOTS, total):
+        core_copy(turn).wait_send()
+    for part in range(2):
+        swap_copy(0, part).wait_send()
+    for piece in range(2 * LAYERS):
+        for way, part in WAYS:
+            for step in range(1, last_step(n, way, part) + 1):
+                ring_copy(piece, way, part, step).wait_send()
+        across_copy(piece).wait_send()
+        local, away = out_copies(piece)
+        if piece < 2:
+            local.wait()
+            away.wait_send()
+        away.wait_recv()
+
+
+def backward_call(n, visible, grad, first, gains, kept, attn_full, ffn_full, slope, act):
+    count, width = grad.shape
+    rows_f = ffn_full.shape[2] // n
+    rows_a = attn_full.shape[2] // n
+    f32, bf16 = jnp.float32, jnp.bfloat16
+    vmem = pl.BlockSpec(memory_space=pltpu.VMEM)
+    anywhere = pl.BlockSpec(memory_space=pl.ANY)
+    shape = jax.ShapeDtypeStruct
+    dma = pltpu.SemaphoreType.DMA
+    regular = pltpu.SemaphoreType.REGULAR
+    ring_sems = dma((2 * LAYERS, 2, 2, n // 2))
+    return pl.pallas_call(
+        functools.partial(backward_kernel, n),
+        out_shape=(
+            shape((LAYERS, 4, rows_a, width), f32),
+            shape((LAYERS, 2, rows_f, width), f32),
+            shape((count, width), f32),
+            shape(gains.shape, f32),
+        ),
+        in_specs=[vmem] * 9 + [anywhere] * 4,
+        out_specs=(anywhere, anywhere, vmem, vmem),
+        scratch_shapes=[
+            pltpu.VMEM((4, width, width), bf16),
+            pltpu.VMEM((SLOTS, 2, rows_f, width), bf16),
+            pltpu.VMEM((SLOTS, count, rows_f), f32),
+            pltpu.VMEM((SLOTS, count, rows_f), bf16),
+            pltpu.VMEM((LAYERS, 2, width, width), bf16),
+            pltpu.VMEM((LAYERS, n, rows_f, width), bf16),
+            pltpu.VMEM((SLOTS, rows_f, width), bf16),
+            pltpu.VMEM((SLOTS, rows_f, width), bf16),
+            pltpu.VMEM((2, width, width), bf16),
+            pltpu.VMEM((2, width, width), bf16),
+            pltpu.VMEM((2, 2, n // 2, rows_a, width), bf16),
+            pltpu.VMEM((2, 2, n // 2, rows_f // 2, width), bf16),
+            pltpu.VMEM((count, width), f32),
+            pltpu.VMEM((5, count, width), bf16),
+            pltpu.VMEM((2, count, width), bf16),
+            pltpu.VMEM((2, count, rows_f), bf16),
+            pltpu.VMEM((2, count, width), bf16),
+            pltpu.VMEM((LAYERS, 2, 2, rows_a, width), bf16),
+            pltpu.VMEM((LAYERS, 2, rows_f, width), bf16),
+            pltpu.VMEM((2, rows_a, width), f32),
+            pltpu.VMEM((rows_f, width), f32),
+            dma((1,)),
+            dma((3, SLOTS)),
+            dma((LAYERS * n,)),
+            dma((LAYERS * n,)),
+            regular((1,)),
+            dma((LAYERS, 2)),
+            dma((LAYERS, 2)),
+            regular((2,)),
+            ring_sems,
+            ring_sems,
+            regular((2, 2, 2)),
+            dma((2 * LAYERS,)),
+            dma((2 * LAYERS,)),
+            dma((2 * LAYERS,)),
+            dma((2 * LAYERS,)),
+            dma((2 * LAYERS,)),
+        ],
+        compiler_params=pltpu.CompilerParams(
+            collective_id=2, has_side_effects=True, vmem_limit_bytes=VMEM_LIMIT
+        ),
+        name="backward_layers",
+    )(visible, grad, first, gains, *kept, attn_full, ffn_full, slope, act)
+
+
 def merged(value, axis, join):
     pieces = jax.tree.map(lambda part: lax.all_gather(part, axis), value)
     head = jax.tree.map(lambda part: part[0], pieces)
@@ -541,55 +1030,6 @@
     peak = jnp.maximum(first[0], second[0])
     total = first[1] * jnp.exp(first[0] - peak) + second[1] * jnp.exp(second[0] - peak)
     return (peak, total, first[2] + second[2])
-
-
-def ffn_backward_kept(grad_out, middle_b, hidden, active, ffn_w, unit_mask):
-    grad_active = jnp.einsum("td,fd->tf", grad_out, ffn_w[1], preferred_element_type=jnp.float32)
-    grad_hidden = (hidden * grad_active).astype(jnp.bfloat16)
-    up_grad = jnp.einsum("tf,td->fd", grad_hidden, middle_b, preferred_element_type=jnp.float32)
-    down_grad = jnp.einsum("tf,td->fd", active, grad_out, preferred_element_type=jnp.float32)
-    from_ffn = jnp.einsum("tf,fd->td", grad_hidden, ffn_w[0], preferred_element_type=jnp.float32)
-    return (jnp.stack([up_grad, down_grad]), from_ffn)
-
-
-def layer_backward_kept(grad, attn_w, ffn_w, pair, length, unit_mask, kept):
-    inputs, heads, log_total, mixed, norm_one, middle_b, hidden, active, norm_two = kept
-    count = inputs.shape[0]
-    grad_two, pair_two = norm_backward(grad, norm_two, pair[1, 0])
-    ffn_grad, from_ffn = ffn_backward_kept(
-        grad_two.astype(jnp.bfloat16), middle_b, hidden, active, ffn_w, unit_mask
-    )
-    grad_one, pair_one = norm_backward(grad_two + from_ffn, norm_one, pair[0, 0])
-    grad_branch = grad_one.astype(jnp.bfloat16)
-    output_grad = jnp.einsum("td,te->de", mixed, grad_branch, preferred_element_type=jnp.float32)
-    grad_mixed = jnp.einsum("te,de->td", grad_branch, attn_w[3], preferred_element_type=jnp.float32)
-    grad_mixed = grad_mixed.astype(jnp.bfloat16).reshape(count, HEADS, -1).transpose(1, 0, 2)
-    scale = heads.shape[-1] ** (-0.5)
-    probs = jnp.exp(masked_scores(heads[0], heads[1], length) - log_total)
-    grad_values = jnp.einsum(
-        "hqk,hqe->hke", probs.astype(jnp.bfloat16), grad_mixed, preferred_element_type=jnp.float32
-    )
-    grad_probs = jnp.einsum(
-        "hqe,hke->hqk", grad_mixed, heads[2], preferred_element_type=jnp.float32
-    )
-    grad_scores = probs * (grad_probs - jnp.sum(grad_probs * probs, axis=-1, keepdims=True))
-    grad_scores = grad_scores.astype(jnp.bfloat16)
-    grad_query = (
-        jnp.einsum("hqk,hke->hqe", grad_scores, heads[1], preferred_element_type=jnp.float32)
-        * scale
-    )
-    grad_key = (
-        jnp.einsum("hqk,hqe->hke", grad_scores, heads[0], preferred_element_type=jnp.float32)
-        * scale
-    )
-    stacked = (
-        jnp.stack([grad_query, grad_key, grad_values]).transpose(0, 2, 1, 3).reshape(3, count, -1)
-    )
-    stacked = stacked.astype(jnp.bfloat16)
-    input_grad = jnp.einsum("td,kte->kde", inputs, stacked, preferred_element_type=jnp.float32)
-    from_attn = jnp.einsum("kte,kde->td", stacked, attn_w[:3], preferred_element_type=jnp.float32)
-    attn_grad = jnp.concatenate([input_grad, output_grad[None]], axis=0)
-    return (grad_one + from_attn, attn_grad, ffn_grad, jnp.stack([pair_one, pair_two]))
 
 
 def local_general(
@@ -769,28 +1209,15 @@
     all_lengths = lengths.reshape(-1)
     length = lax.dynamic_index_in_dim(all_lengths, rank, keepdims=False)
     masks = jnp.minimum(ramp, RAMP).astype(jnp.float32) / RAMP
-    unit_masks = [masks[depth] for depth in range(LAYERS)]
     looked = jnp.take(table, flat_ids, axis=0)
     embedded = lax.all_to_all(looked, "mp", split_axis=0, concat_axis=1, tiled=True)
-    states, norm_zero = layer_norm(
-        embedded + sinusoid(count, embedded.shape[1]), gains[0, 0], gains[0, 1]
-    )
+    first = embedded + sinusoid(count, embedded.shape[1])
+    states, _ = layer_norm(first, gains[0, 0], gains[0, 1])
     n = attn.shape[3] // attn.shape[2]
     visible = (jnp.arange(count) < length).astype(jnp.float32)[None, :]
-    (
-        attn_full, ffn_full, states, inputs_all, proj_all, mixed_all, pre_all, mid_all, slope_all, act_all,
-    ) = forward_call(
+    attn_full, ffn_full, states, *kept, slope, act = forward_call(
         n, visible, states, gains, masks, attn.astype(jnp.bfloat16), ffn.astype(jnp.bfloat16)
     )
-    kept_all = []
-    for depth in range(LAYERS):
-        heads = proj_all[depth].reshape(3, count, HEADS, -1).transpose(0, 2, 1, 3)
-        scores = masked_scores(heads[0], heads[1], length)
-        log_total = jax.nn.logsumexp(scores, axis=-1, keepdims=True)
-        slope = slope_all[depth].transpose(1, 0, 2).reshape(count, -1)
-        act = act_all[depth].transpose(1, 0, 2).reshape(count, -1)
-        kept_all.append((inputs_all[depth], heads, log_total, mixed_all[depth], normed_of(pre_all[depth, 0]),
-           mid_all[depth], slope, act, normed_of(pre_all[depth, 1])))
     spots = places.reshape(-1)
     picked = jnp.take(states, spots, axis=0).astype(jnp.bfloat16)
     picked_all = lax.all_gather(picked, "mp", axis=0, tiled=True)
@@ -824,28 +1251,13 @@
         tiled=True,
     )
     grad = jnp.zeros_like(states).at[spots].add(picked_grad)
-    attn_parts = [None] * LAYERS
-    ffn_parts = [None] * LAYERS
-    pair_grads = [None] * LAYERS
-    for depth in reversed(range(LAYERS)):
-        attn_w, ffn_w = attn_full[depth], ffn_full[depth]
-        grad, attn_grad, ffn_grad, pair_grad = layer_backward_kept(
-            grad,
-            attn_w,
-            ffn_w,
-            gains[1 + 2 * depth : 3 + 2 * depth],
-            length,
-            unit_masks[depth],
-            kept_all[depth],
-        )
-        attn_parts[depth], ffn_parts[depth] = reduce_layer(attn_grad, ffn_grad)
-        pair_grads[depth] = pair_grad
-    grad_sum, zero_grad = norm_backward(grad, norm_zero, gains[0, 0])
+    attn_sum, ffn_sum, grad_sum, gains_grad = backward_call(
+        n, visible, grad, first, gains, kept, attn_full, ffn_full, slope, act
+    )
     returned = lax.all_to_all(grad_sum, "mp", split_axis=1, concat_axis=0, tiled=True)
     table_grad = jnp.zeros_like(table).at[flat_ids].add(returned)
-    gains_grad = jnp.concatenate([zero_grad[None]] + pair_grads, axis=0)
-    attn_sum, ffn_sum, table_sum, out_sum, gains_part, loss = lax.psum(
-        (jnp.stack(attn_parts), jnp.stack(ffn_parts), table_grad, out_grad, gains_grad, loss_pair),
+    table_sum, out_sum, gains_part, loss = lax.psum(
+        (table_grad, out_grad, gains_grad, loss_pair),
         "dp",
     )
     shard_squares = (
@@ -935,7 +1347,6 @@
         P(),
         P(),
     )
-    rows_attn, rows_ffn = 768 // mesh.shape['mp'], 3072 // mesh.shape['mp']
-    fits = mesh.shape['mp'] == 8
+    fits = mesh.shape['mp'] == 8 and mesh.shape['dp'] == 4
     chosen = local if fits else local_general
     return jax.shard_map(chosen, mesh=mesh, in_specs=in_specs, out_specs=out_specs, check_vma=False)

time: 1980 us -> 661 us (0.33)
  waiting for transfers between devices: 1320 us -> 67.8 us
  Pallas kernels: 150 us -> 323 us
  local copies, waits for them, and re-layouts: 132 us -> 19.4 us
  matrix products: 62.5 us -> 2.57 us
  other arithmetic: 127 us -> 67.2 us
    reduce_scatter x2 -> x0, waiting for transfers between devices: 628 us -> none  [reduce_layer(): lax.psum_scatter(ffn_grad, 'mp', scatter_dimension=1, tiled=True)]
    unnamed x7 -> x3, waiting for transfers between devices: 490 us -> 1.33 us
    pallas_call x0 -> x1, Pallas kernels: none -> 173 us  [backward_call(): pl.pallas_call(functools.partial(backward_kernel, n), out_shape=(shape((L...]
    psum x1, waiting for transfers between devices: 166 us -> 42.3 us  [local(): lax.psum((table_grad, out_grad, gains_grad, loss_pair), 'dp')]
    dot_general x26 -> x0, matrix products: 57.1 us -> none  [the longest x2 10.5 us: ffn_backward_kept(): jnp.einsum('tf,fd->td', grad_hidden, ffn_w[0], preferred_element_type=jnp...]
    unnamed x226 -> x52, local copies, waits for them, and re-layouts: 31.4 us -> 4.2 us
    concatenate x2 -> x0, local copies, waits for them, and re-layouts: 24.1 us -> none  [layer_backward_kept(): attn_grad = jnp.concatenate([input_grad, output_grad[None]], axis=0)]
    another operation x4 -> x0, other arithmetic: 20.1 us -> none  [the longest x2 13.6 us: ffn_backward_kept(): return (jnp.stack([up_grad, down_grad]), from_ffn)]
  transfers between devices with their start and end apart: 8 -> 5, of which waited for: 6 -> 4; matrix products, arithmetic and copies ran while one was open for 6% -> 4% of each run, Pallas kernels for 0% -> 0%
where the time goes in v2:
time: 661 us; the launch traced here: 655 us
  Pallas kernels  323 us (49%)
  blocking collectives  139 us (21%)
  waiting for transfers between devices  67.8 us (10%)
  other arithmetic  67.2 us (10%)
  between operations  21.7 us (3%)
  local copies, waits for them, and re-layouts  19.4 us (3%)
  starting transfers between devices  14.4 us (2%)
    pallas_call x1, Pallas kernels, backward_call(): pl.pallas_call(functools.partial(backward_kernel, n), out_shape=(shape((L...  173 us
    pallas_call x1, Pallas kernels, forward_call(): pl.pallas_call(functools.partial(forward_kernel, n), out_shape=(shape((LA...  150 us
    unnamed x2, blocking collectives  57.3 us
    psum x1, waiting for transfers between devices, local(): lax.psum((table_grad, out_grad, gains_grad, loss_pair), 'dp')  42.3 us
    psum x1, blocking collectives, local(): square_total, gains_sum = lax.psum((shard_squares, gains_part), 'mp')  37.2 us
    all_gather x1, blocking collectives, local(): picked_all = lax.all_gather(picked, 'mp', axis=0, tiled=True)  31.7 us
    sub x5, other arithmetic, adamw(): weight - rate * (fixed_one / (jnp.sqrt(fixed_two) + adam_eps) + decay * w...  25.2 us
    all_to_all x1, waiting for transfers between devices, local(): lax.all_to_all(grad_sum, 'mp', split_axis=1, concat_axis=0, tiled=True)  19.2 us
  transfers between devices with their start and end apart: 5, of which 4 were waited for; matrix products, arithmetic and copies ran while one was open for 4% of the time, Pallas kernels for 0%

profile of v2, /device:TPU:0, one launch (start us, length us, event | category | flops | bytes accessed | tf_op | source)
XLA Modules:
  0.0 654.5 jit_solution(15061829885281249072)
XLA Ops:
  7.2 1.8 copy.78
  9.1 5.5 gather_fusion
  14.6 0.3 copy.79
  14.9 1.0 broadcast_select_fusion
  15.9 7.3 %all-to-all-start = ((f32[8,256,96]{1,2,0:T(8,128)}), f32[8,256,96]{1,2,0:T(8,128)S(1)}, u32[]{:S(2)}, u32[]{:S(2)}) async-start(f32[8,256,96]{1,2,0:T(8,128)} %broadcast_select_fusion), calls=%async_computation | async-start | bytes 1572864 | tf_op jit(solution)/shard_map/all_to_all | solution.py:1213
  23.2 0.6 fusion.35
  23.9 0.1 lt.84
  24.0 0.6 constant_dynamic-slice_fusion.3
  24.6 1.2 compare_convert_fusion.1.visible_ref
  25.8 0.8 slice_reduce_fusion.1
  26.6 2.8 convert_element_type.36.attn_sh
  29.4 4.0 convert_element_type.37.ffn_sh
  33.5 0.6 fusion.37
  34.8 1.4 fusion.14
  36.2 1.4 fusion.16
  37.7 0.6 convert_multiply_fusion.mask_ref
  38.3 5.0 all-to-all-done
  43.3 0.2 fusion.21
  43.5 0.2 multiply_reduce_fusion.4
  43.7 0.3 copy.80
  44.0 1.3 multiply_add_fusion.5
  45.3 150.1 %forward_layers.1 = (bf16[2,4,768,768]{3,2,1,0:T(8,128)(2,1)}, bf16[2,2,3072,768]{3,2,1,0:T(8,128)(2,1)}, f32[256,768]{1,0:T(8,128)}, bf16[2,256,768]{2,1,0:T(8,...) custom-call(f32[1,256]{1,0:T(1,128)} %compare_convert_fusion.1.visib, ...), custom_call_target="tpu_custom_call" | custom-call | tf_op jit(solution)/shard_map/forward_layers/pallas_call | solution.py:349
  195.4 1.8 gather_fusion.1
  197.2 31.7 %all-gather.3 = bf16[8,25,768]{2,1,0:T(8,128)(2,1)S(1)} all-gather(bf16[1,25,768]{2,1,0:T(8,128)(2,1)S(1)} %fusion.23), channel_id=1, replica_groups=mesh['dp'=4,'mp'=8] {'mp'}, dimensions={0}, use_global_device_ids=true | all-gather | bytes 345600 | tf_op jit(solution)/shard_map/all_gather | solution.py:1223
  229.0 0.1 reshape.285
  229.1 0.5 fusion.38
  229.6 0.3 dynamic-update-slice
  229.8 0.3 fusion.7
  230.1 0.3 dynamic-update-slice.1
  230.4 0.3 dynamic-update-slice.2
  230.7 34.9 %all-reduce.6 = (f32[1600]{0:T(1024)S(1)}, f32[1600]{0:T(1024)S(1)}, f32[1600]{0:T(1024)S(1)}) all-reduce(f32[1600]{0:T(1024)S(1)} %dynamic-update-slice, f32[1600]{0:T(1024)S(1)} %dynamic-update-slice.1, f32[1600]{0:T(1024)S(1)} %dynamic-update-slice.2), channel_id=2, replica_groups=mesh['dp'=4,'mp'=8] {'mp'}, use_global_device_ids=true, to_apply=%add | all-reduce | flops 4800 | bytes 38400
  265.8 0.1 reshape.272
  266.1 0.6 while.14
  266.7 0.6 select_reduce_fusion
  267.3 0.4 fusion.17
  267.7 22.3 %fusion = f32[32,768]{1,0:T(8,128)S(1)} fusion(f32[200,768]{1,0:T(8,128)S(1)} %fusion.17), kind=kCustom, calls=%all-reduce-scatter | all-reduce-scatter fusion | flops 196609 | bytes 713216
  290.1 2.2 collective-permute-start
  292.3 1.3 collective-permute-start.1
  294.3 1.3 collective-permute-done.1
  295.6 0.3 concatenate.9
  295.9 1.6 scatter_custom_fusion.grad_ref
  297.6 172.6 %backward_layers.1 = (f32[2,4,96,768]{3,2,1,0:T(8,128)}, f32[2,2,384,768]{3,2,1,0:T(8,128)}, f32[256,768]{1,0:T(8,128)}, f32[5,2,768]{2,1,0:T(2,128)}) custom-call(f32[1,256]{1,0:T(1,128)} %compare_convert_fusion.1.visible_ref, f32[256,768]{1,0:T(8,128)} %scatter_custom_fusion.grad_ref, f32[256,768]{1,0:T(8,128)} %get-tuple-element.185.first_ref, ...), custom_call_target="tpu_custom_call" | custom-call | tf_op jit(solution)/shard_map/backward_layers/pallas_call | solution.py:816
  470.1 2.3 copy.81
  472.4 3.5 all-to-all-start.1
  476.0 1.7 fusion.27
  477.7 19.2 %all-to-all-done.1 = f32[256,8,96]{0,2,1:T(8,128)S(1)} async-done(((f32[256,8,96]{0,2,1:T(8,128)}), f32[256,8,96]{0,2,1:T(8,128)S(1)}, u32[]{:S(2)}, u32[]{:S(2)}) %all-to-all-start.1) | async-done | bytes 786464 | tf_op jit(solution)/shard_map/all_to_all | solution.py:1257
  496.9 1.3 copy.85
  498.2 12.3 %scatter_custom_fusion.1 = f32[3840,96]{1,0:T(8,128)S(1)} fusion(s32[2048]{0:T(1024)S(1)} %bitcast.69, f32[2048,96]{1,0:T(8,128)} %bitcast.63, f32[]{:T(128)} %constant.58.clone.1), kind=kCustom, calls=%fused_computation.28 | custom fusion | flops 196608 | bytes 1475072 | tf_op jit(solution)/shard_map/scatter-add | solution.py:1258
  510.5 1.7 copy.84
  512.8 0.7 pad_maximum_fusion
  513.6 12.6 %all-reduce.7 = (f32[2]{0:T(128)}, f32[5,2,768]{2,1,0:T(2,128)S(1)}) all-reduce(f32[2]{0:T(128)S(1)} %pad_maximum_fusion, f32[5,2,768]{2,1,0:T(2,128)S(1)} %copy-done.12), channel_id=1, replica_groups=mesh['dp'=4,'mp'=8] {'dp'}, use_global_device_ids=true, to_apply=%region_9.10 | all-reduce | flops 7682 | bytes 61456 | tf_op jit(solution)/shard_map/psum | solution.py:1259
  526.1 2.9 multiply_reduce_fusion.1
  529.0 4.2 multiply_reduce_fusion
  534.5 42.3 %all-reduce.11.cloned.1.call-done = (f32[3840,96]{0,1:T(8,128)}, f32[480,768]{1,0:T(8,128)}) async-done(((f32[3840,96]{0,1:T(8,128)}, f32[480,768]{1,0:T(8,128)}), (f32[3840,96]{0,1:T(8,128)}, f32[480,768]{1,0:T(8,128)})) %all-reduce.11.cloned.1.call-update) | async-done | bytes 2949136 | tf_op jit(solution)/shard_map/psum | solution.py:1259
  576.8 2.5 multiply_reduce_fusion.3
  579.3 1.0 multiply_reduce_fusion.2
  581.5 37.2 %all-reduce.5 = (f32[]{:T(128)}, f32[5,2,768]{2,1,0:T(2,128)S(1)}) all-reduce(f32[]{:T(128)S(6)} %add.222, f32[5,2,768]{2,1,0:T(2,128)S(1)} %get-tuple-element.162), channel_id=1, replica_groups=mesh['dp'=4,'mp'=8] {'mp'}, use_global_device_ids=true, to_apply=%region_19.20 | all-reduce | flops 7681 | bytes 61448 | tf_op jit(solution)/shard_map/psum | solution.py:1269
  618.7 0.6 multiply_reduce_fusion.5
  620.7 8.1 %multiply_subtract_fusion.1 = (f32[2,4,96,768]{3,2,1,0:T(8,128)}, f32[2,4,96,768]{3,2,1,0:T(8,128)}, f32[2,4,96,768]{3,2,1,0:T(8,128)}) fusion(f32[2,4,96,768]{3,2,1,0:T(8,128)} %param.27, f32[2,4,96,768]{3,2,1,0:T(8,128)} %get-tuple-element.83, f32[]{:T(128)S(6)} %div.110, f32[2,4,96,768]{3,2,1,0:T(8,128)} %param.29, f32[2,4,96,768]{3,2,1,0:T(8,128)} %param.28), kind=kLoop, calls=%fused_computation.15 | loop fusion | flops 9437184 | bytes 16515076 | tf_op jit(solution)/shard_map/sub | solution.py:1025
  628.9 10.7 %multiply_subtract_fusion = (f32[2,2,384,768]{3,2,1,0:T(8,128)}, f32[2,2,384,768]{3,2,1,0:T(8,128)}, f32[2,2,384,768]{3,2,1,0:T(8,128)}) fusion(f32[2,2,384,768]{3,2,1,0:T(8,128)S(1)} %bitcast.59, f32[2,2,384,768]{3,2,1,0:T(8,128)} %get-tuple-element.84, f32[]{:T(128)S(6)} %div.110, f32[2,2,384,768]{3,2,1,0:T(8,128)} %param.32, f32[2,2,384,768]{3,2,1,0:T(8,128)} %param.31), kind=kLoop, calls=%fused_computation.10 | loop fusion | flops 18874368 | bytes 33030148 | tf_op jit(solution)/shard_map/sub | solution.py:1025
  639.6 0.4 copy-done.5
  640.0 2.8 multiply_subtract_fusion.3
  642.8 2.8 multiply_subtract_fusion.2
  645.7 0.7 multiply_subtract_fusion.4
  (98 shorter events, 1.2 us)
Async XLA Ops:
  7.2 1.8 copy-start.9
  14.9 8.3 %copy-start.16 = (s32[1,8]{1,0:T(1,128)S(1)}, s32[1,8]{1,0:T(1,128)}, u32[]{:S(2)}) copy-start(s32[1,8]{1,0:T(1,128)} %param.23) | copy-start | bytes 100
  15.9 27.4 %all-to-all-start = ((f32[8,256,96]{1,2,0:T(8,128)}), f32[8,256,96]{1,2,0:T(8,128)S(1)}, u32[]{:S(2)}, u32[]{:S(2)}) async-start(f32[8,256,96]{1,2,0:T(8,128)} %broadcast_select_fusion), calls=%async_computation | async-start | bytes 1572864 | tf_op jit(solution)/shard_map/all_to_all | solution.py:1213
  29.4 4.0 copy-start.17
  29.4 4.1 copy-start.14
  29.4 4.2 copy-start.15
  29.4 8.3 %copy-start.13 = (s32[2,3072]{1,0:T(2,128)S(1)}, s32[2,3072]{1,0:T(2,128)}, u32[]{:S(2)}) copy-start(s32[2,3072]{1,0:T(2,128)} %param.26) | copy-start | bytes 73732
  45.3 183.8 %copy-start = (f32[480,768]{1,0:T(8,128)S(1)}, f32[480,768]{1,0:T(8,128)}, u32[]{:S(2)}) copy-start(f32[480,768]{1,0:T(8,128)} %param.36) | copy-start | bytes 4423684
  290.1 5.5 collective-permute-start
  292.3 3.3 collective-permute-start.1
  472.4 24.4 %all-to-all-start.1 = ((f32[256,8,96]{0,2,1:T(8,128)}), f32[256,8,96]{0,2,1:T(8,128)S(1)}, u32[]{:S(2)}, u32[]{:S(2)}) async-start(f32[256,8,96]{0,2,1:T(8,128)} %bitcast.17), calls=%async_computation.1 | async-start | bytes 1572864 | tf_op jit(solution)/shard_map/all_to_all | solution.py:1257
  476.0 100.8 %all-reduce.11.cloned.1.call-start = ((), (), s32[]{:S(2)}) async-start(), calls=%async_computation.2 | async-start | bytes 5898240 | tf_op jit(solution)/shard_map/psum | solution.py:1259
  512.2 1.4 copy-start.12
  576.8 2.5 copy-start.2
  579.3 49.6 %slice-start = ((s8[4718592]{0:T(1024)(128)(4,1)}), s8[524288]{0:T(1024)(128)(4,1)S(1)}, s32[]{:S(2)}) async-start(s8[4718592]{0:T(1024)(128)(4,1)} %bitcast.58), calls=%async_computation.3 | async-start | bytes 1048576
  620.7 8.1 %slice-start.1 = ((s8[4718592]{0:T(1024)(128)(4,1)}), s8[4194304]{0:T(1024)(128)(4,1)S(1)}, s32[]{:S(2)}) async-start(s8[4718592]{0:T(1024)(128)(4,1)} %bitcast.58), calls=%async_computation.4 | async-start | bytes 8388608
  628.8 10.7 %copy-start.1 = (f32[3840,96]{0,1:T(8,128)S(1)}, f32[3840,96]{0,1:T(8,128)}, u32[]{:S(2)}) copy-start(f32[3840,96]{0,1:T(8,128)} %param.33) | copy-start | bytes 4423684
  628.8 10.7 %copy-start.3 = (f32[3840,96]{0,1:T(8,128)S(1)}, f32[3840,96]{0,1:T(8,128)}, u32[]{:S(2)}) copy-start(f32[3840,96]{0,1:T(8,128)} %get-tuple-element.163) | copy-start | bytes 4423684
  628.8 10.7 %copy-start.4 = (f32[3840,96]{0,1:T(8,128)S(1)}, f32[3840,96]{0,1:T(8,128)}, u32[]{:S(2)}) copy-start(f32[3840,96]{0,1:T(8,128)} %param.35) | copy-start | bytes 4423684
  628.9 11.1 %copy-start.5 = (f32[3840,96]{0,1:T(8,128)S(1)}, f32[3840,96]{0,1:T(8,128)}, u32[]{:S(2)}) copy-start(f32[3840,96]{0,1:T(8,128)} %param.34) | copy-start | bytes 4423684
  640.0 2.8 copy-start.6
  640.0 2.8 copy-start.7
  642.8 2.9 copy-start.8
  642.8 2.9 copy-start.10
  642.8 2.8 copy-start.11
Sparse Core Ops, SparseCore 0:
  512.3 64.4 all-reduce.10

commit v3 on v2

--- a/solution.py
+++ b/solution.py
@@ -27,6 +27,7 @@
 
 MESH = pl.DeviceIdType.MESH
 VMEM_LIMIT = 60 * 1024 * 1024
+SLOTS = 3
 
 
 def dot_nn(left, right):
@@ -99,15 +100,21 @@
 
 def forward_kernel(
     n,
+    ids_ref,
+    table_ref,
+    where_ref,
     visible_ref,
-    states_ref,
     gains_ref,
     mask_ref,
+    places_ref,
+    labels_ref,
+    valid_ref,
+    out_ref,
     attn_sh,
     ffn_sh,
     attn_full,
     ffn_full,
-    final_ref,
+    first_ref,
     inputs_ref,
     proj_ref,
     mixed_ref,
@@ -115,137 +122,183 @@
     mid_ref,
     slope_ref,
     act_ref,
+    grad_ref,
+    out_grad_ref,
+    loss_ref,
     wa,
     wf,
+    raw_a,
+    raw_f,
+    slope,
+    act,
     state,
-    own_sem,
+    row_out,
+    row_in,
+    picked,
+    stats,
+    back_out,
+    back_in,
+    raw_sem,
     out_sem,
+    kept_sem,
     ring_send,
     ring_recv,
     core_send,
     core_recv,
+    fan_send,
+    fan_recv,
 ):
     spot = Spot(n)
     core = spot.core
     rows_a = attn_sh.shape[2]
     rows_f = ffn_sh.shape[2]
     part_f = rows_f // 2
-    width = attn_sh.shape[3]
     steps = n // 2
+    count = first_ref.shape[0]
+    columns_own = table_ref.shape[1]
+    slots = places_ref.shape[0]
 
     def rows_at(shard, rows):
         return pl.ds(pl.multiple_of(shard * rows, 16), rows)
 
-    def chunk(piece, shard, part):
+    def remote(source, target, send, recv, device):
+        return pltpu.make_async_remote_copy(
+            src_ref=source,
+            dst_ref=target,
+            send_sem=send,
+            recv_sem=recv,
+            device_id=device,
+            device_id_type=MESH,
+        )
+
+    def chunk(piece, shard, part, side):
         kind, depth = piece % 2, piece // 2
         if kind == 0:
-            return wa.at[depth, 2 * core + part, rows_at(shard, rows_a), :]
+            return wa.at[depth, 2 * side + part, rows_at(shard, rows_a), :]
         start = pl.multiple_of(shard * rows_f + part * part_f, 16)
-        return wf.at[depth, core, pl.ds(start, part_f), :]
-
-    def chunk_other(piece, shard, part):
+        return wf.at[depth, side, pl.ds(start, part_f), :]
+
+    def sign(way):
+        return -1 if way == 0 else 1
+
+    def ring_copy(piece, way, part, step, arriving):
+        target = chunk(piece, spot.shard(sign(way) * (step - 1 + arriving)), part, core)
+        return remote(
+            target,
+            target,
+            ring_send.at[piece, way, part, step - 1],
+            ring_recv.at[piece, way, part, step - 1],
+            spot.ring[way],
+        )
+
+    def core_copy(piece, way, part, step, side):
+        target = chunk(piece, spot.shard(sign(way) * step), part, side)
+        return remote(
+            target,
+            target,
+            core_send.at[piece, way, part, step - 1],
+            core_recv.at[piece, way, part, step - 1],
+            spot.partner,
+        )
+
+    def peer(offset):
+        return (spot.mp + offset + n) % n
+
+    def fan_copy(which, offset, source, target):
+        return remote(
+            source,
+            target,
+            fan_send.at[which, offset - 1],
+            fan_recv.at[which, offset - 1],
+            (spot.dp, peer(offset)),
+        )
+
+    def share(which, buffer, offset):
+        return fan_copy(which, offset, buffer.at[spot.mp], buffer.at[spot.mp])
+
+    def arrived(which, buffer, offset):
+        return fan_copy(which, offset, buffer.at[peer(-offset)], buffer.at[peer(-offset)])
+
+    def deal(which, source, target, offset):
+        return fan_copy(which, offset, source.at[peer(offset)], target.at[spot.mp])
+
+    def raw_copy(piece):
         kind, depth = piece % 2, piece // 2
         if kind == 0:
-            return wa.at[depth, 2 * (1 - core) + part, rows_at(shard, rows_a), :]
-        start = pl.multiple_of(shard * rows_f + part * part_f, 16)
-        return wf.at[depth, 1 - core, pl.ds(start, part_f), :]
-
-    def chunk_own(piece, part):
+            return pltpu.make_async_copy(attn_sh.at[depth], raw_a.at[depth], raw_sem.at[piece])
+        return pltpu.make_async_copy(ffn_sh.at[depth], raw_f.at[depth], raw_sem.at[piece])
+
+    def take_own(piece):
         kind, depth = piece % 2, piece // 2
+        raw_copy(piece).wait()
         if kind == 0:
-            return attn_sh.at[depth, 2 * core + part]
-        return ffn_sh.at[depth, core, pl.ds(part * part_f, part_f), :]
-
-    def sign(way):
-        return -1 if way == 0 else 1
-
-    def ring_out(piece, way, part, step):
-        target = chunk(piece, spot.shard(sign(way) * (step - 1)), part)
-        return pltpu.make_async_remote_copy(
-            src_ref=chunk_own(piece, part) if step == 1 else target,
-            dst_ref=target,
-            send_sem=ring_send.at[piece, way, part, step - 1],
-            recv_sem=ring_recv.at[piece, way, part, step - 1],
-            device_id=spot.ring[way],
-            device_id_type=MESH,
-        )
-
-    def ring_in(piece, way, part, step):
-        target = chunk(piece, spot.shard(sign(way) * step), part)
-        return pltpu.make_async_remote_copy(
-            src_ref=target,
-            dst_ref=target,
-            send_sem=ring_send.at[piece, way, part, step - 1],
-            recv_sem=ring_recv.at[piece, way, part, step - 1],
-            device_id=spot.ring[way],
-            device_id_type=MESH,
-        )
-
-    def core_out(piece, way, part, step):
-        target = chunk(piece, spot.shard(sign(way) * step), part)
-        return pltpu.make_async_remote_copy(
-            src_ref=target,
-            dst_ref=target,
-            send_sem=core_send.at[piece, way, part, step - 1],
-            recv_sem=core_recv.at[piece, way, part, step - 1],
-            device_id=spot.partner,
-            device_id_type=MESH,
-        )
-
-    def core_in(piece, way, part, step):
-        target = chunk_other(piece, spot.shard(sign(way) * step), part)
-        return pltpu.make_async_remote_copy(
-            src_ref=target,
-            dst_ref=target,
-            send_sem=core_send.at[piece, way, part, step - 1],
-            recv_sem=core_recv.at[piece, way, part, step - 1],
-            device_id=spot.partner,
-            device_id_type=MESH,
-        )
-
-    own_copies = []
-    for depth in range(LAYERS):
-        for which in range(4):
-            own_copies.append(
-                pltpu.make_async_copy(
-                    attn_sh.at[depth, which],
-                    wa.at[depth, which, rows_at(spot.mp, rows_a), :],
-                    own_sem.at[2 * depth, which],
+            for which in range(4):
+                wa[depth, which, rows_at(spot.mp, rows_a), :] = raw_a[depth, which].astype(
+                    jnp.bfloat16
                 )
-            )
-        for which in range(2):
-            own_copies.append(
-                pltpu.make_async_copy(
-                    ffn_sh.at[depth, which],
-                    wf.at[depth, which, rows_at(spot.mp, rows_f), :],
-                    own_sem.at[2 * depth + 1, which],
+        else:
+            for which in range(2):
+                wf[depth, which, rows_at(spot.mp, rows_f), :] = raw_f[depth, which].astype(
+                    jnp.bfloat16
                 )
-            )
-    greet((spot.ring[0], spot.ring[1], spot.partner))
 
     def launch(piece):
         for way, part in WAYS:
-            ring_out(piece, way, part, 1).start()
+            ring_copy(piece, way, part, 1, 0).start()
 
     def pass_on(piece, step):
         for way, part in WAYS:
             if step <= last_step(n, way, part):
-                ring_in(piece, way, part, step).wait_recv()
+                ring_copy(piece, way, part, step, 1).wait_recv()
                 if step < last_step(n, way, part):
-                    ring_out(piece, way, part, step + 1).start()
-                core_out(piece, way, part, step).start()
+                    ring_copy(piece, way, part, step + 1, 0).start()
+                core_copy(piece, way, part, step, core).start()
 
     def settle(piece, step):
         for way, part in WAYS:
             if step <= last_step(n, way, part):
-                core_in(piece, way, part, step).wait_recv()
-
+                core_copy(piece, way, part, step, 1 - core).wait_recv()
+
+    def look_up(offset):
+        whose = peer(offset)
+
+        @pl.loop(0, count // 8)
+        def _(group):
+            for step in range(8):
+                row = group * 8 + step
+                token = ids_ref[whose, row]
+                row_out[whose, pl.ds(row, 1), :] = table_ref[pl.ds(token, 1), :]
+
+        if offset > 0:
+            deal(0, row_out, row_in, offset).start()
+
+    for piece in range(2 * LAYERS):
+        raw_copy(piece).start()
+    greet([spot.partner] + [(spot.dp, peer(offset)) for offset in range(1, n)])
+    take_own(0)
     launch(0)
-    for copy in own_copies:
-        copy.start()
-    state[...] = states_ref[...]
-    for copy in own_copies:
-        copy.wait()
+    for offset in range(1, 4):
+        look_up(offset)
+    pass_on(0, 1)
+    for offset in range(4, 7):
+        look_up(offset)
+    pass_on(0, 2)
+    take_own(1)
+    launch(1)
+    look_up(7)
+    look_up(0)
+    row_in[spot.mp] = row_out[spot.mp]
+    pass_on(0, 3)
+    for offset in range(1, n):
+        arrived(0, row_in, offset).wait_recv()
+    for whose in range(n):
+        first_ref[:, whose * columns_own : (whose + 1) * columns_own] = row_in[whose]
+    first_ref[...] += where_ref[...]
+    normed, _ = normed_of(first_ref[...])
+    state[...] = normed * gains_ref[0, 0:1, :] + gains_ref[0, 1:2, :]
+    take_own(2)
+    take_own(3)
+    pass_on(0, 4)
 
     lanes = lax.broadcasted_iota(jnp.int32, (1, 128), 1) < 64
     visible = visible_ref[...] > 0.0
@@ -265,25 +318,42 @@
             outs.append(dot_nn((expo / total).astype(jnp.bfloat16), valued))
         mixed_ref[depth, :, columns] = jnp.where(lanes, outs[0], outs[1]).astype(jnp.bfloat16)
 
+    def kept_copies(turn, depth, shard):
+        slot = turn % SLOTS
+        return (
+            pltpu.make_async_copy(slope.at[slot], slope_ref.at[depth, shard], kept_sem.at[0, slot]),
+            pltpu.make_async_copy(act.at[slot], act_ref.at[depth, shard], kept_sem.at[1, slot]),
+        )
+
+    turns = []
+
     def ffn_shard(depth, offset):
         shard = spot.shard(offset)
+        turn = len(turns)
+        turns.append((depth, shard))
+        if turn >= SLOTS:
+            for copy in kept_copies(turn, *turns[turn - SLOTS]):
+                copy.wait()
         rows = rows_at(shard, rows_f)
         hidden = dot_nt(mid_ref[depth], wf[depth, 0, rows, :])
         spread = 0.5 * (1.0 + lax.erf(hidden * (0.5**0.5)))
         mask = mask_ref[depth : depth + 1, pl.ds(pl.multiple_of(shard * rows_f, 128), rows_f)]
         bell = jnp.exp(hidden * hidden * -0.5) * (1.0 / math.sqrt(2.0 * math.pi))
-        slope_ref[depth, shard] = (spread + hidden * bell) * mask
+        slope[turn % SLOTS] = (spread + hidden * bell) * mask
         active = (hidden * spread * mask).astype(jnp.bfloat16)
-        act_ref[depth, shard] = active
+        act[turn % SLOTS] = active
+        for copy in kept_copies(turn, depth, shard):
+            copy.start()
         pre_ref[depth, 1] += dot_nn(active, wf[depth, 1, rows, :])
 
     out_copies = []
     for depth in range(LAYERS):
         piece_a, piece_f = 2 * depth, 2 * depth + 1
-        for step in range(1, steps + 1):
-            pass_on(piece_a, step)
-            if step == steps - 1:
-                launch(piece_f)
+        if depth > 0:
+            for step in range(1, steps + 1):
+                pass_on(piece_a, step)
+                if step == steps - 1:
+                    launch(piece_f)
         for step in range(1, steps + 1):
             settle(piece_a, step)
         copy = pltpu.make_async_copy(wa.at[depth], attn_full.at[depth], out_sem.at[piece_a])
@@ -328,24 +398,89 @@
         out_copies.append(copy)
         normed, _ = normed_of(pre_ref[depth, 1])
         state[...] = normed * gains_ref[2 + 2 * depth, 0:1, :] + gains_ref[2 + 2 * depth, 1:2, :]
-    final_ref[...] = state[...]
+
+    spots = (
+        lax.broadcasted_iota(jnp.int32, (slots, count), 1) == places_ref[...]
+    ).astype(jnp.bfloat16)
+    picked[spot.mp] = dot_nn(spots, state[...].astype(jnp.bfloat16)).astype(jnp.bfloat16)
+    for offset in range(1, n):
+        share(1, picked, offset).start()
+    out_b = out_ref[...].astype(jnp.bfloat16)
+    rows_v = out_ref.shape[0]
+    hits = (
+        labels_ref[...] == spot.mp * rows_v + lax.broadcasted_iota(jnp.int32, (rows_v, 1), 0)
+    ).astype(jnp.float32)
+    for offset in range(1, n):
+        arrived(1, picked, offset).wait_recv()
+    picked_all = picked[...].reshape(n * slots, -1)
+    logits = dot_nt(out_b, picked_all)
+    peak = jnp.max(logits, axis=0, keepdims=True)
+    expsum = jnp.sum(jnp.exp(logits - peak), axis=0, keepdims=True)
+    stats[spot.mp, 0:1, :] = peak
+    stats[spot.mp, 1:2, :] = expsum
+    stats[spot.mp, 2:3, :] = jnp.sum(hits * logits, axis=0, keepdims=True)
+    for offset in range(1, n):
+        share(2, stats, offset).start()
+    for offset in range(1, n):
+        arrived(2, stats, offset).wait_recv()
+    peak = stats[0, 0:1, :]
+    for whose in range(1, n):
+        peak = jnp.maximum(peak, stats[whose, 0:1, :])
+    expsum = stats[0, 1:2, :] * jnp.exp(stats[0, 0:1, :] - peak)
+    target = stats[0, 2:3, :]
+    for whose in range(1, n):
+        expsum = expsum + stats[whose, 1:2, :] * jnp.exp(stats[whose, 0:1, :] - peak)
+        target = target + stats[whose, 2:3, :]
+    log_total = peak + jnp.log(expsum)
+    valid = valid_ref[...] > 0.0
+    loss_ref[...] = jnp.where(valid, log_total - target, 0.0)
+    grad_logits = jnp.where(valid, jnp.exp(logits - log_total) - hits, 0.0).astype(jnp.bfloat16)
+    picked_grad = dot_tn(grad_logits, out_b).astype(jnp.bfloat16)
+    for whose in range(n):
+        back_out[whose] = picked_grad[whose * slots : (whose + 1) * slots, :]
+    for offset in range(1, n):
+        deal(3, back_out, back_in, offset).start()
+    back_in[spot.mp] = back_out[spot.mp]
+    out_grad_ref[...] = dot_nn(grad_logits, picked_all)
+    for offset in range(1, n):
+        arrived(3, back_in, offset).wait_recv()
+    summed = back_in[0].astype(jnp.float32)
+    for whose in range(1, n):
+        summed = summed + back_in[whose].astype(jnp.float32)
+    high = summed.astype(jnp.bfloat16)
+    low = (summed - high.astype(jnp.float32)).astype(jnp.bfloat16)
+    grad_ref[...] = dot_tn(spots, high) + dot_tn(spots, low)
+
     for piece in range(2 * LAYERS):
         for way, part in WAYS:
             for step in range(1, last_step(n, way, part) + 1):
-                ring_out(piece, way, part, step).wait_send()
-                core_out(piece, way, part, step).wait_send()
+                ring_copy(piece, way, part, step, 0).wait_send()
+                core_copy(piece, way, part, step, core).wait_send()
+    for offset in range(1, n):
+        deal(0, row_out, row_in, offset).wait_send()
+        share(1, picked, offset).wait_send()
+        share(2, stats, offset).wait_send()
+        deal(3, back_out, back_in, offset).wait_send()
+    for turn in range(len(turns) - SLOTS, len(turns)):
+        for copy in kept_copies(turn, *turns[turn]):
+            copy.wait()
     for copy in out_copies:
         copy.wait()
 
 
-def forward_call(n, visible, states, gains, masks, attn_b, ffn_b):
-    count, width = states.shape
-    rows_f = ffn_b.shape[2]
+def forward_call(
+    n, ids, table, where, visible, gains, masks, places, labels, valid, out_table, attn, ffn
+):
+    count, width = where.shape
+    rows_f = ffn.shape[2]
+    slots = places.shape[0]
     f32, bf16 = jnp.float32, jnp.bfloat16
     vmem = pl.BlockSpec(memory_space=pltpu.VMEM)
+    smem = pl.BlockSpec(memory_space=pltpu.SMEM)
     anywhere = pl.BlockSpec(memory_space=pl.ANY)
     shape = jax.ShapeDtypeStruct
-    sems = pltpu.SemaphoreType.DMA((2 * LAYERS, 2, 2, n // 2))
+    dma = pltpu.SemaphoreType.DMA
+    sems = dma((2 * LAYERS, 2, 2, n // 2))
     return pl.pallas_call(
         functools.partial(forward_kernel, n),
         out_shape=(
@@ -359,25 +494,41 @@
             shape((LAYERS, count, width), bf16),
             shape((LAYERS, n, count, rows_f), f32),
             shape((LAYERS, n, count, rows_f), bf16),
+            shape((count, width), f32),
+            shape(out_table.shape, f32),
+            shape((1, n * slots), f32),
         ),
-        in_specs=[vmem, vmem, vmem, vmem, anywhere, anywhere],
-        out_specs=(anywhere, anywhere) + (vmem,) * 8,
+        in_specs=[smem] + [vmem] * 9 + [anywhere] * 2,
+        out_specs=(anywhere,) * 2 + (vmem,) * 6 + (anywhere,) * 2 + (vmem,) * 3,
         scratch_shapes=[
             pltpu.VMEM((LAYERS, 4, width, width), bf16),
             pltpu.VMEM((LAYERS, 2, rows_f * n, width), bf16),
+            pltpu.VMEM(attn.shape, f32),
+            pltpu.VMEM(ffn.shape, f32),
+            pltpu.VMEM((SLOTS, count, rows_f), f32),
+            pltpu.VMEM((SLOTS, count, rows_f), bf16),
             pltpu.VMEM((count, width), f32),
-            pltpu.SemaphoreType.DMA((2 * LAYERS, 4)),
-            pltpu.SemaphoreType.DMA((2 * LAYERS,)),
+            pltpu.VMEM((n, count, table.shape[1]), f32),
+            pltpu.VMEM((n, count, table.shape[1]), f32),
+            pltpu.VMEM((n, slots, width), bf16),
+            pltpu.VMEM((n, 8, n * slots), f32),
+            pltpu.VMEM((n, slots, width), bf16),
+            pltpu.VMEM((n, slots, width), bf16),
+            dma((2 * LAYERS,)),
+            dma((2 * LAYERS,)),
+            dma((2, SLOTS)),
             sems,
             sems,
             sems,
             sems,
+            dma((4, n - 1)),
+            dma((4, n - 1)),
         ],
         compiler_params=pltpu.CompilerParams(
             collective_id=1, has_side_effects=True, vmem_limit_bytes=VMEM_LIMIT
         ),
         name="forward_layers",
-    )(visible, states, gains, masks, attn_b, ffn_b)
+    )(ids, table, where, visible, gains, masks, places, labels, valid, out_table, attn, ffn)
 
 
 def norm_back(grad, values, gain):
@@ -390,9 +541,6 @@
         jnp.sum(grad * normed, axis=0, keepdims=True),
         jnp.sum(grad, axis=0, keepdims=True),
     )
-
-
-SLOTS = 3
 
 
 def backward_kernel(
@@ -1204,53 +1352,25 @@
     gains_v,
 ):
     rank = lax.axis_index("mp")
-    count = tokens.shape[2]
+    n = tokens.shape[1]
+    count, width = tokens.shape[2], gains.shape[2]
     flat_ids = tokens.reshape(-1)
     all_lengths = lengths.reshape(-1)
     length = lax.dynamic_index_in_dim(all_lengths, rank, keepdims=False)
     masks = jnp.minimum(ramp, RAMP).astype(jnp.float32) / RAMP
-    looked = jnp.take(table, flat_ids, axis=0)
-    embedded = lax.all_to_all(looked, "mp", split_axis=0, concat_axis=1, tiled=True)
-    first = embedded + sinusoid(count, embedded.shape[1])
-    states, _ = layer_norm(first, gains[0, 0], gains[0, 1])
-    n = attn.shape[3] // attn.shape[2]
     visible = (jnp.arange(count) < length).astype(jnp.float32)[None, :]
-    attn_full, ffn_full, states, *kept, slope, act = forward_call(
-        n, visible, states, gains, masks, attn.astype(jnp.bfloat16), ffn.astype(jnp.bfloat16)
-    )
-    spots = places.reshape(-1)
-    picked = jnp.take(states, spots, axis=0).astype(jnp.bfloat16)
-    picked_all = lax.all_gather(picked, "mp", axis=0, tiled=True)
-    out_b = out_table.astype(jnp.bfloat16)
-    logits = jnp.einsum("rd,vd->rv", picked_all, out_b, preferred_element_type=jnp.float32)
-    labels = targets.reshape(-1)
-    columns = rank * out_table.shape[0] + jnp.arange(out_table.shape[0])
-    hits = (labels[:, None] == columns[None, :]).astype(jnp.float32)
-    peak = jnp.max(logits, axis=1)
-    expsum = jnp.sum(jnp.exp(logits - peak[:, None]), axis=1)
-    target_part = jnp.sum(hits * logits, axis=1)
-    peak_all, expsum_all, target_all = merged((peak, expsum, target_part), "mp", combine_vocab)
-    log_total = peak_all + jnp.log(expsum_all)
     slot_count = targets.shape[2]
+    slots = 32 * -(-slot_count // 32)
     counted = jnp.maximum(1, all_lengths * slot_count // count)
-    valid = (jnp.arange(slot_count)[None, :] < counted[:, None]).reshape(-1)
-    loss_pair = jnp.stack(
-        [
-            jnp.sum(jnp.where(valid, log_total - target_all, 0.0)),
-            jnp.sum(counted).astype(jnp.float32),
-        ]
-    )
-    grad_logits = jnp.where(
-        valid[:, None], jnp.exp(logits - log_total[:, None]) - hits, 0.0
-    ).astype(jnp.bfloat16)
-    out_grad = jnp.einsum("rv,rd->vd", grad_logits, picked_all, preferred_element_type=jnp.float32)
-    picked_grad = lax.psum_scatter(
-        jnp.dot(grad_logits, out_b, preferred_element_type=jnp.float32),
-        "mp",
-        scatter_dimension=0,
-        tiled=True,
-    )
-    grad = jnp.zeros_like(states).at[spots].add(picked_grad)
+    valid = (jnp.arange(slots)[None, :] < counted[:, None]).astype(jnp.float32).reshape(1, -1)
+    extra = slots - slot_count
+    spots = jnp.pad(places.reshape(-1), (0, extra), constant_values=-1)[:, None]
+    labels = jnp.pad(targets[0], ((0, 0), (0, extra)), constant_values=-1).reshape(1, -1)
+    where = sinusoid(count, width)
+    attn_full, ffn_full, first, *kept, slope, act, grad, out_grad, losses = forward_call(
+        n, tokens[0], table, where, visible, gains, masks, spots, labels, valid, out_table, attn, ffn
+    )
+    loss_pair = jnp.stack([jnp.sum(losses), jnp.sum(counted).astype(jnp.float32)])
     attn_sum, ffn_sum, grad_sum, gains_grad = backward_call(
         n, visible, grad, first, gains, kept, attn_full, ffn_full, slope, act
     )

time: 661 us -> 585 us (0.89)
  blocking collectives: 139 us -> 49.4 us
  Pallas kernels: 323 us -> 374 us
  other arithmetic: 67.2 us -> 52.8 us
  starting transfers between devices: 14.4 us -> 3.61 us
  local copies, waits for them, and re-layouts: 19.4 us -> 11.6 us
    unnamed x2 -> x0, blocking collectives: 57.3 us -> none
    pallas_call x1, Pallas kernels: 150 us -> 202 us  [forward_call(): pl.pallas_call(functools.partial(forward_kernel, n), out_shape=(shape((LA...]
    all_gather x1 -> x0, blocking collectives: 31.7 us -> none  [local(): picked_all = lax.all_gather(picked, 'mp', axis=0, tiled=True)]
    gather x3 -> x0, local copies, waits for them, and re-layouts: 7.55 us -> none  [the longest x2 5.79 us: local(): looked = jnp.take(table, flat_ids, axis=0)]
    all_to_all x1 -> x0, starting transfers between devices: 7.25 us -> none  [local(): lax.all_to_all(looked, 'mp', split_axis=0, concat_axis=1, tiled=True)]
    convert_element_type x2 -> x1, other arithmetic: 6.83 us -> 0.07 us  [local(): (jnp.arange(slots)[None, :] < counted[:, None]).astype(jnp.float32)]
  transfers between devices with their start and end apart: 5 -> 2, of which waited for: 4 -> 2; matrix products, arithmetic and copies ran while one was open for 4% -> 1% of each run, Pallas kernels for 0% -> 0%
where the time goes in v3:
time: 585 us; the launch traced here: 577 us
  Pallas kernels  374 us (64%)
  waiting for transfers between devices  64.3 us (11%)
  other arithmetic  52.8 us (9%)
  blocking collectives  49.4 us (8%)
  between operations  20.6 us (4%)
  local copies, waits for them, and re-layouts  11.6 us (2%)
    pallas_call x1, Pallas kernels, forward_call(): pl.pallas_call(functools.partial(forward_kernel, n), out_shape=(shape((LA...  202 us
    pallas_call x1, Pallas kernels, backward_call(): pl.pallas_call(functools.partial(backward_kernel, n), out_shape=(shape((L...  172 us
    psum x1, waiting for transfers between devices, local(): lax.psum((table_grad, out_grad, gains_grad, loss_pair), 'dp')  43.5 us
    psum x1, blocking collectives, local(): square_total, gains_sum = lax.psum((shard_squares, gains_part), 'mp')  37.2 us
    sub x5, other arithmetic, adamw(): weight - rate * (fixed_one / (jnp.sqrt(fixed_two) + adam_eps) + decay * w...  24.5 us
    all_to_all x1, waiting for transfers between devices, local(): lax.all_to_all(grad_sum, 'mp', split_axis=1, concat_axis=0, tiled=True)  20.8 us
    psum x1, blocking collectives, local(): lax.psum((table_grad, out_grad, gains_grad, loss_pair), 'dp')  12.3 us
    scatter-add x1, other arithmetic, local(): table_grad = jnp.zeros_like(table).at[flat_ids].add(returned)  11.9 us
  transfers between devices with their start and end apart: 2, of which 2 were waited for; matrix products, arithmetic and copies ran while one was open for 1% of the time, Pallas kernels for 0%

profile of v3, /device:TPU:0, one launch (start us, length us, event | category | flops | bytes accessed | tf_op | source)
XLA Modules:
  0.0 576.7 jit_solution(9841214012706658473)
XLA Ops:
  7.2 1.3 fusion.16
  8.5 0.0 copy-start.18
  8.5 2.8 copy.62.table_ref
  11.3 1.4 fusion.7
  12.7 0.0 copy-done.18
  12.7 0.6 constant_dynamic-slice_fusion
  13.3 1.2 compare_convert_fusion.visible_ref
  14.5 0.0 copy-done.15
  14.5 0.6 convert_multiply_fusion.mask_ref
  15.2 0.0 copy-done.19
  15.2 0.7 copy.63.places_ref
  15.9 0.0 copy-done.16
  15.9 0.6 reshape.147.labels_ref
  16.5 0.1 fusion.9
  16.6 0.6 reshape.150.valid_ref
  17.2 0.9 pad_maximum_fusion.where_ref
  18.2 202.0 %forward_layers.1 = (bf16[2,4,768,768]{3,2,1,0:T(8,128)(2,1)}, bf16[2,2,3072,768]{3,2,1,0:T(8,128)(2,1)}, f32[256,768]{1,0:T(8,128)}, bf16[2,256,768]{2,1,0:T(8,...) custom-call(s32[8,256]{1,0:T(8,128)} %bitcast.32, ...), custom_call_target="tpu_custom_call" | custom-call | tf_op jit(solution)/shard_map/forward_layers/pallas_call | solution.py:484
  220.1 172.4 %backward_layers.1 = (f32[2,4,96,768]{3,2,1,0:T(8,128)}, f32[2,2,384,768]{3,2,1,0:T(8,128)}, f32[256,768]{1,0:T(8,128)}, f32[5,2,768]{2,1,0:T(2,128)}) custom-call(f32[1,256]{1,0:T(1,128)} %compare_convert_fusion.visible_ref, f32[256,768]{1,0:T(8,128)} %get-tuple-element.35.grad_ref, f32[256,768]{1,0:T(8,128)} %get-tuple-element.36.first_ref, ...), custom_call_target="tpu_custom_call" | custom-call | tf_op jit(solution)/shard_map/backward_layers/pallas_call | solution.py:964
  392.5 0.0 copy-start.11
  392.5 2.3 copy.64
  394.8 3.6 all-to-all-start
  398.4 0.0 all-reduce.7.cloned.1.call-start
  398.4 0.0 copy-done.11
  398.5 20.8 %all-to-all-done = f32[256,8,96]{0,2,1:T(8,128)S(1)} async-done(((f32[256,8,96]{0,2,1:T(8,128)}), f32[256,8,96]{0,2,1:T(8,128)S(1)}, u32[]{:S(2)}, u32[]{:S(2)}) %all-to-all-start) | async-done | bytes 786464 | tf_op jit(solution)/shard_map/all_to_all | solution.py:1377
  419.2 0.3 copy.68
  419.6 11.9 %scatter_custom_fusion = f32[3840,96]{1,0:T(8,128)S(1)} fusion(s32[2048]{0:T(1024)S(1)} %bitcast.34, f32[2048,96]{1,0:T(8,128)S(1)} %bitcast.30, f32[]{:T(128)} %constant.33.clone.1), kind=kCustom, calls=%fused_computation.21 | custom fusion | flops 196608 | bytes 1474564 | tf_op jit(solution)/shard_map/scatter-add | solution.py:1378
  431.5 1.7 copy.67
  433.2 0.0 all-reduce.7.cloned.1.call-update
  434.0 0.0 copy-done.17
  434.0 0.6 reduce_sum.63
  434.6 0.7 pad_maximum_fusion.1
  435.4 0.0 copy-done.14
  435.4 12.3 %all-reduce.3 = (f32[2]{0:T(128)}, f32[5,2,768]{2,1,0:T(2,128)S(1)}) all-reduce(f32[2]{0:T(128)S(1)} %pad_maximum_fusion.1, f32[5,2,768]{2,1,0:T(2,128)S(1)} %copy-done.14), channel_id=1, replica_groups=mesh['dp'=4,'mp'=8] {'dp'}, use_global_device_ids=true, to_apply=%region_2.3 | all-reduce | flops 7682 | bytes 61456 | tf_op jit(solution)/shard_map/psum | solution.py:1379
  447.7 0.0 copy-done
  447.7 1.2 multiply_reduce_fusion.1
  448.9 4.2 multiply_reduce_fusion
  454.4 43.5 %all-reduce.7.cloned.1.call-done = (f32[3840,96]{0,1:T(8,128)}, f32[480,768]{1,0:T(8,128)}) async-done(((f32[3840,96]{0,1:T(8,128)}, f32[480,768]{1,0:T(8,128)}), (f32[3840,96]{0,1:T(8,128)}, f32[480,768]{1,0:T(8,128)})) %all-reduce.7.cloned.1.call-update) | async-done | bytes 2949136 | tf_op jit(solution)/shard_map/psum | solution.py:1379
  497.8 2.5 multiply_reduce_fusion.3
  500.3 0.0 copy-done.3
  500.3 1.0 multiply_reduce_fusion.2
  502.6 37.2 %all-reduce.2 = (f32[]{:T(128)}, f32[5,2,768]{2,1,0:T(2,128)S(1)}) all-reduce(f32[]{:T(128)S(6)} %add.132, f32[5,2,768]{2,1,0:T(2,128)S(1)} %get-tuple-element.88), channel_id=1, replica_groups=mesh['dp'=4,'mp'=8] {'mp'}, use_global_device_ids=true, to_apply=%region_10.11 | all-reduce | flops 7681 | bytes 61448 | tf_op jit(solution)/shard_map/psum | solution.py:1389
  539.7 0.6 multiply_reduce_fusion.4
  541.8 0.0 slice-start.1
  541.8 7.4 %multiply_subtract_fusion.1 = (f32[2,4,96,768]{3,2,1,0:T(8,128)}, f32[2,4,96,768]{3,2,1,0:T(8,128)}, f32[2,4,96,768]{3,2,1,0:T(8,128)}) fusion(f32[2,4,96,768]{3,2,1,0:T(8,128)} %attn_sh.1, f32[2,4,96,768]{3,2,1,0:T(8,128)S(1)} %copy-done, f32[]{:T(128)S(6)} %div.102, f32[2,4,96,768]{3,2,1,0:T(8,128)} %param.27, f32[2,4,96,768]{3,2,1,0:T(8,128)} %param.26), kind=kLoop, calls=%fused_computation.8 | loop fusion | flops 9437184 | bytes 16515076 | tf_op jit(solution)/shard_map/sub | solution.py:1173
  549.2 0.0 slice-done
  549.2 0.0 slice-done.1
  549.2 0.0 copy-start.5
  549.2 0.0 copy-start.6
  549.2 0.0 copy-start.7
  549.2 10.7 %multiply_subtract_fusion = (f32[2,2,384,768]{3,2,1,0:T(8,128)}, f32[2,2,384,768]{3,2,1,0:T(8,128)}, f32[2,2,384,768]{3,2,1,0:T(8,128)}) fusion(f32[2,2,384,768]{3,2,1,0:T(8,128)S(1)} %bitcast.28, f32[2,2,384,768]{3,2,1,0:T(8,128)} %get-tuple-element.47, f32[]{:T(128)S(6)} %div.102, f32[2,2,384,768]{3,2,1,0:T(8,128)} %param.30, f32[2,2,384,768]{3,2,1,0:T(8,128)} %param.29), kind=kLoop, calls=%fused_computation.3 | loop fusion | flops 18874368 | bytes 33030148 | tf_op jit(solution)/shard_map/sub | solution.py:1173
  559.9 0.0 copy-done.1
  559.9 0.0 copy-done.5
  559.9 0.0 copy-done.6
  559.9 0.4 copy-done.7
  560.4 2.8 multiply_subtract_fusion.3
  563.2 0.0 copy-done.2
  563.2 0.0 copy-done.4
  563.2 1.0 copy-done.8
  564.2 0.4 copy-done.9
  564.7 2.9 multiply_subtract_fusion.2
  567.5 0.0 copy-done.10
  567.5 0.0 copy-done.12
  567.5 0.0 copy-done.13
  567.5 0.7 multiply_subtract_fusion.4
  (22 shorter events, 0.1 us)
Async XLA Ops:
  8.5 4.2 copy-start.18
  8.5 6.0 %copy-start.15 = (s32[2,3072]{1,0:T(2,128)S(1)}, s32[2,3072]{1,0:T(2,128)}, u32[]{:S(2)}) copy-start(s32[2,3072]{1,0:T(2,128)} %param.24) | copy-start | bytes 73732
  8.5 6.7 %copy-start.19 = (s32[1,1,25]{2,1,0:T(1,128)S(1)}, s32[1,1,25]{2,1,0:T(1,128)}, u32[]{:S(2)}) copy-start(s32[1,1,25]{2,1,0:T(1,128)} %param.22) | copy-start | bytes 304
  8.5 7.4 %copy-start.16 = (s32[1,8,25]{2,1,0:T(8,128)S(1)}, s32[1,8,25]{2,1,0:T(8,128)}, u32[]{:S(2)}) copy-start(s32[1,8,25]{2,1,0:T(8,128)} %param.23) | copy-start | bytes 2404
  392.5 5.9 %copy-start.11 = (s32[1,8,256]{2,1,0:T(8,128)S(1)}, s32[1,8,256]{2,1,0:T(8,128)}, u32[]{:S(2)}) copy-start(s32[1,8,256]{2,1,0:T(8,128)} %param.20) | copy-start | bytes 24580
  394.8 24.4 %all-to-all-start = ((f32[256,8,96]{0,2,1:T(8,128)}), f32[256,8,96]{0,2,1:T(8,128)S(1)}, u32[]{:S(2)}, u32[]{:S(2)}) async-start(f32[256,8,96]{0,2,1:T(8,128)} %bitcast.9), calls=%async_computation | async-start | bytes 1572864 | tf_op jit(solution)/shard_map/all_to_all | solution.py:1377
  398.4 99.5 %all-reduce.7.cloned.1.call-start = ((), (), s32[]{:S(2)}) async-start(), calls=%async_computation.1 | async-start | bytes 5898240 | tf_op jit(solution)/shard_map/psum | solution.py:1379
  433.2 0.8 copy-start.17
  433.2 2.2 copy-start.14
  433.2 14.4 %copy-start = (f32[2,4,96,768]{3,2,1,0:T(8,128)S(1)}, f32[2,4,96,768]{3,2,1,0:T(8,128)}, u32[]{:S(2)}) copy-start(f32[2,4,96,768]{3,2,1,0:T(8,128)} %get-tuple-element.46) | copy-start | bytes 7077892
  497.8 2.5 copy-start.3
  500.3 48.9 %slice-start = ((s8[4718592]{0:T(1024)(128)(4,1)}), s8[524288]{0:T(1024)(128)(4,1)S(1)}, s32[]{:S(2)}) async-start(s8[4718592]{0:T(1024)(128)(4,1)} %bitcast.27), calls=%async_computation.2 | async-start | bytes 1048576
  541.8 7.4 %slice-start.1 = ((s8[4718592]{0:T(1024)(128)(4,1)}), s8[4194304]{0:T(1024)(128)(4,1)S(1)}, s32[]{:S(2)}) async-start(s8[4718592]{0:T(1024)(128)(4,1)} %bitcast.27), calls=%async_computation.3 | async-start | bytes 8388608
  549.2 10.7 %copy-start.1 = (f32[3840,96]{0,1:T(8,128)S(1)}, f32[3840,96]{0,1:T(8,128)}, u32[]{:S(2)}) copy-start(f32[3840,96]{0,1:T(8,128)} %param.31) | copy-start | bytes 4423684
  549.2 10.7 %copy-start.5 = (f32[3840,96]{0,1:T(8,128)S(1)}, f32[3840,96]{0,1:T(8,128)}, u32[]{:S(2)}) copy-start(f32[3840,96]{0,1:T(8,128)} %get-tuple-element.89) | copy-start | bytes 4423684
  549.2 10.7 %copy-start.6 = (f32[3840,96]{0,1:T(8,128)S(1)}, f32[3840,96]{0,1:T(8,128)}, u32[]{:S(2)}) copy-start(f32[3840,96]{0,1:T(8,128)} %param.33) | copy-start | bytes 4423684
  549.2 11.1 %copy-start.7 = (f32[3840,96]{0,1:T(8,128)S(1)}, f32[3840,96]{0,1:T(8,128)}, u32[]{:S(2)}) copy-start(f32[3840,96]{0,1:T(8,128)} %param.32) | copy-start | bytes 4423684
  560.4 2.8 copy-start.2
  560.4 2.8 copy-start.4
  560.4 3.9 copy-start.8
  560.4 4.3 copy-start.9
  564.7 2.9 copy-start.10
  564.7 2.9 copy-start.12
  564.7 2.9 copy-start.13
Sparse Core Ops, SparseCore 0:
  433.4 64.4 all-reduce.6

commit v4 on v3

--- a/solution.py
+++ b/solution.py
@@ -26,7 +26,7 @@
 
 
 MESH = pl.DeviceIdType.MESH
-VMEM_LIMIT = 60 * 1024 * 1024
+VMEM_LIMIT = 62 * 1024 * 1024
 SLOTS = 3
 
 
@@ -545,23 +545,31 @@
 
 def backward_kernel(
     n,
+    ids_ref,
+    counted_ref,
+    losses_ref,
     visible_ref,
     grad_ref,
     first_ref,
     gains_ref,
+    out_grad_ref,
     inputs_ref,
-    proj_ref,
     mixed_ref,
-    pre_ref,
     mid_ref,
+    proj_all,
+    pre_all,
     attn_full,
     ffn_full,
     slope_all,
     act_all,
     attn_sum,
     ffn_sum,
-    grad_out,
-    pair_out,
+    table_sum,
+    out_sum,
+    small_out,
+    square_out,
+    proj,
+    pre,
     wa,
     wf,
     slope,
@@ -570,7 +578,6 @@
     sum_f,
     theirs_f,
     land_f,
-    theirs_a,
     land_a,
     ring_a,
     ring_f,
@@ -599,6 +606,26 @@
     out_sem,
     last_send,
     last_recv,
+    small,
+    small_in,
+    columns_out,
+    columns_in,
+    table_grad,
+    table_half,
+    out_half,
+    out_done,
+    squares,
+    square_parts,
+    proj_sem,
+    small_send,
+    small_recv,
+    deal_send,
+    deal_recv,
+    half_send,
+    half_recv,
+    half_sem,
+    norm_send,
+    norm_recv,
 ):
     spot = Spot(n)
     core = spot.core
@@ -612,6 +639,9 @@
     def rows_at(shard, rows):
         return pl.ds(pl.multiple_of(shard * rows, 16), rows)
 
+    def peer(offset):
+        return (spot.mp + offset + n) % n
+
     def remote(source, target, send, recv, device):
         return pltpu.make_async_remote_copy(
             src_ref=source,
@@ -635,6 +665,12 @@
             pltpu.make_async_copy(slope_all.at[depth, shard], slope.at[slot], load_sem.at[1, slot]),
             pltpu.make_async_copy(act_all.at[depth, shard], act.at[slot], load_sem.at[2, slot]),
         )
+
+    def load_pre(depth):
+        return pltpu.make_async_copy(pre_all.at[depth], pre, proj_sem.at[0])
+
+    def load_proj(depth):
+        return pltpu.make_async_copy(proj_all.at[depth], proj, proj_sem.at[1])
 
     def load_attn(depth):
         return pltpu.make_async_copy(attn_full.at[depth], wa, wa_sem.at[0])
@@ -663,7 +699,7 @@
 
     def swap_copy(depth, part):
         return remote(
-            theirs_a.at[part],
+            wa.at[part],
             land_a.at[part],
             swap_send.at[depth, part],
             swap_recv.at[depth, part],
@@ -763,21 +799,28 @@
             local.wait()
             away.wait_send()
         if kind == 0:
-            done_a[...] = spread_a[depth, 0].astype(jnp.float32) + spread_a[depth, 1].astype(
+            for part in range(2):
+                value = spread_a[depth, 0, part].astype(jnp.float32) + spread_a[
+                    depth, 1, part
+                ].astype(jnp.float32)
+                done_a[part] = value
+                add_squares(value)
+        else:
+            value = spread_f[depth, 0].astype(jnp.float32) + spread_f[depth, 1].astype(
                 jnp.float32
             )
-        else:
-            done_f[...] = spread_f[depth, 0].astype(jnp.float32) + spread_f[depth, 1].astype(
-                jnp.float32
-            )
+            done_f[...] = value
+            add_squares(value)
         for copy in out_copies(piece):
             copy.start()
 
-    load_attn(LAYERS - 1).start()
+    load_pre(LAYERS - 1).start()
     for turn in range(SLOTS):
         for copy in loads(turn):
             copy.start()
-    greet((spot.ring[0], spot.ring[1], spot.partner, spot.across))
+    load_attn(LAYERS - 1).start()
+    load_proj(LAYERS - 1).start()
+    greet([spot.partner, spot.across] + [(spot.dp, peer(offset)) for offset in range(1, n)])
     state[...] = grad_ref[...]
     lanes = lax.broadcasted_iota(jnp.int32, (1, 128), 1) < 64
     visible = visible_ref[...] > 0.0
@@ -804,9 +847,9 @@
 
     def head_pair(depth, pair):
         columns = pl.ds(pl.multiple_of(pair * 128, 128), 128)
-        query = proj_ref[depth, 0, :, columns]
-        keyed = proj_ref[depth, 1, :, columns]
-        valued = proj_ref[depth, 2, :, columns]
+        query = proj[0, :, columns]
+        keyed = proj[1, :, columns]
+        valued = proj[2, :, columns]
         grad_mixed = grad_rows[4, :, columns]
         outs = []
         for side in range(2):
@@ -833,8 +876,9 @@
     def layer(depth, hooks):
         base = (LAYERS - 1 - depth) * n
         piece_a, piece_f = 2 * depth, 2 * depth + 1
-        grad_two, pair_out[2 + 2 * depth, 0:1, :], pair_out[2 + 2 * depth, 1:2, :] = norm_back(
-            state[...], pre_ref[depth, 1], gains_ref[2 + 2 * depth, 0:1, :]
+        load_pre(depth).wait()
+        grad_two, small[0, 4 + 4 * depth : 5 + 4 * depth, :], small[0, 5 + 4 * depth : 6 + 4 * depth, :] = norm_back(
+            state[...], pre[1], gains_ref[2 + 2 * depth, 0:1, :]
         )
         state[...] = grad_two
         right_f[0] = mid_ref[depth]
@@ -850,26 +894,31 @@
             hooks.get(("ffn", step), lambda: None)()
         fold(base + n - 1)
         hooks.get("middle", lambda: None)()
-        grad_one, pair_out[1 + 2 * depth, 0:1, :], pair_out[1 + 2 * depth, 1:2, :] = norm_back(
-            state[...], pre_ref[depth, 0], gains_ref[1 + 2 * depth, 0:1, :]
-        )
+        grad_one, small[0, 2 + 4 * depth : 3 + 4 * depth, :], small[0, 3 + 4 * depth : 4 + 4 * depth, :] = norm_back(
+            state[...], pre[0], gains_ref[1 + 2 * depth, 0:1, :]
+        )
+        if depth > 0:
+            load_pre(depth - 1).start()
         state[...] = grad_one
         grad_rows[3] = grad_one.astype(jnp.bfloat16)
         load_attn(depth).wait()
+        load_proj(depth).wait()
         grad_rows[4] = dot_nt(grad_rows[3], wa[3]).astype(jnp.bfloat16)
 
         @pl.loop(0, HEADS // 2)
         def _(pair):
             head_pair(depth, pair)
 
+        if depth > 0:
+            load_proj(depth - 1).start()
         hooks.get("heads", lambda: None)()
+        for which in range(3):
+            state[...] += dot_nt(grad_rows[which], wa[which])
         left_a[0] = inputs_ref[depth]
         left_a[1] = mixed_ref[depth]
         for part in range(2):
-            if depth < LAYERS - 1:
-                swap_copy(depth + 1, part).wait_send()
             left = 0 if part == 0 else other
-            theirs_a[part] = dot_tn(left_a[left], grad_rows[2 * other + part]).astype(jnp.bfloat16)
+            wa[part] = dot_tn(left_a[left], grad_rows[2 * other + part]).astype(jnp.bfloat16)
             if depth < LAYERS - 1:
                 pl.semaphore_wait(swap_free.at[part], 1)
             swap_copy(depth, part).start()
@@ -896,15 +945,110 @@
                 )
         launch(piece_a, True)
         launch(piece_a, False)
-        for which in range(3):
-            state[...] += dot_nt(grad_rows[which], wa[which])
-        if depth > 0:
-            load_attn(depth - 1).start()
-
+
+    def reload_attn():
+        for part in range(2):
+            swap_copy(1, part).wait_send()
+        load_attn(0).start()
+
+    def half_copy(which, stage):
+        buffer = out_half if which == 0 else table_half
+        return remote(
+            buffer.at[2 * stage],
+            buffer.at[2 * stage + 1],
+            half_send.at[which, stage],
+            half_recv.at[which, stage],
+            spot.partner if stage == 0 else spot.across,
+        )
+
+    def half_rows(rows, side):
+        return pl.ds(pl.multiple_of(side * (rows // 2), 16), rows // 2)
+
+    def half_start(which, source):
+        buffer = out_half if which == 0 else table_half
+        buffer[0] = source[half_rows(source.shape[0], other), :].astype(jnp.bfloat16)
+        half_copy(which, 0).start()
+
+    def half_fold(which, source):
+        buffer = out_half if which == 0 else table_half
+        half_copy(which, 0).wait_recv()
+        own = source[half_rows(source.shape[0], core), :]
+        buffer[2] = (own + buffer[1].astype(jnp.float32)).astype(jnp.bfloat16)
+        half_copy(which, 1).start()
+
+    def half_out(which):
+        if which == 0:
+            source, target = out_done, out_sum.at[half_rows(out_sum.shape[0], core), :]
+        else:
+            source = table_grad.at[half_rows(table_sum.shape[0], core), :]
+            target = table_sum.at[half_rows(table_sum.shape[0], core), :]
+        return (
+            pltpu.make_async_copy(source, target, half_sem.at[which]),
+            remote(source, target, half_send.at[which, 2], half_recv.at[which, 2], spot.partner),
+        )
+
+    def add_squares(value):
+        squares[...] += jnp.sum(value * value, axis=0, keepdims=True)
+
+    def half_end(which):
+        buffer = out_half if which == 0 else table_half
+        half_copy(which, 1).wait_recv()
+        value = buffer[2].astype(jnp.float32) + buffer[3].astype(jnp.float32)
+        if which == 0:
+            out_done[...] = value
+        else:
+            table_grad[half_rows(table_sum.shape[0], core), :] = value
+        width = squares.shape[1]
+        for start in range(0, value.shape[1], width):
+            add_squares(value[:, start : start + width])
+        for copy in half_out(which):
+            copy.start()
+
+    def small_copy(stage):
+        bit = 1 << max(0, stage - 2)
+        pair = spot.mp + bit - 2 * bit * ((spot.mp // bit) % 2)
+        device = (spot.partner, spot.across)[stage] if stage < 2 else (spot.dp, pair)
+        return remote(
+            small.at[stage],
+            small_in.at[stage],
+            small_send.at[stage],
+            small_recv.at[stage],
+            device,
+        )
+
+    def small_next(stage):
+        small_copy(stage).wait_recv()
+        small[stage + 1] = small[stage] + small_in[stage]
+        if stage < 4:
+            small_copy(stage + 1).start()
+
+    def deal_copy(offset, arriving):
+        source = columns_out.at[peer(offset)]
+        target = columns_in.at[peer(-offset) if arriving else spot.mp]
+        return remote(
+            source,
+            target,
+            deal_send.at[offset - 1],
+            deal_recv.at[offset - 1],
+            (spot.dp, peer(offset)),
+        )
+
+    def table_blocks(first, last):
+        @pl.loop(first, last)
+        def _(block):
+            row = lax.broadcasted_iota(jnp.int32, (256, 1), 0) + block * 256
+            value = jnp.zeros((columns_in.shape[1], 256), jnp.float32)
+            for whose in range(n):
+                chosen = (row == ids_ref[whose : whose + 1, :]).astype(jnp.bfloat16)
+                value = value + dot_nt(columns_in[whose], chosen)
+            table_grad[:, pl.ds(pl.multiple_of(block * 256, 256), 256)] = value
+
+    squares[...] = jnp.zeros_like(squares)
+    half_start(0, out_grad_ref)
     layer(
         1,
         {
-            "middle": lambda: relay(3, 1),
+            "middle": lambda: (relay(3, 1), half_fold(0, out_grad_ref)),
             "heads": lambda: relay(3, 2),
         },
     )
@@ -913,27 +1057,98 @@
     layer(
         0,
         {
+            ("ffn", 0): reload_attn,
             ("ffn", 3): lambda: relay(2, 1),
             ("ffn", 5): lambda: conclude(3),
-            "middle": lambda: relay(2, 2),
+            "middle": lambda: (relay(2, 2), half_end(0)),
             "heads": lambda: relay(1, 1),
             "mats": lambda: (relay(2, 3), finish(2)),
         },
     )
-    grad_sum, pair_out[0, 0:1, :], pair_out[0, 1:2, :] = norm_back(
+    grad_sum, small[0, 0:1, :], small[0, 1:2, :] = norm_back(
         state[...], first_ref[...], gains_ref[0, 0:1, :]
     )
-    grad_out[...] = grad_sum
+    width = squares.shape[1]
+    lane = lax.broadcasted_iota(jnp.int32, (1, width), 1)
+    loss = jnp.sum(losses_ref[...], axis=1, keepdims=True) * (1.0 / n)
+    slots = counted_ref[0:1, 0:1] * (1.0 / n)
+    small[0, 10:11, :] = jnp.where(lane == 0, loss, jnp.where(lane == 1, slots, 0.0))
+    small[0, 11:16, :] = jnp.zeros((5, width), jnp.float32)
+    small_copy(0).start()
+    turned = grad_sum.T.astype(jnp.bfloat16)
+    share = columns_in.shape[1]
+    for whose in range(n):
+        columns_out[whose] = turned[whose * share : (whose + 1) * share, :]
+    for offset in range(1, n):
+        deal_copy(offset, False).start()
+    columns_in[spot.mp] = columns_out[spot.mp]
     relay(1, 2)
+    small_next(0)
     conclude(2)
+    for offset in range(1, n):
+        deal_copy(offset, True).wait_recv()
+    blocks = table_sum.shape[1] // 256
+    table_blocks(0, blocks // 2)
     relay(0, 1)
+    small_next(1)
+    table_blocks(blocks // 2, blocks)
+    half_start(1, table_grad)
     relay(1, 3)
+    small_next(2)
+    half_fold(1, table_grad)
     relay(0, 2)
     finish(1)
+    small_next(3)
+    half_end(1)
     relay(0, 3)
     conclude(1)
+    small_next(4)
     finish(0)
+    small_out[...] = small[5]
     conclude(0)
+
+    square = jnp.sum(squares[...], axis=1, keepdims=True)
+    square_parts[n] = jnp.broadcast_to(square, square_parts.shape[1:])
+    swap = remote(
+        square_parts.at[n],
+        square_parts.at[n + 1],
+        norm_send.at[0],
+        norm_recv.at[0],
+        spot.partner,
+    )
+    swap.start()
+    swap.wait_recv()
+    square_parts[spot.mp] = square_parts[n] + square_parts[n + 1]
+
+    def norm_copy(offset, arriving):
+        source = square_parts.at[spot.mp]
+        target = square_parts.at[peer(-offset) if arriving else spot.mp]
+        return remote(
+            source, target, norm_send.at[offset], norm_recv.at[offset], (spot.dp, peer(offset))
+        )
+
+    for offset in range(1, n):
+        norm_copy(offset, False).start()
+    gains_grad = small[5, 0:10, :]
+    square = jnp.sum(jnp.sum(gains_grad * gains_grad, axis=0, keepdims=True), axis=1, keepdims=True)
+    for offset in range(1, n):
+        norm_copy(offset, True).wait_recv()
+    for whose in range(n):
+        square = square + square_parts[whose, 0:1, :]
+    square_out[...] = square
+
+    swap.wait_send()
+    for offset in range(1, n):
+        norm_copy(offset, False).wait_send()
+        deal_copy(offset, False).wait_send()
+    for stage in range(5):
+        small_copy(stage).wait_send()
+    for which in range(2):
+        half_copy(which, 0).wait_send()
+        half_copy(which, 1).wait_send()
+        local, away = half_out(which)
+        local.wait()
+        away.wait()
     for turn in range(total - SLOTS, total):
         core_copy(turn).wait_send()
     for part in range(2):
@@ -950,10 +1165,15 @@
         away.wait_recv()
 
 
-def backward_call(n, visible, grad, first, gains, kept, attn_full, ffn_full, slope, act):
+def backward_call(
+    n, ids, counted, losses, visible, grad, first, gains, out_grad, kept, attn_full, ffn_full, slope, act, table
+):
+    inputs, proj, mixed, pre, mid = kept
     count, width = grad.shape
     rows_f = ffn_full.shape[2] // n
     rows_a = attn_full.shape[2] // n
+    rows_v = out_grad.shape[0]
+    words, share = table.shape
     f32, bf16 = jnp.float32, jnp.bfloat16
     vmem = pl.BlockSpec(memory_space=pltpu.VMEM)
     anywhere = pl.BlockSpec(memory_space=pl.ANY)
@@ -966,12 +1186,16 @@
         out_shape=(
             shape((LAYERS, 4, rows_a, width), f32),
             shape((LAYERS, 2, rows_f, width), f32),
-            shape((count, width), f32),
-            shape(gains.shape, f32),
+            shape((share, words), f32),
+            shape((rows_v, width), f32),
+            shape((16, width), f32),
+            shape((1, 128), f32),
         ),
-        in_specs=[vmem] * 9 + [anywhere] * 4,
-        out_specs=(anywhere, anywhere, vmem, vmem),
+        in_specs=[vmem] * 11 + [anywhere] * 6,
+        out_specs=(anywhere,) * 4 + (vmem,) * 2,
         scratch_shapes=[
+            pltpu.VMEM((3, count, width), bf16),
+            pltpu.VMEM((2, count, width), f32),
             pltpu.VMEM((4, width, width), bf16),
             pltpu.VMEM((SLOTS, 2, rows_f, width), bf16),
             pltpu.VMEM((SLOTS, count, rows_f), f32),
@@ -980,7 +1204,6 @@
             pltpu.VMEM((LAYERS, n, rows_f, width), bf16),
             pltpu.VMEM((SLOTS, rows_f, width), bf16),
             pltpu.VMEM((SLOTS, rows_f, width), bf16),
-            pltpu.VMEM((2, width, width), bf16),
             pltpu.VMEM((2, width, width), bf16),
             pltpu.VMEM((2, 2, n // 2, rows_a, width), bf16),
             pltpu.VMEM((2, 2, n // 2, rows_f // 2, width), bf16),
@@ -1009,12 +1232,35 @@
             dma((2 * LAYERS,)),
             dma((2 * LAYERS,)),
             dma((2 * LAYERS,)),
+            pltpu.VMEM((6, 16, width), f32),
+            pltpu.VMEM((5, 16, width), f32),
+            pltpu.VMEM((n, share, count), bf16),
+            pltpu.VMEM((n, share, count), bf16),
+            pltpu.VMEM((share, words), f32),
+            pltpu.VMEM((4, share // 2, words), bf16),
+            pltpu.VMEM((4, rows_v // 2, width), bf16),
+            pltpu.VMEM((rows_v // 2, width), f32),
+            pltpu.VMEM((1, width), f32),
+            pltpu.VMEM((n + 2, 8, 128), f32),
+            dma((2,)),
+            dma((5,)),
+            dma((5,)),
+            dma((n - 1,)),
+            dma((n - 1,)),
+            dma((2, 3)),
+            dma((2, 3)),
+            dma((2,)),
+            dma((n,)),
+            dma((n,)),
         ],
         compiler_params=pltpu.CompilerParams(
             collective_id=2, has_side_effects=True, vmem_limit_bytes=VMEM_LIMIT
         ),
         name="backward_layers",
-    )(visible, grad, first, gains, *kept, attn_full, ffn_full, slope, act)
+    )(
+        ids, counted, losses, visible, grad, first, gains, out_grad, inputs, mixed, mid,
+        proj, pre, attn_full, ffn_full, slope, act,
+    )
 
 
 def merged(value, axis, join):
@@ -1370,24 +1616,13 @@
     attn_full, ffn_full, first, *kept, slope, act, grad, out_grad, losses = forward_call(
         n, tokens[0], table, where, visible, gains, masks, spots, labels, valid, out_table, attn, ffn
     )
-    loss_pair = jnp.stack([jnp.sum(losses), jnp.sum(counted).astype(jnp.float32)])
-    attn_sum, ffn_sum, grad_sum, gains_grad = backward_call(
-        n, visible, grad, first, gains, kept, attn_full, ffn_full, slope, act
-    )
-    returned = lax.all_to_all(grad_sum, "mp", split_axis=1, concat_axis=0, tiled=True)
-    table_grad = jnp.zeros_like(table).at[flat_ids].add(returned)
-    table_sum, out_sum, gains_part, loss = lax.psum(
-        (table_grad, out_grad, gains_grad, loss_pair),
-        "dp",
-    )
-    shard_squares = (
-        jnp.sum(attn_sum * attn_sum)
-        + jnp.sum(ffn_sum * ffn_sum)
-        + jnp.sum(table_sum * table_sum)
-        + jnp.sum(out_sum * out_sum)
-    )
-    square_total, gains_sum = lax.psum((shard_squares, gains_part), "mp")
-    grad_norm = jnp.sqrt(square_total + jnp.sum(gains_sum * gains_sum))
+    tally = jnp.broadcast_to(jnp.sum(counted).astype(jnp.float32), (1, 128))
+    attn_sum, ffn_sum, table_turned, out_sum, small, square = backward_call(
+        n, tokens[0], tally, losses, visible, grad, first, gains, out_grad, kept, attn_full, ffn_full, slope, act, table
+    )
+    table_sum = table_turned.T
+    gains_sum = small[:10].reshape(gains.shape)
+    grad_norm = jnp.sqrt(square[0, 0])
     factor = clip_limit / jnp.maximum(grad_norm, clip_limit)
     attn_m_new, attn_v_new, attn_new = adamw(
         attn, attn_m, attn_v, attn_sum * factor, weight_decay, learn_rate
@@ -1405,7 +1640,7 @@
         gains, gains_m, gains_v, gains_sum * factor, 0.0, gain_rate
     )
     return (
-        loss,
+        small[10, :2],
         grad_norm.reshape(1),
         attn_m_new,
         attn_v_new,

time: 585 us -> 437 us (0.75)
  the two profiles are of different devices: /device:TPU:0 before, /device:TPU:1 now
where the time goes in v4:
time: 437 us; the launch traced here: 428 us
  Pallas kernels  384 us (88%)
  other arithmetic  30.1 us (7%)
  local copies, waits for them, and re-layouts  10.1 us (2%)
    pallas_call x1, Pallas kernels, forward_call(): pl.pallas_call(functools.partial(forward_kernel, n), out_shape=(shape((LA...  197 us
    pallas_call x1, Pallas kernels, backward_call(): pl.pallas_call(functools.partial(backward_kernel, n), out_shape=(shape((L...  188 us
    sub x5, other arithmetic, adamw(): weight - rate * (fixed_one / (jnp.sqrt(fixed_two) + adam_eps) + decay * w...  23 us

profile of v4, /device:TPU:1, one launch (start us, length us, event | category | flops | bytes accessed | tf_op | source)
XLA Modules:
  0.0 428.4 jit_solution(1555851693221633987)
XLA Ops:
  0.7 0.0 copy-start.1
  0.7 1.4 constant_dynamic-slice_fusion
  2.0 1.2 compare_convert_fusion.visible_ref
  3.2 0.7 pad_bitcast_fusion
  3.9 1.3 fusion.16
  5.8 0.5 broadcast_in_dim.4.counted_ref
  6.4 0.1 fusion.8
  6.4 0.6 reshape.124.valid_ref
  7.1 0.7 pad.9
  7.8 0.6 reshape.122.labels_ref
  8.4 0.7 copy.38.places_ref
  9.1 1.4 convert_multiply_fusion.mask_ref
  10.5 1.4 fusion.6
  11.9 0.9 pad_maximum_fusion.where_ref
  12.8 0.0 copy-done.1
  12.8 1.7 copy.37.table_ref
  14.6 196.7 %forward_layers.1 = (bf16[2,4,768,768]{3,2,1,0:T(8,128)(2,1)}, bf16[2,2,3072,768]{3,2,1,0:T(8,128)(2,1)}, f32[256,768]{1,0:T(8,128)}, bf16[2,256,768]{2,1,0:T(8,...) custom-call(s32[8,256]{1,0:T(8,128)} %bitcast.37, ...), custom_call_target="tpu_custom_call" | custom-call | tf_op jit(solution)/shard_map/forward_layers/pallas_call | solution.py:484
  211.3 0.0 copy-start.7
  211.3 0.0 copy-start.8
  211.3 0.0 copy-start.9
  211.3 187.8 %backward_layers.1 = (f32[2,4,96,768]{3,2,1,0:T(8,128)}, f32[2,2,384,768]{3,2,1,0:T(8,128)}, f32[96,3840]{1,0:T(8,128)}, f32[480,768]{1,0:T(8,128)}, f32[16,768]{1,0:T(8,128)}, /*index=5*/f32[1,128]{1,0:T(1,128)}) custom-call(s32[8,256]{1,0:T(8,128)} %bitcast.38, f32[1,128]{1,0:T(1,128)} %broadcast_in_dim.4.counted_ref, ...), custom_call_target="tpu_custom_call" | custom-call | tf_op jit(solution)/shard_map/backward_layers/pallas_call | solution.py:1184
  399.8 1.2 slice_bitcast_fusion
  401.0 0.8 slice_multiply_fusion
  401.8 0.0 copy-done.7
  401.8 0.0 copy-done.8
  401.8 0.0 copy-done.9
  401.9 0.0 copy-start.4
  401.9 0.0 copy-start.5
  401.9 0.0 copy-start.6
  401.9 0.7 multiply_subtract_fusion.4
  402.6 0.0 copy-start.2
  402.6 0.0 slice-start.4
  402.6 0.0 slice-start.6
  402.6 5.5 %multiply_subtract_fusion.3 = (f32[3840,96]{0,1:T(8,128)}, f32[3840,96]{0,1:T(8,128)}, f32[3840,96]{0,1:T(8,128)}) fusion(f32[3840,96]{0,1:T(8,128)S(1)} %copy-done.1, f32[96,3840]{1,0:T(8,128)} %get-tuple-element.53, f32[]{:T(128)} %bitcast.8, f32[3840,96]{0,1:T(8,128)} %param.33, f32[3840,96]{0,1:T(8,128)} %param.32), kind=kLoop, calls=%fused_computation.16 | loop fusion | flops 5898240 | bytes 10321924 | tf_op jit(solution)/shard_map/sub | solution.py:1419
  408.1 0.0 copy-done.4
  408.1 0.0 copy-done.5
  408.1 0.0 copy-done.6
  408.1 0.0 copy-done.2
  408.1 0.0 copy-start
  408.1 0.0 copy-start.3
  408.1 0.0 slice-start.5
  408.2 0.0 slice-start.7
  408.2 2.9 multiply_subtract_fusion.2
  411.0 0.0 slice-start
  411.0 0.0 slice-start.2
  411.0 1.1 copy-done
  412.1 0.7 copy-done.3
  412.9 0.0 slice-start.1
  412.9 0.0 slice-start.3
  412.9 7.5 %multiply_subtract_fusion.1 = (f32[2,4,96,768]{3,2,1,0:T(8,128)}, f32[2,4,96,768]{3,2,1,0:T(8,128)}, f32[2,4,96,768]{3,2,1,0:T(8,128)}) fusion(f32[2,4,96,768]{3,2,1,0:T(8,128)S(1)} %copy-done, f32[2,4,96,768]{3,2,1,0:T(8,128)} %get-tuple-element.51, f32[]{:T(128)} %bitcast.8, f32[2,4,96,768]{3,2,1,0:T(8,128)S(1)} %copy-done.3, f32[2,4,96,768]{3,2,1,0:T(8,128)} %param.26), kind=kLoop, calls=%fused_computation.6 | loop fusion | flops 9437184 | bytes 16515076 | tf_op jit(solution)/shard_map/sub | solution.py:1419
  420.3 0.0 slice-done.4
  420.3 0.0 slice-done.6
  420.3 0.0 slice-done.5
  420.3 0.0 slice-done.7
  420.3 0.0 slice-done
  420.3 0.0 slice-done.2
  420.4 0.0 slice-done.1
  420.4 0.0 slice-done.3
  420.4 6.5 %multiply_subtract_fusion = (f32[2,2,384,768]{3,2,1,0:T(8,128)}, f32[2,2,384,768]{3,2,1,0:T(8,128)}, f32[2,2,384,768]{3,2,1,0:T(8,128)}) fusion(f32[2,2,384,768]{3,2,1,0:T(8,128)S(1)} %bitcast.30, f32[2,2,384,768]{3,2,1,0:T(8,128)S(1)} %bitcast.36, f32[]{:T(128)} %bitcast.8, f32[2,2,384,768]{3,2,1,0:T(8,128)S(1)} %bitcast.32, f32[2,2,384,768]{3,2,1,0:T(8,128)S(1)} %bitcast.34), kind=kLoop, calls=%fused_computation.2 | loop fusion | flops 18874368 | bytes 33030148 | tf_op jit(solution)/shard_map/sub | solution.py:1419
  (6 shorter events, 0.0 us)
Async XLA Ops:
  0.7 12.2 %copy-start.1 = (f32[3840,96]{0,1:T(8,128)S(1)}, f32[3840,96]{0,1:T(8,128)}, u32[]{:S(2)}) copy-start(f32[3840,96]{0,1:T(8,128)} %param.31) | copy-start | bytes 4423684
  211.3 190.5 %copy-start.7 = (f32[5,2,768]{2,1,0:T(2,128)S(1)}, f32[5,2,768]{2,1,0:T(2,128)}, u32[]{:S(2)}) copy-start(f32[5,2,768]{2,1,0:T(2,128)} %gains_ref.3) | copy-start | bytes 92164
  211.3 190.5 %copy-start.8 = (f32[5,2,768]{2,1,0:T(2,128)S(1)}, f32[5,2,768]{2,1,0:T(2,128)}, u32[]{:S(2)}) copy-start(f32[5,2,768]{2,1,0:T(2,128)} %param.39) | copy-start | bytes 92164
  211.3 190.5 %copy-start.9 = (f32[5,2,768]{2,1,0:T(2,128)S(1)}, f32[5,2,768]{2,1,0:T(2,128)}, u32[]{:S(2)}) copy-start(f32[5,2,768]{2,1,0:T(2,128)} %param.38) | copy-start | bytes 92164
  401.9 6.2 %copy-start.4 = (f32[480,768]{1,0:T(8,128)S(1)}, f32[480,768]{1,0:T(8,128)}, u32[]{:S(2)}) copy-start(f32[480,768]{1,0:T(8,128)} %param.36) | copy-start | bytes 4423684
  401.9 6.2 %copy-start.5 = (f32[480,768]{1,0:T(8,128)S(1)}, f32[480,768]{1,0:T(8,128)}, u32[]{:S(2)}) copy-start(f32[480,768]{1,0:T(8,128)} %param.35) | copy-start | bytes 4423684
  401.9 6.2 %copy-start.6 = (f32[480,768]{1,0:T(8,128)S(1)}, f32[480,768]{1,0:T(8,128)}, u32[]{:S(2)}) copy-start(f32[480,768]{1,0:T(8,128)} %get-tuple-element.54) | copy-start | bytes 4423684
  402.6 5.5 %copy-start.2 = (f32[480,768]{1,0:T(8,128)S(1)}, f32[480,768]{1,0:T(8,128)}, u32[]{:S(2)}) copy-start(f32[480,768]{1,0:T(8,128)} %out_ref.1) | copy-start | bytes 4423684
  402.6 17.7 %slice-start.4 = ((s8[4718592]{0:T(1024)(128)(4,1)}), s8[4194304]{0:T(1024)(128)(4,1)S(1)}, s32[]{:S(2)}) async-start(s8[4718592]{0:T(1024)(128)(4,1)} %bitcast.33), calls=%async_computation.4 | async-start | bytes 8388608
  402.6 17.7 %slice-start.6 = ((s8[4718592]{0:T(1024)(128)(4,1)}), s8[4194304]{0:T(1024)(128)(4,1)S(1)}, s32[]{:S(2)}) async-start(s8[4718592]{0:T(1024)(128)(4,1)} %bitcast.35), calls=%async_computation.6 | async-start | bytes 8388608
  408.1 4.0 copy-start
  408.1 4.7 %copy-start.3 = (f32[2,4,96,768]{3,2,1,0:T(8,128)S(1)}, f32[2,4,96,768]{3,2,1,0:T(8,128)}, u32[]{:S(2)}) copy-start(f32[2,4,96,768]{3,2,1,0:T(8,128)} %param.27) | copy-start | bytes 7077892
  408.1 12.2 %slice-start.5 = ((s8[4718592]{0:T(1024)(128)(4,1)}), s8[524288]{0:T(1024)(128)(4,1)S(1)}, s32[]{:S(2)}) async-start(s8[4718592]{0:T(1024)(128)(4,1)} %bitcast.33), calls=%async_computation.5 | async-start | bytes 1048576
  408.2 12.2 %slice-start.7 = ((s8[4718592]{0:T(1024)(128)(4,1)}), s8[524288]{0:T(1024)(128)(4,1)S(1)}, s32[]{:S(2)}) async-start(s8[4718592]{0:T(1024)(128)(4,1)} %bitcast.35), calls=%async_computation.7 | async-start | bytes 1048576
  411.0 9.3 %slice-start = ((s8[4718592]{0:T(1024)(128)(4,1)}), s8[4194304]{0:T(1024)(128)(4,1)S(1)}, s32[]{:S(2)}) async-start(s8[4718592]{0:T(1024)(128)(4,1)} %bitcast.29), calls=%async_computation | async-start | bytes 8388608
  411.0 9.3 %slice-start.2 = ((s8[4718592]{0:T(1024)(128)(4,1)}), s8[4194304]{0:T(1024)(128)(4,1)S(1)}, s32[]{:S(2)}) async-start(s8[4718592]{0:T(1024)(128)(4,1)} %bitcast.31), calls=%async_computation.2 | async-start | bytes 8388608
  412.9 7.5 %slice-start.1 = ((s8[4718592]{0:T(1024)(128)(4,1)}), s8[524288]{0:T(1024)(128)(4,1)S(1)}, s32[]{:S(2)}) async-start(s8[4718592]{0:T(1024)(128)(4,1)} %bitcast.29), calls=%async_computation.1 | async-start | bytes 1048576
  412.9 7.5 %slice-start.3 = ((s8[4718592]{0:T(1024)(128)(4,1)}), s8[524288]{0:T(1024)(128)(4,1)S(1)}, s32[]{:S(2)}) async-start(s8[4718592]{0:T(1024)(128)(4,1)} %bitcast.31), calls=%async_computation.3 | async-start | bytes 1048576
